TPU v7x, 256 devices: a whole 4x4x8 slice. The times are simulated.
256 devices in a mesh: ctx: 32 (over x, z_hi, core), head: 8 (over z_lo, y).
Axes of the slice: x: 4, y: 4, z: 8 (z_hi: 4, z_lo: 2; z = z_hi * 2 + z_lo), core: 2. Of those that a mesh axis runs over, the one named last changes fastest.
Arguments:
- hidden: bfloat16 [16384, 8192], P('ctx', 'head'), may hold values from -6 to 6
- dt_weight: bfloat16 [8192, 256], P('head'), may hold values from -0.375 to 0.375
- dt_bias: float32 [256], P('head'), may hold values from -2 to 1
- decay_rate: float32 [256], P('head'), may hold values from 1.2207031e-06 to 0.05
- skip_gain: float32 [256], P('head'), may hold values from 0.5 to 2
- ssm_in: bfloat16 [16384, 16384], P('ctx', 'head'), may hold values from -6 to 6
- bc_in: bfloat16 [16384, 8, 512], P('ctx', 'head'), may hold values from -6 to 6
- conv_x: float32 [4, 16384], P(None, 'head'), may hold values from -3 to 3
- conv_bc: float32 [4, 8, 512], P(None, 'head'), may hold values from -3 to 3
- gate_in: bfloat16 [16384, 16384], P('ctx', 'head'), may hold values from -6 to 6
- norm_gain: float32 [16384], P('head'), may hold values from 0.1 to 1.9
- query_heads: bfloat16 [16384, 4096], P('ctx', 'head'), may hold values from -32 to 32
- key_heads: bfloat16 [16384, 1024], P('ctx', 'head'), may hold values from -6 to 6
- value_heads: bfloat16 [16384, 1024], P('ctx', 'head'), may hold values from -6 to 6
Outputs:
- mamba_out: bfloat16 [16384, 16384], P('ctx', 'head')
- attn_out: bfloat16 [16384, 4096], P('ctx', 'head')
All inputs are finite; a program needn't handle non-finite values.
Results may differ from a plain program's by a relative error of at most 0.0075.
Values may be sent and summed in bfloat16 or wider, within the bound.
No kernel may reach another device: no remote copies, remote signals or barrier semaphores. Data moves between devices by JAX's collectives and lax.ppermute only.
A program may use at most 256 MiB of HBM per device.

v0:
```python
import math

import jax
import jax.numpy as jnp
from jax import lax
from jax.sharding import PartitionSpec as P

SPAN = 128
HD = 128


def shifted(value, axis, steps):
    count = lax.axis_size(axis)
    first, last = (max(0, -steps), min(count, count - steps))
    return lax.ppermute(value, axis, [(source, source + steps) for source in range(first, last)])


def entering(value, axis, join, neutral):
    count, mine = (lax.axis_size(axis), lax.axis_index(axis))
    pieces = jax.tree.map(lambda part: lax.all_gather(part, axis), value)
    subtotal = jax.tree.map(
        lambda part, zero: jnp.full_like(part, 0) + jnp.asarray(zero, part.dtype), value, neutral
    )

    def step(position, subtotal):
        longer = join(subtotal, jax.tree.map(lambda part: part[position], pieces))
        return jax.tree.map(lambda new, old: jnp.where(position < mine, new, old), longer, subtotal)

    return lax.fori_loop(0, count - 1, step, subtotal)


def conv_silu(window, weights, length):
    running = weights[0] * window[0:length].astype(jnp.float32)
    for offset in range(1, weights.shape[0]):
        running = running + weights[offset] * window[offset : offset + length].astype(jnp.float32)
    return jax.nn.silu(running).astype(jnp.bfloat16)


def span_terms(inputs_span, bmatrix, cmatrix, steps_span, decay_rates):
    length, head_count, head_size = inputs_span.shape
    groups = bmatrix.shape[1]
    per_group = head_count // groups
    cumulative = jnp.cumsum(-steps_span * decay_rates[None, :], axis=0)
    products = jnp.einsum("igm,jgm->gij", cmatrix, bmatrix, preferred_element_type=jnp.float32)
    products = jnp.broadcast_to(products[:, None], (groups, per_group, length, length)).reshape(
        head_count, length, length
    )
    causal = jnp.tril(jnp.ones((length, length), dtype=bool))
    across = cumulative.T[:, :, None] - cumulative.T[:, None, :]
    decays = jnp.exp(jnp.where(causal[None], across, -1e30))
    mixing = (products * decays * steps_span.T[:, None, :]).astype(jnp.bfloat16)
    intra = jnp.einsum("hij,jhp->ihp", mixing, inputs_span, preferred_element_type=jnp.float32)
    to_last = jnp.exp(cumulative[-1][None, :] - cumulative) * steps_span
    weighted = (inputs_span.astype(jnp.float32) * to_last[:, :, None]).astype(jnp.bfloat16)
    increment = jnp.einsum(
        "jghp,jgm->ghpm",
        weighted.reshape(length, groups, per_group, head_size),
        bmatrix,
        preferred_element_type=jnp.float32,
    )
    return (intra, cumulative, increment.reshape(head_count, head_size, bmatrix.shape[2]))


def state_readout(cmatrix, state, cumulative):
    length = cmatrix.shape[0]
    groups = cmatrix.shape[1]
    head_count, head_size, state_size = state.shape
    shaped = state.astype(jnp.bfloat16).reshape(groups, head_count // groups, head_size, state_size)
    readout = jnp.einsum("igm,ghpm->ighp", cmatrix, shaped, preferred_element_type=jnp.float32)
    return readout.reshape(length, head_count, head_size) * jnp.exp(cumulative)[:, :, None]


def gated_norm(mixed, gate, gain, groups):
    row_count, inner_width = mixed.shape
    gated = mixed * jax.nn.silu(gate.astype(jnp.float32))
    shaped = gated.reshape(row_count, groups, inner_width // groups)
    factor = lax.rsqrt(jnp.mean(shaped * shaped, axis=-1, keepdims=True) + 1e-05)
    return ((shaped * factor).reshape(row_count, inner_width) * gain[None, :]).astype(jnp.bfloat16)


def combine_states(earlier, later):
    return (earlier[0] * later[0], later[0][:, None, None] * earlier[1] + later[1])


def attend_block(carry, query_rows, query_pos, key_block, value_block, key_pos):
    maximum, denominator, weighted_sum = carry
    scale = query_rows.shape[-1] ** (-0.5)
    scores = (
        jnp.einsum("rghd,sgd->rghs", query_rows, key_block, preferred_element_type=jnp.float32)
        * scale
    )
    visible = (key_pos[None, :] <= query_pos[:, None])[:, None, None, :]
    scores = jnp.where(visible, scores, -1e30)
    updated = jnp.maximum(maximum, jnp.max(scores, axis=-1))
    weights = jnp.where(visible, jnp.exp(scores - updated[..., None]), 0.0)
    factor = jnp.exp(maximum - updated)
    denominator = denominator * factor + jnp.sum(weights, axis=-1)
    weighted_sum = weighted_sum * factor[..., None] + jnp.einsum(
        "rghs,sgd->rghd",
        weights.astype(jnp.bfloat16),
        value_block,
        preferred_element_type=jnp.float32,
    )
    return (updated, denominator, weighted_sum)


def fold_piece(carry, piece, query_rows, query_pos):
    key_piece, value_piece = piece
    row_count = key_piece.shape[0]
    block = math.gcd(row_count, 512)
    blocks = row_count // block
    key_blocks = key_piece.reshape(blocks, block, key_piece.shape[1], key_piece.shape[2])
    value_blocks = value_piece.reshape(blocks, block, value_piece.shape[1], value_piece.shape[2])
    last_query = query_pos[-1]

    def visit(state, items):
        key_block, value_block, block_index = items
        first_key = block_index * block
        key_pos = first_key + jnp.arange(block, dtype=jnp.int32)
        state = lax.cond(
            first_key <= last_query,
            lambda inner_state: attend_block(
                inner_state, query_rows, query_pos, key_block, value_block, key_pos
            ),
            lambda inner_state: inner_state,
            state,
        )
        return (state, None)

    result, unused = lax.scan(
        visit, carry, (key_blocks, value_blocks, jnp.arange(blocks, dtype=jnp.int32))
    )
    return result


def local(
    hidden,
    dt_weight,
    dt_bias,
    decay_rate,
    skip_gain,
    ssm_in,
    bc_in,
    conv_x,
    conv_bc,
    gate_in,
    norm_gain,
    query_heads,
    key_heads,
    value_heads,
):
    tok_count = ssm_in.shape[0]
    head_count = dt_bias.shape[0]
    inner_width = ssm_in.shape[1]
    head_size = inner_width // head_count
    groups = bc_in.shape[1]
    pair_width = bc_in.shape[2]
    state_size = pair_width // 2
    tail_rows = conv_x.shape[0] - 1
    partial_steps = jnp.dot(hidden, dt_weight, preferred_element_type=jnp.float32)
    summed = lax.psum(partial_steps, "head")
    raw_steps = lax.dynamic_slice_in_dim(summed, lax.axis_index("head") * head_count, head_count, 1)
    step_size = jax.nn.softplus(raw_steps + dt_bias[None, :])
    tails = jnp.concatenate(
        [
            ssm_in[tok_count - tail_rows :],
            bc_in[tok_count - tail_rows :].reshape(tail_rows, groups * pair_width),
        ],
        axis=1,
    )
    arrived = shifted(tails, "ctx", 1)
    inner_window = jnp.concatenate([arrived[:, :inner_width], ssm_in], axis=0)
    pair_window = jnp.concatenate(
        [arrived[:, inner_width:].reshape(tail_rows, groups, pair_width), bc_in], axis=0
    )
    conv_inner = conv_silu(inner_window, conv_x, tok_count)
    conv_pair = conv_silu(pair_window, conv_bc, tok_count)
    spans = tok_count // SPAN
    heads_in = conv_inner.reshape(spans, SPAN, head_count, head_size)
    pairs = conv_pair.reshape(spans, SPAN, groups, pair_width)
    bmatrix = pairs[..., :state_size]
    cmatrix = pairs[..., state_size:]
    steps_spanned = step_size.reshape(spans, SPAN, head_count)
    intra, cumulative, increment = lax.map(
        lambda items: span_terms(items[0], items[1], items[2], items[3], decay_rate),
        (heads_in, bmatrix, cmatrix, steps_spanned),
    )

    def accumulate(carry, items):
        state, log_total = carry
        span_increment, span_cumulative = items
        new_state = jnp.exp(span_cumulative[-1])[:, None, None] * state + span_increment
        return ((new_state, log_total + span_cumulative[-1]), (state, log_total))

    initial_state = (
        jnp.zeros((head_count, head_size, state_size), jnp.float32),
        jnp.zeros((head_count,), jnp.float32),
    )
    (end_state, device_log), (start_states, start_logs) = lax.scan(
        accumulate, initial_state, (increment, cumulative)
    )
    identity = (
        jnp.ones((head_count,), jnp.float32),
        jnp.zeros((head_count, head_size, state_size), jnp.float32),
    )
    carried_decay, carried_state = entering(
        (jnp.exp(device_log), end_state), "ctx", combine_states, identity
    )
    full_states = start_states + jnp.exp(start_logs)[:, :, None, None] * carried_state[None]
    readout = jax.vmap(state_readout)(cmatrix, full_states, cumulative)
    mixed = intra + readout + skip_gain[None, None, :, None] * heads_in.astype(jnp.float32)
    mamba_out = gated_norm(mixed.reshape(tok_count, inner_width), gate_in, norm_gain, groups)
    kv_count = key_heads.shape[1] // HD
    query_rows = query_heads.reshape(tok_count, kv_count, -1, HD)
    key_rows = key_heads.reshape(tok_count, kv_count, HD)
    value_rows = value_heads.reshape(tok_count, kv_count, HD)
    offset = lax.axis_index("ctx") * tok_count
    query_pos = offset + jnp.arange(tok_count, dtype=jnp.int32)
    initial = (
        jnp.full(query_rows.shape[:3], -1e30, jnp.float32),
        jnp.zeros(query_rows.shape[:3], jnp.float32),
        jnp.zeros(query_rows.shape, jnp.float32),
    )
    attn_state = fold_piece(
        initial,
        (
            lax.all_gather(key_rows, "ctx", axis=0, tiled=True),
            lax.all_gather(value_rows, "ctx", axis=0, tiled=True),
        ),
        query_rows,
        query_pos,
    )
    final_max, denominator, weighted_sum = attn_state
    attn_out = (weighted_sum / denominator[..., None]).astype(jnp.bfloat16).reshape(tok_count, -1)
    return (mamba_out, attn_out)


def solution(mesh):
    in_specs = (
        P("ctx", "head"),
        P("head", None),
        P("head"),
        P("head"),
        P("head"),
        P("ctx", "head"),
        P("ctx", "head", None),
        P(None, "head"),
        P(None, "head", None),
        P("ctx", "head"),
        P("head"),
        P("ctx", "head"),
        P("ctx", "head"),
        P("ctx", "head"),
    )
    out_specs = (P("ctx", "head"), P("ctx", "head"))
    return jax.shard_map(local, mesh=mesh, in_specs=in_specs, out_specs=out_specs, check_vma=False)
```

profile of v0, /device:TPU:35, one launch (start us, length us, event | category | flops | bytes accessed | tf_op | source)
XLA Modules:
  0.0 616.1 jit_solution(6101973741744308503)
XLA Ops:
  9.2 2.3 fusion.74
  13.7 5.5 collective-permute-start
  20.9 2.5 copy.55
  25.3 10.3 %multiply_convert_fusion.4 = bf16[512,2048]{0,1:T(8,128)(2,1)} fusion(bf16[512,2048]{0,1:T(8,128)(2,1)} %copy.55, bf16[3,2048]{0,1:T(8,128)(2,1)} %copy.54, f32[2048]{0:T(1024)S(1)} %bitcast.222, f32[2048]{0:T(1024)S(1)} %bitcast.223, f32[2048]{0:T(1024)S(1)} %bitcast.221, f32[2048]{0:T(1024)S(1)} %bitcast.220), kind=kLoop, calls=%fused_computation.89 | loop fusion | flops 26214400 | bytes 4239360 | tf_op jit(solution)/shard_map/convert_element_type | solution.py:36
  35.6 4.0 reshape.228
  39.7 3.5 copy.57
  43.1 48.8 %all-reduce.3.cloned.1.call-done = f32[512,256]{0,1:T(8,128)} async-done(((f32[512,256]{0,1:T(8,128)}), f32[512,256]{0,1:T(8,128)}) %all-reduce.3.cloned.1.call-update) | async-done | bytes 524304 | tf_op jit(solution)/shard_map/psum | solution.py:161
  93.0 4.3 broadcast.82.clone
  97.3 25.7 %while.60 = (s32[]{:T(128)}, f32[4,128,32,64]{1,3,2,0:T(8,128)}, f32[4,128,32]{2,1,0:T(8,128)S(1)}, f32[4,32,64,256]{3,2,1,0:T(8,128)}, bf16[4,128,32,64]{1,3,2,...) while((s32[]{:T(128)}, f32[4,128,32,64]{1,3,2,0:T(8,128)}, ...), condition=%wide.region_3.4_spmd, body=%wide.region_1.3_spmd.sunk | while | flops 213676032 | bytes 5001345 | solution.py:184
  97.6 2.8 bitcast_dynamic-update-slice_fusion.7
  100.8 2.9 fusion.94
  104.0 2.8 bitcast_dynamic-update-slice_fusion.7
  107.1 2.9 fusion.94
  110.4 2.8 bitcast_dynamic-update-slice_fusion.7
  113.5 2.9 fusion.94
  116.8 2.9 bitcast_dynamic-update-slice_fusion.7
  120.0 3.0 fusion.94
  123.0 4.3 broadcast.82
  127.3 14.2 %while.62 = (s32[]{:T(128)}, f32[32,64,256]{2,1,0:T(8,128)S(1)}, f32[32]{0:T(128)S(1)}, f32[4,32,64,256]{3,2,1,0:T(8,128)}, f32[4,32]{1,0:T(4,128)S(1)}, /*index...) while((s32[]{:T(128)}, f32[32,64,256]{2,1,0:T(8,128)S(1)}, ...), condition=%wide.region_5.6_spmd.clone, body=%wide.region_4.5_spmd.clone.sunk | while | flops 2097220 | bytes 10487437 | solution.py:199
  142.9 3.9 copy.64
  149.3 87.7 %all-reduce = f32[1024]{0:T(1024)S(1)} all-reduce(f32[1024]{0:T(1024)S(1)} %exponential_dynamic-update-slice_fusion), channel_id=2, replica_groups=mesh['ctx'=32,'head'=8] {'ctx'}, use_global_device_ids=true, to_apply=%add | all-reduce | flops 1024 | bytes 8192
  237.2 6.5 %copy.67 = bf16[32,512,1,128]{1,3,2,0:T(8,128)(2,1)} copy(bf16[32,512,1,128]{3,1,0,2:T(8,128)(2,1)} %bitcast.211) | data formatting | bytes 8388608
  244.9 127.4 %while.61 = (s32[]{:T(128)}, f32[512,1,4]{0,2,1:T(4,128)S(1)}, f32[512,1,4]{0,2,1:T(4,128)S(1)}, f32[512,1,4,128]{0,3,2,1:T(8,128)}, s32[32]{0:T(128)S(1)}, /*in...) while((s32[]{:T(128)}, f32[512,1,4]{0,2,1:T(4,128)S(1)}, ...), condition=%wide.region_14.15_spmd.clone, body=%wide.region_9.14_spmd.clone.sunk | while | flops 551296000 | bytes 16661811 | solution.py:130
  246.7 7.2 %conditional.3 = ((f32[512,1,4]{0,2,1:T(4,128)S(1)}, f32[512,1,4]{0,2,1:T(4,128)S(1)}, f32[512,1,4,128]{0,3,2,1:T(8,128)})) conditional(s32[]{:T(128)} %convert_element_type.144, (f32[512,1,4]{0,2,1:T(4,128)S(1)}, f32[512,1,4]{0,2,1:T(4,128)S(1)}, f32[512,1,4,128]{0,3,2,1:T(8,128)}) %tuple.115, (s32[]{:T(128)}, s32[512]{0:T(512)S(1)}, s32[]{:T(128)}, ...), branch_computations={%region_10.10_spmd, %region_11.13_spmd} | conditional | flops 551296000 | bytes 16659496 | solution.py:120
  248.8 4.1 fusion.37
  255.8 6.8 %conditional.3 = ((f32[512,1,4]{0,2,1:T(4,128)S(1)}, f32[512,1,4]{0,2,1:T(4,128)S(1)}, f32[512,1,4,128]{0,3,2,1:T(8,128)})) conditional(s32[]{:T(128)} %convert_element_type.144, (f32[512,1,4]{0,2,1:T(4,128)S(1)}, f32[512,1,4]{0,2,1:T(4,128)S(1)}, f32[512,1,4,128]{0,3,2,1:T(8,128)}) %tuple.115, (s32[]{:T(128)}, s32[512]{0:T(512)S(1)}, s32[]{:T(128)}, ...), branch_computations={%region_10.10_spmd, %region_11.13_spmd} | conditional | flops 551296000 | bytes 16659496 | solution.py:120
  257.8 3.7 fusion.37
  264.4 6.8 %conditional.3 = ((f32[512,1,4]{0,2,1:T(4,128)S(1)}, f32[512,1,4]{0,2,1:T(4,128)S(1)}, f32[512,1,4,128]{0,3,2,1:T(8,128)})) conditional(s32[]{:T(128)} %convert_element_type.144, (f32[512,1,4]{0,2,1:T(4,128)S(1)}, f32[512,1,4]{0,2,1:T(4,128)S(1)}, f32[512,1,4,128]{0,3,2,1:T(8,128)}) %tuple.115, (s32[]{:T(128)}, s32[512]{0:T(512)S(1)}, s32[]{:T(128)}, ...), branch_computations={%region_10.10_spmd, %region_11.13_spmd} | conditional | flops 551296000 | bytes 16659496 | solution.py:120
  266.5 3.7 fusion.37
  273.1 6.8 %conditional.3 = ((f32[512,1,4]{0,2,1:T(4,128)S(1)}, f32[512,1,4]{0,2,1:T(4,128)S(1)}, f32[512,1,4,128]{0,3,2,1:T(8,128)})) conditional(s32[]{:T(128)} %convert_element_type.144, (f32[512,1,4]{0,2,1:T(4,128)S(1)}, f32[512,1,4]{0,2,1:T(4,128)S(1)}, f32[512,1,4,128]{0,3,2,1:T(8,128)}) %tuple.115, (s32[]{:T(128)}, s32[512]{0:T(512)S(1)}, s32[]{:T(128)}, ...), branch_computations={%region_10.10_spmd, %region_11.13_spmd} | conditional | flops 551296000 | bytes 16659496 | solution.py:120
  275.1 3.7 fusion.37
  281.7 6.9 %conditional.3 = ((f32[512,1,4]{0,2,1:T(4,128)S(1)}, f32[512,1,4]{0,2,1:T(4,128)S(1)}, f32[512,1,4,128]{0,3,2,1:T(8,128)})) conditional(s32[]{:T(128)} %convert_element_type.144, (f32[512,1,4]{0,2,1:T(4,128)S(1)}, f32[512,1,4]{0,2,1:T(4,128)S(1)}, f32[512,1,4,128]{0,3,2,1:T(8,128)}) %tuple.115, (s32[]{:T(128)}, s32[512]{0:T(512)S(1)}, s32[]{:T(128)}, ...), branch_computations={%region_10.10_spmd, %region_11.13_spmd} | conditional | flops 551296000 | bytes 16659496 | solution.py:120
  283.8 3.8 fusion.37
  290.4 6.8 %conditional.3 = ((f32[512,1,4]{0,2,1:T(4,128)S(1)}, f32[512,1,4]{0,2,1:T(4,128)S(1)}, f32[512,1,4,128]{0,3,2,1:T(8,128)})) conditional(s32[]{:T(128)} %convert_element_type.144, (f32[512,1,4]{0,2,1:T(4,128)S(1)}, f32[512,1,4]{0,2,1:T(4,128)S(1)}, f32[512,1,4,128]{0,3,2,1:T(8,128)}) %tuple.115, (s32[]{:T(128)}, s32[512]{0:T(512)S(1)}, s32[]{:T(128)}, ...), branch_computations={%region_10.10_spmd, %region_11.13_spmd} | conditional | flops 551296000 | bytes 16659496 | solution.py:120
  292.5 3.7 fusion.37
  299.1 6.8 %conditional.3 = ((f32[512,1,4]{0,2,1:T(4,128)S(1)}, f32[512,1,4]{0,2,1:T(4,128)S(1)}, f32[512,1,4,128]{0,3,2,1:T(8,128)})) conditional(s32[]{:T(128)} %convert_element_type.144, (f32[512,1,4]{0,2,1:T(4,128)S(1)}, f32[512,1,4]{0,2,1:T(4,128)S(1)}, f32[512,1,4,128]{0,3,2,1:T(8,128)}) %tuple.115, (s32[]{:T(128)}, s32[512]{0:T(512)S(1)}, s32[]{:T(128)}, ...), branch_computations={%region_10.10_spmd, %region_11.13_spmd} | conditional | flops 551296000 | bytes 16659496 | solution.py:120
  301.2 3.7 fusion.37
  307.8 7.0 %conditional.3 = ((f32[512,1,4]{0,2,1:T(4,128)S(1)}, f32[512,1,4]{0,2,1:T(4,128)S(1)}, f32[512,1,4,128]{0,3,2,1:T(8,128)})) conditional(s32[]{:T(128)} %convert_element_type.144, (f32[512,1,4]{0,2,1:T(4,128)S(1)}, f32[512,1,4]{0,2,1:T(4,128)S(1)}, f32[512,1,4,128]{0,3,2,1:T(8,128)}) %tuple.115, (s32[]{:T(128)}, s32[512]{0:T(512)S(1)}, s32[]{:T(128)}, ...), branch_computations={%region_10.10_spmd, %region_11.13_spmd} | conditional | flops 551296000 | bytes 16659496 | solution.py:120
  309.9 3.8 fusion.37
  316.5 6.8 %conditional.3 = ((f32[512,1,4]{0,2,1:T(4,128)S(1)}, f32[512,1,4]{0,2,1:T(4,128)S(1)}, f32[512,1,4,128]{0,3,2,1:T(8,128)})) conditional(s32[]{:T(128)} %convert_element_type.144, (f32[512,1,4]{0,2,1:T(4,128)S(1)}, f32[512,1,4]{0,2,1:T(4,128)S(1)}, f32[512,1,4,128]{0,3,2,1:T(8,128)}) %tuple.115, (s32[]{:T(128)}, s32[512]{0:T(512)S(1)}, s32[]{:T(128)}, ...), branch_computations={%region_10.10_spmd, %region_11.13_spmd} | conditional | flops 551296000 | bytes 16659496 | solution.py:120
  318.6 3.7 fusion.37
  325.2 6.8 %conditional.3 = ((f32[512,1,4]{0,2,1:T(4,128)S(1)}, f32[512,1,4]{0,2,1:T(4,128)S(1)}, f32[512,1,4,128]{0,3,2,1:T(8,128)})) conditional(s32[]{:T(128)} %convert_element_type.144, (f32[512,1,4]{0,2,1:T(4,128)S(1)}, f32[512,1,4]{0,2,1:T(4,128)S(1)}, f32[512,1,4,128]{0,3,2,1:T(8,128)}) %tuple.115, (s32[]{:T(128)}, s32[512]{0:T(512)S(1)}, s32[]{:T(128)}, ...), branch_computations={%region_10.10_spmd, %region_11.13_spmd} | conditional | flops 551296000 | bytes 16659496 | solution.py:120
  327.3 3.7 fusion.37
  374.8 151.4 %all-gather.8.cloned.1.call-done = f32[1024,64,256]{2,1,0:T(8,128)} async-done(((f32[32,64,256]{2,1,0:T(8,128)}), f32[1024,64,256]{2,1,0:T(8,128)}) %all-gather.8.cloned.1.call-update) | async-done | bytes 67108880 | tf_op jit(solution)/shard_map/all_gather | solution.py:20
  526.2 66.5 %while.63 = (s32[]{:T(128)}, f32[32,64,256]{2,1,0:T(8,128)S(1)}, s32[]{:T(128)}, f32[32,32]{1,0:T(8,128)S(1)}, f32[32,32,64,256]{3,2,1,0:T(8,128)}, /*index=5*/s32[]{:T(128)}, s32[]{:T(128)}) while((s32[]{:T(128)}, f32[32,64,256]{2,1,0:T(8,128)S(1)}, s32[]{:T(128)}, f32[32,32]{1,0:T(8,128)S(1)}, f32[32,32,64,256]{3,2,1,0:T(8,128)}, ...), condition=%wide.region_7.8_spmd.clone, body=%wide.region_6.7_spmd.clone.sunk | while | flops 2097156 | bytes 6291945 | solution.py:29
  526.2 2.2 fusion.96
  528.4 2.1 fusion.96
  530.5 2.1 fusion.96
  532.7 2.1 fusion.96
  534.8 2.1 fusion.96
  537.0 2.1 fusion.96
  539.1 2.1 fusion.96
  541.3 2.1 fusion.96
  543.4 2.1 fusion.96
  545.6 2.1 fusion.96
  547.7 2.1 fusion.96
  549.8 2.1 fusion.96
  556.3 2.1 fusion.96
  558.4 2.1 fusion.96
  571.3 2.1 fusion.96
  584.2 2.1 fusion.96
  592.7 6.8 %fusion.63 = f32[4,128,32,64]{1,3,2,0:T(8,128)S(1)} fusion(f32[4,128,32,64]{1,3,2,0:T(8,128)} %get-tuple-element.330, f32[32]{0:T(128)S(1)} %copy-done.11, f32[4,128,32]{1,2,0:T(8,128)S(1)} %copy.61, f32[4,32,64,256]{3,2,1,0:T(8,128)} %get-tuple-element.333, f32[32,64,256]{2,1,0:T(8,128)S(1)} %get-tuple-element.337, f32[4,32]{1,0:T(4,128)S(1)} %exp.54, ...), kind=kOutput, calls=%fused_computation.84 | convolution fusion | flops 548405248 | bytes 21301760 | tf_op jit(solution)/shard_map/vmap(igm,ghpm->ighp)/dot_general | solution.py:69
  599.6 3.6 copy.63
  606.2 2.4 copy.69
  (339 shorter events, 116.3 us)
Async XLA Ops:
  8.0 1.2 copy-start
  8.0 12.9 %copy-start.6 = (bf16[512,2048]{1,0:T(8,128)(2,1)S(1)}, bf16[512,2048]{1,0:T(8,128)(2,1)}, u32[]{:S(2)}) copy-start(bf16[512,2048]{1,0:T(8,128)(2,1)} %param.29) | copy-start | bytes 6291460
  8.0 83.9 %all-reduce.3.cloned.1.call-start = ((), (), s32[]{:S(2)}) async-start(), calls=%async_computation | async-start | bytes 1048576 | tf_op jit(solution)/shard_map/psum | solution.py:161
  11.6 11.9 %copy-start.7 = (bf16[512,1,512]{2,0,1:T(8,128)(2,1)S(1)}, bf16[512,1,512]{2,0,1:T(8,128)(2,1)}, u32[]{:S(2)}) copy-start(bf16[512,1,512]{2,0,1:T(8,128)(2,1)} %param.30) | copy-start | bytes 1572868
  11.6 225.7 %all-gather.12.cloned.1.call-start = ((), (), s32[]{:S(2)}) async-start(), calls=%async_computation.3 | async-start | bytes 4325376 | tf_op jit(solution)/shard_map/all_gather | solution.py:228
  12.2 231.6 %all-gather.10.cloned.1.call-start = ((), (), s32[]{:S(2)}) async-start(), calls=%async_computation.2 | async-start | bytes 4325376 | tf_op jit(solution)/shard_map/all_gather | solution.py:227
  13.7 9.7 %collective-permute-start = (bf16[3,2560]{1,0:T(4,128)(2,1)S(1)}, bf16[3,2560]{1,0:T(4,128)(2,1)S(1)}, u32[]{:S(2)}, u32[]{:S(2)}) collective-permute-start(bf16[3,2560]{1,0:T(4,128)(2,1)S(1)} %pad_maximum_fusion.2), channel_id=1, source_target_pairs={{0,8},{8,16},{16,24},{24,32},{32,40},{40,48},{48,56},{56,64},{64,7... | collective-permute-start | bytes 46088 | tf_op jit(solution)/shard_map/ppermute | solution.py:15
  19.2 507.0 %all-gather.8.cloned.1.call-start = ((), (), s32[]{:S(2)}) async-start(), calls=%async_computation.1 | async-start | bytes 69206016 | tf_op jit(solution)/shard_map/all_gather | solution.py:20
  24.1 15.5 %copy-start.4 = (bf16[512,1,512]{2,0,1:T(8,128)(2,1)}, bf16[512,1,512]{2,0,1:T(8,128)(2,1)S(1)}, u32[]{:S(2)}) copy-start(bf16[512,1,512]{2,0,1:T(8,128)(2,1)S(1)} %multiply_convert_fusion.5) | copy-start | bytes 1572868
  35.6 56.3 %copy-start.12 = (f32[32]{0:T(128)S(1)}, f32[32]{0:T(128)}, u32[]{:S(2)}) copy-start(f32[32]{0:T(128)} %param.26) | copy-start | bytes 388
  93.0 4.3 copy-start.9
  141.5 1.3 copy-start.2
  141.5 5.9 copy-start.8
  141.6 6.4 %copy-start.13 = (u32[256]{0:T(256)S(1)}, u32[256]{0:T(256)}, u32[]{:S(2)}) copy-start(u32[256]{0:T(256)} %constant.139) | copy-start | bytes 3076
  526.2 66.5 %copy-start.5 = (bf16[512,1,512]{2,0,1:T(8,128)(2,1)S(1)}, bf16[512,1,512]{2,0,1:T(8,128)(2,1)}, u32[]{:S(2)}) copy-start(bf16[512,1,512]{2,0,1:T(8,128)(2,1)} %copy-done.4) | copy-start | bytes 1572868
  526.2 66.5 %copy-start.11 = (f32[32]{0:T(128)S(1)}, f32[32]{0:T(128)}, u32[]{:S(2)}) copy-start(f32[32]{0:T(128)} %param.28) | copy-start | bytes 388
  599.6 3.6 copy-start.3
  603.2 1.5 copy-start.10
  604.7 3.9 copy-start.1
Sparse Core Ops, SparseCore 0:
  11.7 80.1 all-reduce.2
Sparse Core Ops, SparseCore 1:
  14.9 63.1 all-gather.11
  80.9 57.7 all-gather.9
  143.0 383.1 all-gather.7
where the time goes:
time: 624 us; the launch traced here: 616 us
  waiting for transfers between devices  201 us (32%)
  other arithmetic  110 us (18%)
  matrix products  88.2 us (14%)
  blocking collectives  87.7 us (14%)
  local copies, waits for them, and re-layouts  66.2 us (11%)
  loops' own time  41.3 us (7%)
  between operations  16.6 us (3%)
    all_gather x1, waiting for transfers between devices, entering(): pieces = jax.tree.map(lambda part: lax.all_gather(part, axis), value)  151 us
    unnamed x1, blocking collectives  87.7 us
    select_n x31, other arithmetic, step(): jnp.where(position < mine, new, old)  65.3 us
    psum x1, waiting for transfers between devices, local(): summed = lax.psum(partial_steps, 'head')  48.8 us
    another operation x1, loops' own time, fold_piece(): lax.scan(visit, carry, (key_blocks, value_blocks, jnp.arange(blocks, dtyp...  39.4 us
    dot_general x10, matrix products, attend_block(): jnp.einsum('rghs,sgd->rghd', weights.astype(jnp.bfloat16), value_block, p...  37.5 us
    unnamed x37, local copies, waits for them, and re-layouts  19 us
    dynamic_slice x32, local copies, waits for them, and re-layouts, fold_piece(): lax.scan(visit, carry, (key_blocks, value_blocks, jnp.arange(blocks, dtyp...  18.8 us
  transfers between devices with their start and end apart: 5, of which 2 were waited for; matrix products, arithmetic and copies ran while one was open for 29% of the time, Pallas kernels for 0%

commit v1 on v0

v1 whole, which is shorter than its diff:
```python
import functools
import math

import jax
import jax.numpy as jnp
import numpy as np
from jax import lax
from jax.experimental import pallas as pl
from jax.experimental.pallas import tpu as pltpu
from jax.sharding import PartitionSpec as P

SPAN = 128
HD = 128
BF = jnp.bfloat16
F32 = jnp.float32
NX, NZ, NC = 4, 4, 2
HEADS, PSIZE, STATE = 32, 64, 256
CHAN = HEADS * PSIZE
TOK = 512
HB = 8
HBC = HB * PSIZE
CHUNK = 1024
VMEM_LIMIT = 58 << 20


def pairs_of(move):
    found = []
    for x in range(NX):
        for z in range(NZ):
            for c in range(NC):
                target = move(x, z, c)
                if target is not None:
                    tx, tz, tc = target
                    found.append(((x * NZ + z) * NC + c, (tx * NZ + tz) * NC + tc))
    return found


def send(value, move):
    return lax.ppermute(value, "ctx", pairs_of(move))


def swap_core(value):
    return send(value, lambda x, z, c: (x, z, 1 - c))


def along_z(value, steps):
    return send(value, lambda x, z, c: (x, (z + steps) % NZ, c))


def along_x(value, steps, wrap=False):
    def move(x, z, c):
        if wrap or 0 <= x + steps < NX:
            return ((x + steps) % NX, z, c)
        return None

    return send(value, move)


def shifted_rows(rows, tail, steps):
    if steps == 0:
        return rows
    rolled = pltpu.roll(rows, steps, 0)
    before = pltpu.roll(tail, steps, 0)
    at = lax.broadcasted_iota(jnp.int32, before.shape, 0)
    top = jnp.where(at < steps, before, rolled[:8])
    return jnp.concatenate([top, rolled[8:]], axis=0)


def conv_silu(rows, tail, taps):
    taps_count = taps.shape[0]
    total = None
    for k in range(taps_count):
        term = taps[k : k + 1] * shifted_rows(rows, tail, taps_count - 1 - k)
        total = term if total is None else total + term
    return (total * jax.nn.sigmoid(total)).astype(BF)


def two_parts(value):
    high = value.astype(BF).astype(F32)
    return [high, (value - high).astype(BF).astype(F32)]


def three_parts(value):
    high = value.astype(BF).astype(F32)
    return [high] + two_parts(value - high)


def span_kernel(
    x_ref,
    before_ref,
    xtail_ref,
    pair_ref,
    pbefore_ref,
    ptail_ref,
    steps_ref,
    rate_ref,
    skip_ref,
    taps_ref,
    ptaps_ref,
    spread_ref,
    column_ref,
    rows_ref,
    y_ref,
    c_ref,
    log_ref,
    end_ref,
    b_s,
    g_s,
    cum_s,
    ci_s,
    ex_s,
    dec_s,
    start_s,
    state_s,
):
    span, block = pl.program_id(0), pl.program_id(1)

    @pl.when(block == 0)
    def _():
        @pl.when(span == 0)
        def _():
            start_s[...] = jnp.zeros_like(start_s)

        before = jnp.where(span == 0, ptail_ref[...], pbefore_ref[...]).astype(F32)[8:]
        pair = conv_silu(pair_ref[...].astype(F32), before, ptaps_ref[...])
        bmat, cmat = pair[:, :STATE], pair[:, STATE:]
        b_s[...] = bmat
        c_ref[...] = cmat
        product = lax.dot_general(
            cmat, bmat, (((1,), (1,)), ((), ())), preferred_element_type=F32
        )
        at_i = lax.broadcasted_iota(jnp.int32, (SPAN, SPAN), 0)
        at_j = lax.broadcasted_iota(jnp.int32, (SPAN, SPAN), 1)
        g_s[...] = jnp.where(at_j <= at_i, product, 0.0)
        steps = steps_ref[...]
        upper = jnp.where(at_i <= at_j, 1.0, 0.0)
        cum = jnp.dot(
            -steps * rate_ref[...], upper, precision=lax.Precision.HIGHEST, preferred_element_type=F32
        )
        cum_s[...] = cum
        last = cum[:, SPAN - 1 : SPAN]
        ci_s[...] = jnp.concatenate(three_parts(cum) + [jnp.zeros_like(cum)], axis=0).T.astype(BF)
        ex_s[...] = jnp.concatenate(
            two_parts(jnp.exp(last - cum) * steps) + two_parts(jnp.exp(cum)), axis=0
        ).T.astype(BF)
        dec_s[...] = jnp.broadcast_to(
            jnp.concatenate(two_parts(jnp.exp(last)), axis=0), dec_s.shape
        ).astype(BF)
        log_ref[...] = start_s[:, :SPAN] + cum
        start_s[...] = start_s[...] + last

    x_rows = x_ref[...].astype(F32)
    before = jnp.where(span == 0, xtail_ref[...], before_ref[...]).astype(F32)[8:]
    xin = conv_silu(x_rows, before, taps_ref[...])
    xf = xin.astype(F32)
    spread = spread_ref[...]
    zero = jnp.zeros_like(spread)
    weight = jnp.dot(ex_s[...], jnp.concatenate([spread, zero], axis=0), preferred_element_type=F32)
    grown = jnp.dot(ex_s[...], jnp.concatenate([zero, spread], axis=0), preferred_element_type=F32)
    rows_i = jnp.dot(ci_s[...], column_ref[...], preferred_element_type=F32)
    first = span == 0
    state = jnp.where(first, 0.0, state_s[block])
    read = lax.dot_general(
        c_ref[...], state.astype(BF), (((1,), (1,)), ((), ())), preferred_element_type=F32
    )
    base = read * grown + skip_ref[...] * xf
    cum_rows = cum_s[pl.ds(block * HB, HB), :]
    step_rows = steps_ref[pl.ds(block * HB, HB), :]
    masked = g_s[...]
    lane = lax.broadcasted_iota(jnp.int32, (SPAN, 2 * PSIZE), 1)
    for pair in range(HB // 2):
        mixes = []
        for h in (2 * pair, 2 * pair + 1):
            gap = rows_i[:, h * SPAN : (h + 1) * SPAN] - cum_rows[h : h + 1]
            mixes.append(
                (masked * jnp.exp(jnp.minimum(gap, 0.0)) * step_rows[h : h + 1]).astype(BF)
            )
        two = xf[:, pair * 128 : (pair + 1) * 128]
        left = jnp.where(lane < PSIZE, two, 0.0).astype(BF)
        right = jnp.where(lane < PSIZE, 0.0, two).astype(BF)
        intra = jnp.dot(
            jnp.concatenate(mixes, axis=1),
            jnp.concatenate([left, right], axis=0),
            preferred_element_type=F32,
        )
        y_ref[:, pair * 128 : (pair + 1) * 128] = base[:, pair * 128 : (pair + 1) * 128] + intra
    weighted = (xf * weight).astype(BF)
    gain = lax.dot_general(
        weighted, b_s[...], (((0,), (0,)), ((), ())), preferred_element_type=F32
    )
    decay = jnp.dot(rows_ref[...], dec_s[...], preferred_element_type=F32)
    state = state * decay + gain
    state_s[block] = state
    end_ref[...] = state.astype(BF)


def own_tokens(ssm_in, tail, bc_in, steps, rate, skip, conv_x, conv_bc):
    spread = np.zeros((2 * HEADS, CHAN), np.float32)
    column = np.zeros((4 * HEADS, HEADS * SPAN), np.float32)
    for h in range(HEADS):
        for part in range(2):
            spread[part * HEADS + h, h * PSIZE : (h + 1) * PSIZE] = 1
        for part in range(3):
            column[part * HEADS + h, h * SPAN : (h + 1) * SPAN] = 1
    grid = (TOK // SPAN, HEADS // HB)
    prior = lambda s, b: (jnp.maximum(s * (SPAN // 16) - 1, 0), b)
    prior0 = lambda s, b: (jnp.maximum(s * (SPAN // 16) - 1, 0), 0)
    return pl.pallas_call(
        span_kernel,
        grid=grid,
        in_specs=[
            pl.BlockSpec((SPAN, HBC), lambda s, b: (s, b)),
            pl.BlockSpec((16, HBC), prior),
            pl.BlockSpec((16, HBC), lambda s, b: (0, b)),
            pl.BlockSpec((SPAN, 2 * STATE), lambda s, b: (s, 0)),
            pl.BlockSpec((16, 2 * STATE), prior0),
            pl.BlockSpec((16, 2 * STATE), lambda s, b: (0, CHAN // (2 * STATE))),
            pl.BlockSpec((HEADS, SPAN), lambda s, b: (0, s)),
            pl.BlockSpec((HEADS, 1), lambda s, b: (0, 0)),
            pl.BlockSpec((1, HBC), lambda s, b: (0, b)),
            pl.BlockSpec((4, HBC), lambda s, b: (0, b)),
            pl.BlockSpec((4, 2 * STATE), lambda s, b: (0, 0)),
            pl.BlockSpec((2 * HEADS, HBC), lambda s, b: (0, b)),
            pl.BlockSpec((4 * HEADS, HB * SPAN), lambda s, b: (0, b)),
            pl.BlockSpec((HBC, 2 * HEADS), lambda s, b: (b, 0)),
        ],
        out_specs=[
            pl.BlockSpec((SPAN, HBC), lambda s, b: (s, b)),
            pl.BlockSpec((SPAN, STATE), lambda s, b: (s, 0)),
            pl.BlockSpec((HEADS, SPAN), lambda s, b: (0, s)),
            pl.BlockSpec((HBC, STATE), lambda s, b: (b, 0)),
        ],
        out_shape=[
            jax.ShapeDtypeStruct((TOK, CHAN), F32),
            jax.ShapeDtypeStruct((TOK, STATE), BF),
            jax.ShapeDtypeStruct((HEADS, TOK), F32),
            jax.ShapeDtypeStruct((CHAN, STATE), BF),
        ],
        scratch_shapes=[
            pltpu.VMEM((SPAN, STATE), BF),
            pltpu.VMEM((SPAN, SPAN), F32),
            pltpu.VMEM((HEADS, SPAN), F32),
            pltpu.VMEM((SPAN, 4 * HEADS), BF),
            pltpu.VMEM((SPAN, 4 * HEADS), BF),
            pltpu.VMEM((2 * HEADS, STATE), BF),
            pltpu.VMEM((HEADS, SPAN), F32),
            pltpu.VMEM((HEADS // HB, HBC, STATE), F32),
        ],
        compiler_params=pltpu.CompilerParams(vmem_limit_bytes=VMEM_LIMIT),
        cost_estimate=pl.CostEstimate(flops=8 << 30, bytes_accessed=12 << 20, transcendentals=4 << 20),
    )(
        ssm_in,
        ssm_in,
        tail,
        bc_in,
        bc_in,
        tail,
        steps,
        rate,
        skip,
        conv_x,
        conv_bc,
        jnp.asarray(spread, BF),
        jnp.asarray(column, BF),
        jnp.asarray(spread.T, BF),
    )


def entering_state(end, logs, c, z, x):
    half = end.reshape(2, 16, PSIZE, STATE)
    keep = lax.dynamic_index_in_dim(half, c, 0, False)
    give = lax.dynamic_index_in_dim(half, 1 - c, 0, False)
    other = swap_core(give)
    by_half = logs.reshape(NX, NZ, NC, 2, 16)
    mine = lax.dynamic_index_in_dim(by_half, c, 3, False)
    here = lax.dynamic_index_in_dim(lax.dynamic_index_in_dim(mine, x, 0, False), z, 0, False)
    early = jnp.where(c == 0, keep, other).astype(F32)
    late = jnp.where(c == 0, other, keep).astype(F32)
    total = (late + jnp.exp(here[1])[:, None, None] * early).astype(BF).reshape(NZ, 4, PSIZE, STATE)
    quarters = [lax.dynamic_index_in_dim(total, (z + s) % NZ, 0, False) for s in range(NZ)]
    got = [quarters[0]] + [along_z(quarters[s], s) for s in range(1, NZ)]
    chip = jnp.sum(mine, axis=2).reshape(NX, NZ, NZ, 4)
    chip = lax.dynamic_index_in_dim(chip, z, 2, False)
    plane = lax.dynamic_index_in_dim(chip, x, 0, False)
    upto = jnp.concatenate([jnp.zeros((1, 4), F32), jnp.cumsum(plane, axis=0)], axis=0)
    sources = (z - jnp.arange(NZ)) % NZ
    first = jnp.take(upto, sources + 1, axis=0)
    reach = upto[:, None, :] - first[None]
    weights = jnp.where(
        sources[None, :, None] < jnp.arange(NZ + 1)[:, None, None], jnp.exp(jnp.minimum(reach, 0.0)), 0.0
    )

    def joined(to):
        return sum(weights[to, s][:, None, None] * got[s].astype(F32) for s in range(NZ))

    whole = joined(NZ).astype(BF)
    planes = jnp.sum(chip, axis=1)
    passed = jnp.concatenate([jnp.zeros((1, 4), F32), jnp.cumsum(planes, axis=0)], axis=0)
    into = lax.dynamic_index_in_dim(passed, x, 0, False)
    carried = jnp.zeros((4, PSIZE, STATE), F32)
    for s in range(1, NX):
        after = lax.dynamic_index_in_dim(passed, jnp.maximum(x - s, 0) + 1, 0, False)
        factor = jnp.where(x >= s, jnp.exp(jnp.minimum(into - after, 0.0)), 0.0)
        carried = carried + factor[:, None, None] * along_x(whole, s).astype(F32)
    prefix = [joined(to) for to in range(NZ)]
    outs = jnp.stack(
        [
            (prefix[to] + jnp.exp(upto[to])[:, None, None] * carried).astype(BF)
            for to in range(NZ)
        ]
    )
    back = [lax.dynamic_index_in_dim(outs, z, 0, False)]
    for s in range(1, NZ):
        back.append(along_z(lax.dynamic_index_in_dim(outs, (z + s) % NZ, 0, False), s))
    back = jnp.stack(back)
    chip_in = jnp.stack(
        [lax.dynamic_index_in_dim(back, (z - q) % NZ, 0, False) for q in range(NZ)]
    ).reshape(16, PSIZE, STATE)
    second = (early + jnp.exp(here[0])[:, None, None] * chip_in.astype(F32)).astype(BF)
    for_me = jnp.where(c == 0, chip_in, second)
    for_other = swap_core(jnp.where(c == 0, second, chip_in))
    return jnp.stack(
        [jnp.where(c == 0, for_me, for_other), jnp.where(c == 0, for_other, for_me)]
    ).reshape(CHAN, STATE)


def finish_kernel(y_ref, c_ref, log_ref, in_ref, gate_ref, gain_ref, spread_ref, out_ref):
    grown = jnp.concatenate(
        two_parts(jnp.exp(log_ref[...])) + [jnp.zeros((2 * HEADS, SPAN), F32)], axis=0
    ).T.astype(BF)
    spread = spread_ref[...]
    scale = jnp.dot(
        grown, jnp.concatenate([spread, jnp.zeros_like(spread)], axis=0), preferred_element_type=F32
    )
    read = lax.dot_general(
        c_ref[...], in_ref[...], (((1,), (1,)), ((), ())), preferred_element_type=F32
    )
    mixed = y_ref[...] + read * scale
    gate = gate_ref[...].astype(F32)
    gated = mixed * (gate * jax.nn.sigmoid(gate))
    mean = jnp.mean(gated * gated, axis=1, keepdims=True)
    out_ref[...] = (gated * lax.rsqrt(mean + 1e-05) * gain_ref[...]).astype(BF)


def finish(y, cmat, logs, entering, gate, gain):
    spread = np.zeros((2 * HEADS, CHAN), np.float32)
    for h in range(HEADS):
        for part in range(2):
            spread[part * HEADS + h, h * PSIZE : (h + 1) * PSIZE] = 1
    return pl.pallas_call(
        finish_kernel,
        grid=(TOK // SPAN,),
        in_specs=[
            pl.BlockSpec((SPAN, CHAN), lambda s: (s, 0)),
            pl.BlockSpec((SPAN, STATE), lambda s: (s, 0)),
            pl.BlockSpec((HEADS, SPAN), lambda s: (0, s)),
            pl.BlockSpec((CHAN, STATE), lambda s: (0, 0)),
            pl.BlockSpec((SPAN, CHAN), lambda s: (s, 0)),
            pl.BlockSpec((1, CHAN), lambda s: (0, 0)),
            pl.BlockSpec((2 * HEADS, CHAN), lambda s: (0, 0)),
        ],
        out_specs=pl.BlockSpec((SPAN, CHAN), lambda s: (s, 0)),
        out_shape=jax.ShapeDtypeStruct((TOK, CHAN), BF),
        compiler_params=pltpu.CompilerParams(vmem_limit_bytes=VMEM_LIMIT),
        cost_estimate=pl.CostEstimate(flops=2 << 30, bytes_accessed=10 << 20, transcendentals=1 << 20),
    )(y, cmat, logs, entering, gate, gain, jnp.asarray(spread, BF))


def attend_kernel(
    list_ref,
    q_ref,
    *refs,
    planes,
):
    pieces = refs[: 2 * planes]
    out_ref, kv, sums, top, qq, sa, sb, ma, mb, sems = refs[2 * planes :]
    sub = 256

    def copies():
        found = []
        for p in range(planes):
            for side in range(2):
                for slot in range(NZ):
                    found.append(
                        pltpu.make_async_copy(
                            pieces[2 * p + side].at[slot],
                            kv.at[p * NZ + slot, pl.ds(side * TOK, TOK)],
                            sems.at[(p * 2 + side) * NZ + slot],
                        )
                    )
        return found

    @pl.when(pl.program_id(0) == 0)
    def _():
        for copy in copies():
            copy.start()

    scaled = q_ref[...].astype(F32) * (HD**-0.5 * math.log2(math.e))
    high = scaled.astype(BF)
    low = (scaled - high.astype(F32)).astype(BF)
    qq[...] = jnp.concatenate([high, low], axis=1)
    sums[...] = jnp.zeros_like(sums)
    top[...] = jnp.full_like(top, -1e30)

    @pl.when(pl.program_id(0) == 0)
    def _():
        for copy in copies():
            copy.wait()

    count = list_ref[0]
    core = list_ref[1]
    ones = jnp.ones((CHUNK, HD), BF)

    def score(at, s_ref, m_ref, masked=False):
        keys = kv[at, :, :HD]
        twice = jnp.concatenate([keys, keys], axis=1)
        for r in range(TOK // sub):
            rows = slice(r * sub, (r + 1) * sub)
            s = lax.dot_general(
                qq[rows, :], twice, (((1,), (1,)), ((), ())), preferred_element_type=F32
            )
            if masked:
                row = lax.broadcasted_iota(jnp.int32, s.shape, 0) + r * sub
                key = lax.broadcasted_iota(jnp.int32, s.shape, 1)
                limit = jnp.where(core == 1, 2 * TOK, TOK)
                seen = ((key < TOK) & (key <= row)) | ((key >= TOK) & (key < limit))
                s = jnp.where(seen, s, -1e30)
            s_ref[rows, :] = s
            m_ref[rows, :] = jnp.broadcast_to(jnp.max(s, axis=1, keepdims=True), (sub, HD))

    def gather(at, s_ref, m_ref):
        values = jnp.concatenate([kv[at, :, HD:], ones], axis=1)
        for r in range(TOK // sub):
            rows = slice(r * sub, (r + 1) * sub)
            old = top[rows, :]
            new = jnp.maximum(old, m_ref[rows, :])
            weights = jnp.exp2(s_ref[rows, :] - new[:, :1]).astype(BF)
            factor = jnp.exp2(old - new)
            part = jnp.dot(weights, values, preferred_element_type=F32)
            sums[rows, :] = sums[rows, :] * jnp.concatenate([factor, factor], axis=1) + part
            top[rows, :] = new

    def chunk(i):
        return list_ref[2 + jnp.minimum(i, count - 1)]

    score(chunk(0), sa, ma, masked=True)

    def body(j, _):
        i = 2 * j
        score(chunk(i + 1), sb, mb)
        gather(chunk(i), sa, ma)
        score(chunk(i + 2), sa, ma)
        gather(chunk(i + 1), sb, mb)
        return 0

    lax.fori_loop(0, count // 2, body, 0)

    @pl.when(count % 2 == 1)
    def _():
        gather(chunk(count - 1), sa, ma)

    out_ref[...] = (sums[:, :HD] / sums[:, HD:]).astype(BF)


def attend(order, query, pieces):
    planes = len(pieces) // 2
    return pl.pallas_call(
        functools.partial(attend_kernel, planes=planes),
        grid=(4,),
        in_specs=[
            pl.BlockSpec(memory_space=pltpu.SMEM),
            pl.BlockSpec((TOK, HD), lambda h: (0, h)),
        ]
        + [pl.BlockSpec(memory_space=pl.ANY)] * len(pieces),
        out_specs=pl.BlockSpec((TOK, HD), lambda h: (0, h)),
        out_shape=jax.ShapeDtypeStruct((TOK, 4 * HD), BF),
        scratch_shapes=[
            pltpu.VMEM((planes * NZ, CHUNK, 2 * HD), BF),
            pltpu.VMEM((TOK, 2 * HD), F32),
            pltpu.VMEM((TOK, HD), F32),
            pltpu.VMEM((TOK, 2 * HD), BF),
            pltpu.VMEM((TOK, CHUNK), F32),
            pltpu.VMEM((TOK, CHUNK), F32),
            pltpu.VMEM((TOK, HD), F32),
            pltpu.VMEM((TOK, HD), F32),
            pltpu.SemaphoreType.DMA((planes * 2 * NZ,)),
        ],
        compiler_params=pltpu.CompilerParams(vmem_limit_bytes=VMEM_LIMIT),
        cost_estimate=pl.CostEstimate(flops=50 << 30, bytes_accessed=10 << 20, transcendentals=32 << 20),
    )(order, query, *pieces)


def gathered_keys(key_heads, value_heads):
    own = jnp.concatenate([key_heads, value_heads], axis=1)
    up = along_z(own, 1)
    down = along_z(own, -1)
    two = along_z(up, 1)
    plane = jnp.stack([own, up, down, two])
    left = along_x(plane, 1, wrap=True)
    right = along_x(plane, -1, wrap=True)
    far = jnp.concatenate(
        [along_x(left[:2], 1, wrap=True), along_x(right[2:], -1, wrap=True)], axis=0
    )
    pieces = []
    for part in (plane, left, right, far):
        pieces += [part, swap_core(part)]
    return pieces


def visible_chunks(c, z, x):
    px = (x + jnp.array([0, -1, 1, -2])) % NX
    pz = (z + jnp.array([0, -1, 1, -2])) % NZ
    chip = (px[:, None] * NZ + pz[None, :]).reshape(-1)
    mine = x * NZ + z
    ids = jnp.arange(NX * NZ)
    rank = jnp.where(chip == mine, -1, jnp.where(chip < mine, ids, 99))
    place = jnp.sum(rank[None, :] < rank[:, None], axis=1)
    listed = jnp.sum(
        jnp.where((place[:, None] == ids[None, :]) & (rank[:, None] < 99), ids[:, None], 0), axis=0
    )
    return jnp.concatenate([jnp.stack([mine + 1, c]), listed]).astype(jnp.int32)


def local(
    hidden,
    dt_weight,
    dt_bias,
    decay_rate,
    skip_gain,
    ssm_in,
    bc_in,
    conv_x,
    conv_bc,
    gate_in,
    norm_gain,
    query_heads,
    key_heads,
    value_heads,
):
    mine = lax.axis_index("ctx")
    x, z, c = mine // (NZ * NC), (mine // NC) % NZ, mine % NC
    bc = bc_in.reshape(TOK, 2 * STATE)
    ends = jnp.concatenate([ssm_in[TOK - 16 :], bc[TOK - 16 :]], axis=1)
    tail = lax.ppermute(ends, "ctx", [(i, i + 1) for i in range(31)])
    partial = lax.dot_general(
        dt_weight, hidden, (((0,), (1,)), ((), ())), preferred_element_type=F32
    )
    parts = lax.all_to_all(partial.reshape(8, HEADS, TOK), "head", 0, 0, tiled=True)
    steps = jax.nn.softplus(jnp.sum(parts, axis=0) + dt_bias[:, None])
    total = -jnp.sum(steps, axis=1) * decay_rate
    logs = lax.all_gather(total, "ctx")
    y, cmat, grown, end = own_tokens(
        ssm_in,
        tail,
        bc,
        steps,
        decay_rate[:, None],
        jnp.repeat(skip_gain, PSIZE)[None],
        conv_x,
        conv_bc.reshape(4, 2 * STATE),
    )
    pieces = gathered_keys(key_heads, value_heads)
    entering = entering_state(end, logs, c, z, x)
    attn_out = attend(visible_chunks(c, z, x), query_heads, pieces)
    mamba_out = finish(y, cmat, grown, entering, gate_in, norm_gain[None])
    return (mamba_out, attn_out)


def solution(mesh):
    in_specs = (
        P("ctx", "head"),
        P("head", None),
        P("head"),
        P("head"),
        P("head"),
        P("ctx", "head"),
        P("ctx", "head", None),
        P(None, "head"),
        P(None, "head", None),
        P("ctx", "head"),
        P("head"),
        P("ctx", "head"),
        P("ctx", "head"),
        P("ctx", "head"),
    )
    out_specs = (P("ctx", "head"), P("ctx", "head"))
    return jax.shard_map(local, mesh=mesh, in_specs=in_specs, out_specs=out_specs, check_vma=False)
```

time: 624 us -> 248 us (0.40)
  the two profiles are of different devices: /device:TPU:35 before, /device:TPU:199 now
where the time goes in v1:
time: 248 us; the launch traced here: 246 us
  Pallas kernels  78.1 us (31%)
  blocking collectives  69.8 us (28%)
  waiting for transfers between devices  38.6 us (16%)
  starting transfers between devices  33.3 us (13%)
  local copies, waits for them, and re-layouts  12.1 us (5%)
  other arithmetic  10.1 us (4%)
    unnamed x1, blocking collectives  69.8 us
    pallas_call x1, Pallas kernels, attend(): pl.pallas_call(functools.partial(attend_kernel, planes=planes), grid=(4,)...  51.7 us
    ppermute x22, waiting for transfers between devices, send(): return lax.ppermute(value, 'ctx', pairs_of(move))  38.6 us
    ppermute x22, starting transfers between devices, send(): return lax.ppermute(value, 'ctx', pairs_of(move))  27.3 us
    pallas_call x1, Pallas kernels, own_tokens(): pl.pallas_call(span_kernel, grid=grid, in_specs=[pl.BlockSpec((SPAN, HBC)...  19.3 us
    pallas_call x1, Pallas kernels, finish(): pl.pallas_call(finish_kernel, grid=(TOK // SPAN,), in_specs=[pl.BlockSpec...  7.09 us
  transfers between devices with their start and end apart: 24, of which 9 were waited for; matrix products, arithmetic and copies ran while one was open for 9% of the time, Pallas kernels for 11%

profile of v1, /device:TPU:199, one launch (start us, length us, event | category | flops | bytes accessed | tf_op | source)
XLA Modules:
  0.0 246.5 jit_solution(7264297012768407332)
XLA Ops:
  0.7 1.0 constant_dynamic-update-slice_fusion.1
  1.7 1.0 constant_dynamic-update-slice_fusion
  2.8 2.4 collective-permute-start.13
  5.1 2.3 fusion.52
  7.5 4.8 %all-to-all-start = ((f32[8,32,512]{2,1,0:T(8,128)}), f32[8,32,512]{2,1,0:T(8,128)S(1)}, u32[]{:S(2)}, u32[]{:S(2)}) async-start(f32[8,32,512]{2,1,0:T(8,128)} %bitcast.2), calls=%async_computation | async-start | bytes 1048576 | tf_op jit(solution)/shard_map/all_to_all | solution.py:548
  12.2 0.7 slice_bitcast_fusion
  13.0 1.3 collective-permute-start
  14.5 4.1 %collective-permute-start.14 = (bf16[512,256]{1,0:T(8,128)(2,1)S(1)}, bf16[512,256]{1,0:T(8,128)(2,1)S(1)}, u32[]{:S(2)}, u32[]{:S(2)}) collective-permute-start(bf16[512,256]{1,0:T(8,128)(2,1)S(1)} %collective-permute-done.12), channel_id=1, source_target_pairs={{0,16},{8,24},{16,32},{24,40},{32,48},{40,56},{48,0},{56,8},{64,80... | collective-permute-start | bytes 786440 | tf_op jit(solution)/shard_map/ppermute | solution.py:39
  19.0 0.7 broadcast_in_dim_reshape.3.skip_ref
  19.7 0.7 copy.24.rate_ref
  20.4 0.6 copy.27
  21.0 0.6 dynamic-slice.5
  22.3 13.7 %collective-permute-done.14 = bf16[512,256]{1,0:T(8,128)(2,1)S(1)} collective-permute-done((bf16[512,256]{1,0:T(8,128)(2,1)S(1)}, bf16[512,256]{1,0:T(8,128)(2,1)S(1)}, u32[]{:S(2)}, u32[]{:S(2)}) %collective-permute-start.14) | collective-permute-done | bytes 262176 | tf_op jit(solution)/shard_map/ppermute | solution.py:39
  36.0 1.1 pad_maximum_fusion.1.refs_0_
  37.1 0.2 collective-permute-start.16
  37.3 1.3 collective-permute-start.18
  38.6 0.8 fusion.51
  39.5 0.1 multiply_dynamic-update-slice_fusion
  39.6 69.8 %all-reduce.2 = f32[1024]{0:T(1024)S(1)} all-reduce(f32[1024]{0:T(1024)S(1)} %multiply_dynamic-update-slice_fusion), channel_id=2, replica_groups=mesh['ctx'=32,'head'=8] {'ctx'}, use_global_device_ids=true, to_apply=%add.2 | all-reduce | flops 1024 | bytes 8192
  109.4 0.1 reshape.317
  109.8 0.6 copy-done.7
  110.4 19.3 %shard_map.203 = (f32[512,2048]{1,0:T(8,128)}, bf16[512,256]{1,0:T(8,128)(2,1)}, f32[32,512]{1,0:T(8,128)}, bf16[2048,256]{1,0:T(8,128)(2,1)}) custom-call(bf16[512,2048]{1,0:T(8,128)(2,1)} %before_ref.1, bf16[512,2048]{1,0:T(8,128)(2,1)} %before_ref.1, bf16[16,2560]{1,0:T(8,128)(2,1)} %copy-done.7, bf16[512,512]{1,0:T(8,128)(2,1)} %bitcast.160, ...), custom_call_target="tpu_custom_call" | custom-call | flops 8589934592 | bytes 12582912 | tf_op jit(solution)/shard_map/pallas_call | solution.py:208
  129.7 1.1 dynamic-slice_bitcast_fusion
  130.8 0.1 collective-permute-start.1
  131.0 0.6 gather_fusion
  131.7 1.1 collective-permute-done.1
  132.8 1.3 fusion.1
  134.2 0.1 collective-permute-start.3
  134.3 2.3 collective-permute-start.4
  136.6 3.5 %collective-permute-done.2 = bf16[4,64,256]{2,1,0:T(8,128)(2,1)S(1)} collective-permute-done((bf16[4,64,256]{2,1,0:T(8,128)(2,1)S(1)}, bf16[4,64,256]{2,1,0:T(8,128)(2,1)S(1)}, u32[]{:S(2)}, u32[]{:S(2)}) %collective-permute-start.2) | collective-permute-done | bytes 131104 | tf_op jit(solution)/shard_map/ppermute | solution.py:39
  140.1 3.5 %collective-permute-done.3 = bf16[4,64,256]{2,1,0:T(8,128)(2,1)S(1)} collective-permute-done((bf16[4,64,256]{2,1,0:T(8,128)(2,1)S(1)}, bf16[4,64,256]{2,1,0:T(8,128)(2,1)S(1)}, u32[]{:S(2)}, u32[]{:S(2)}) %collective-permute-start.3) | collective-permute-done | bytes 131104 | tf_op jit(solution)/shard_map/ppermute | solution.py:39
  143.6 0.6 collective-permute-done.4
  144.2 0.2 fusion.13
  144.4 1.3 collective-permute-start.5
  145.7 1.3 collective-permute-start.6
  147.0 1.3 collective-permute-start.7
  148.3 2.3 collective-permute-done.5
  150.6 2.8 %collective-permute-done.6 = bf16[4,64,256]{2,1,0:T(8,128)(2,1)S(1)} collective-permute-done((bf16[4,64,256]{2,1,0:T(8,128)(2,1)S(1)}, bf16[4,64,256]{2,1,0:T(8,128)(2,1)S(1)}, u32[]{:S(2)}, u32[]{:S(2)}) %collective-permute-start.6) | collective-permute-done | bytes 131104 | tf_op jit(solution)/shard_map/ppermute | solution.py:39
  153.4 6.2 %collective-permute-done.7 = bf16[4,64,256]{2,1,0:T(8,128)(2,1)S(1)} collective-permute-done((bf16[4,64,256]{2,1,0:T(8,128)(2,1)S(1)}, bf16[4,64,256]{2,1,0:T(8,128)(2,1)S(1)}, u32[]{:S(2)}, u32[]{:S(2)}) %collective-permute-start.7) | collective-permute-done | bytes 131104 | tf_op jit(solution)/shard_map/ppermute | solution.py:39
  159.6 0.3 fusion.32
  159.9 0.3 fusion.29
  160.1 0.3 fusion.31
  160.4 0.3 fusion.30
  160.8 1.1 collective-permute-start.8
  162.0 2.6 %collective-permute-start.9 = (bf16[4,64,256]{2,1,0:T(8,128)(2,1)S(1)}, bf16[4,64,256]{2,1,0:T(8,128)(2,1)S(1)}, u32[]{:S(2)}, u32[]{:S(2)}) collective-permute-start(bf16[4,64,256]{2,1,0:T(8,128)(2,1)S(1)} %get-tuple-element.22), channel_id=1, source_target_pairs={{0,32},{8,40},{16,48},{24,56},{32,0},{40,8},{48,16},{56,24},{64,96... | collective-permute-start | bytes 393224 | tf_op jit(solution)/shard_map/ppermute | solution.py:39
  164.5 0.7 collective-permute-start.10
  165.2 1.1 slice.144
  166.4 1.1 slice.145
  167.6 1.5 collective-permute-start.21
  169.0 4.8 %collective-permute-done.9 = bf16[4,64,256]{2,1,0:T(8,128)(2,1)S(1)} collective-permute-done((bf16[4,64,256]{2,1,0:T(8,128)(2,1)S(1)}, bf16[4,64,256]{2,1,0:T(8,128)(2,1)S(1)}, u32[]{:S(2)}, u32[]{:S(2)}) %collective-permute-start.9) | collective-permute-done | bytes 131104 | tf_op jit(solution)/shard_map/ppermute | solution.py:39
  174.1 1.1 fusion.3
  175.2 2.1 collective-permute-start.11
  177.4 0.2 convert_reduce_fusion
  177.6 0.5 collective-permute-start.17
  178.1 2.6 %collective-permute-start.19 = (bf16[4,512,256]{2,1,0:T(8,128)(2,1)}, bf16[4,512,256]{2,1,0:T(8,128)(2,1)}, u32[]{:S(2)}, u32[]{:S(2)}) collective-permute-start(bf16[4,512,256]{2,1,0:T(8,128)(2,1)} %collective-permute-done.18.refs_4_), channel_id=1, source_target_pairs={{0,8},{8,0},{16,24},{24,16},{32,40},{40,32},{48,56},{56,48},{64,72... | collective-permute-start | bytes 3145736 | tf_op jit(solution)/shard_map/ppermute | solution.py:39
  180.7 0.9 constant_dynamic-update-slice_fusion.3
  181.6 0.8 constant_dynamic-update-slice_fusion.2.refs_6_
  182.5 1.6 collective-permute-start.22
  184.0 0.1 select_reduce_fusion
  184.1 0.7 pad_add_fusion.list_ref
  184.8 1.5 select_bitcast_fusion.1
  186.4 1.1 pad_maximum_fusion
  187.5 7.1 %shard_map.204 = bf16[512,2048]{1,0:T(8,128)(2,1)} custom-call(f32[512,2048]{1,0:T(8,128)} %get-tuple-element.6.y_ref, bf16[512,256]{1,0:T(8,128)(2,1)} %get-tuple-element.7.c_ref, f32[32,512]{1,0:T(8,128)} %get-tuple-element.8.log_ref, bf16[2048,256]{1,0:T(8,128)(2,1)} %bitcast.148, bf16[512,2048]{1,0:T(8,128)(2,1)} %gate_ref.1, f32[1,2048]{1,0:T(1,128)} %bitcast.158, ...), custom_call_target="tpu_custom_call" | custom-call | flops 2147483648 | bytes 10485760 | tf_op jit(solution)/shard_map/pallas_call | solution.py:350
  194.6 51.7 %shard_map.205 = bf16[512,512]{1,0:T(8,128)(2,1)} custom-call(s32[18]{0:T(128)} %pad_add_fusion.list_ref, bf16[512,512]{1,0:T(8,128)(2,1)} %q_ref.1, bf16[4,512,256]{2,1,0:T(8,128)(2,1)} %pad_maximum_fusion.1.refs_0_, bf16[4,512,256]{2,1,0:T(8,128)(2,1)} %collective-permute-done.15.refs_1_, bf16[4,512,256]{2,1,0:T(8,128)(2,1)} %collective-permute-done.16.refs_2_, ...), custom_call_target="tpu_custom_call" | custom-call | flops 53687091200 | bytes 10485760 | tf_op jit(solution)/shard_map/pallas_call | solution.py:467
  (71 shorter events, 1.7 us)
Async XLA Ops:
  0.6 4.5 %copy-start = (bf16[512,1024]{1,0:T(8,128)(2,1)S(1)}, bf16[512,1024]{1,0:T(8,128)(2,1)}, u32[]{:S(2)}) copy-start(bf16[512,1024]{1,0:T(8,128)(2,1)} %param.20) | copy-start | bytes 3145732
  0.6 13.7 %copy-start.6 = (s32[4]{0:T(128)S(1)}, s32[4]{0:T(128)}, u32[]{:S(2)}) copy-start(s32[4]{0:T(128)} %constant.300.clone) | copy-start | bytes 52
  0.7 12.3 %slice-start = ((bf16[512,2048]{1,0:T(8,128)(2,1)}), bf16[16,2048]{1,0:T(8,128)(2,1)S(1)}, s32[]{:S(2)}) async-start(bf16[512,2048]{1,0:T(8,128)(2,1)} %before_ref.1), calls=%async_computation.1 | async-start | bytes 131072 | tf_op jit(solution)/shard_map/slice | solution.py:543
  1.7 17.3 %copy-start.5 = (f32[32]{0:T(128)S(1)}, f32[32]{0:T(128)}, u32[]{:S(2)}) copy-start(f32[32]{0:T(128)} %param.24) | copy-start | bytes 388
  1.7 18.0 %copy-start.3 = (f32[32]{0:T(128)S(1)}, f32[32]{0:T(128)}, u32[]{:S(2)}) copy-start(f32[32]{0:T(128)} %param.23) | copy-start | bytes 388
  1.7 18.7 %copy-start.2 = (f32[4,1,512]{2,1,0:T(1,128)S(1)}, f32[4,1,512]{2,1,0:T(1,128)}, u32[]{:S(2)}) copy-start(f32[4,1,512]{2,1,0:T(1,128)} %param.28) | copy-start | bytes 24580
  1.7 19.3 %copy-start.8 = (u32[256]{0:T(256)S(1)}, u32[256]{0:T(256)}, u32[]{:S(2)}) copy-start(u32[256]{0:T(256)} %constant.309) | copy-start | bytes 3076
  2.7 11.8 %collective-permute-start.12 = (bf16[512,256]{1,0:T(8,128)(2,1)S(1)}, bf16[512,256]{1,0:T(8,128)(2,1)S(1)}, u32[]{:S(2)}, u32[]{:S(2)}) collective-permute-start(bf16[512,256]{1,0:T(8,128)(2,1)S(1)} %constant_dynamic-update-slice_fusion), channel_id=1, source_target_pairs={{0,16},{8,24},{16,32},{24,40},{32,48},{40,56},{48,0},{56,8},{64,80... | collective-permute-start | bytes 786440 | tf_op jit(solution)/shard_map/ppermute | solution.py:39
  2.8 19.5 %collective-permute-start.13 = (bf16[512,256]{1,0:T(8,128)(2,1)S(1)}, bf16[512,256]{1,0:T(8,128)(2,1)S(1)}, u32[]{:S(2)}, u32[]{:S(2)}) collective-permute-start(bf16[512,256]{1,0:T(8,128)(2,1)S(1)} %constant_dynamic-update-slice_fusion), channel_id=1, source_target_pairs={{0,48},{8,56},{16,0},{24,8},{32,16},{40,24},{48,32},{56,40},{64,11... | collective-permute-start | bytes 786440 | tf_op jit(solution)/shard_map/ppermute | solution.py:39
  7.5 31.2 %copy-start.4 = (f32[32]{0:T(128)S(1)}, f32[32]{0:T(128)}, u32[]{:S(2)}) copy-start(f32[32]{0:T(128)} %param.22) | copy-start | bytes 388
  7.5 31.1 %all-to-all-start = ((f32[8,32,512]{2,1,0:T(8,128)}), f32[8,32,512]{2,1,0:T(8,128)S(1)}, u32[]{:S(2)}, u32[]{:S(2)}) async-start(f32[8,32,512]{2,1,0:T(8,128)} %bitcast.2), calls=%async_computation | async-start | bytes 1048576 | tf_op jit(solution)/shard_map/all_to_all | solution.py:548
  13.0 96.8 %collective-permute-start = (bf16[16,2560]{1,0:T(8,128)(2,1)S(1)}, bf16[16,2560]{1,0:T(8,128)(2,1)S(1)}, u32[]{:S(2)}, u32[]{:S(2)}) collective-permute-start(bf16[16,2560]{1,0:T(8,128)(2,1)S(1)} %pad_maximum_fusion.5), channel_id=1, source_target_pairs={{0,8},{8,16},{16,24},{24,32},{32,40},{40,48},{48,56},{56,64},{64,7... | collective-permute-start | bytes 245768 | tf_op jit(solution)/shard_map/ppermute | solution.py:544
  14.5 21.6 %collective-permute-start.14 = (bf16[512,256]{1,0:T(8,128)(2,1)S(1)}, bf16[512,256]{1,0:T(8,128)(2,1)S(1)}, u32[]{:S(2)}, u32[]{:S(2)}) collective-permute-start(bf16[512,256]{1,0:T(8,128)(2,1)S(1)} %collective-permute-done.12), channel_id=1, source_target_pairs={{0,16},{8,24},{16,32},{24,40},{32,48},{40,56},{48,0},{56,8},{64,80... | collective-permute-start | bytes 786440 | tf_op jit(solution)/shard_map/ppermute | solution.py:39
  37.1 128.1 %collective-permute-start.16 = (bf16[4,512,256]{2,1,0:T(8,128)(2,1)}, bf16[4,512,256]{2,1,0:T(8,128)(2,1)}, u32[]{:S(2)}, u32[]{:S(2)}) collective-permute-start(bf16[4,512,256]{2,1,0:T(8,128)(2,1)} %pad_maximum_fusion.1.refs_0_), channel_id=1, source_target_pairs={{0,64},{8,72},{16,80},{24,88},{32,96},{40,104},{48,112},{56,120},{... | collective-permute-start | bytes 3145736 | tf_op jit(solution)/shard_map/ppermute | solution.py:39
  37.3 129.1 %collective-permute-start.18 = (bf16[4,512,256]{2,1,0:T(8,128)(2,1)}, bf16[4,512,256]{2,1,0:T(8,128)(2,1)}, u32[]{:S(2)}, u32[]{:S(2)}) collective-permute-start(bf16[4,512,256]{2,1,0:T(8,128)(2,1)} %pad_maximum_fusion.1.refs_0_), channel_id=1, source_target_pairs={{0,192},{8,200},{16,208},{24,216},{32,224},{40,232},{48,240},{56,2... | collective-permute-start | bytes 3145736 | tf_op jit(solution)/shard_map/ppermute | solution.py:39
  109.8 0.6 copy-start.7
  130.8 2.0 collective-permute-start.1
  134.1 5.9 %collective-permute-start.2 = (bf16[4,64,256]{2,1,0:T(8,128)(2,1)S(1)}, bf16[4,64,256]{2,1,0:T(8,128)(2,1)S(1)}, u32[]{:S(2)}, u32[]{:S(2)}) collective-permute-start(bf16[4,64,256]{2,1,0:T(8,128)(2,1)S(1)} %get-tuple-element.24), channel_id=1, source_target_pairs={{0,16},{8,24},{16,32},{24,40},{32,48},{40,56},{48,0},{56,8},{64,80... | collective-permute-start | bytes 393224 | tf_op jit(solution)/shard_map/ppermute | solution.py:39
  134.2 9.3 %collective-permute-start.3 = (bf16[4,64,256]{2,1,0:T(8,128)(2,1)S(1)}, bf16[4,64,256]{2,1,0:T(8,128)(2,1)S(1)}, u32[]{:S(2)}, u32[]{:S(2)}) collective-permute-start(bf16[4,64,256]{2,1,0:T(8,128)(2,1)S(1)} %get-tuple-element.26), channel_id=1, source_target_pairs={{0,32},{8,40},{16,48},{24,56},{32,0},{40,8},{48,16},{56,24},{64,96... | collective-permute-start | bytes 393224 | tf_op jit(solution)/shard_map/ppermute | solution.py:39
  134.3 9.8 %collective-permute-start.4 = (bf16[4,64,256]{2,1,0:T(8,128)(2,1)S(1)}, bf16[4,64,256]{2,1,0:T(8,128)(2,1)S(1)}, u32[]{:S(2)}, u32[]{:S(2)}) collective-permute-start(bf16[4,64,256]{2,1,0:T(8,128)(2,1)S(1)} %get-tuple-element.25), channel_id=1, source_target_pairs={{0,48},{8,56},{16,0},{24,8},{32,16},{40,24},{48,32},{56,40},{64,11... | collective-permute-start | bytes 393224 | tf_op jit(solution)/shard_map/ppermute | solution.py:39
  144.4 6.2 %collective-permute-start.5 = (bf16[4,64,256]{2,1,0:T(8,128)(2,1)S(1)}, bf16[4,64,256]{2,1,0:T(8,128)(2,1)S(1)}, u32[]{:S(2)}, u32[]{:S(2)}) collective-permute-start(bf16[4,64,256]{2,1,0:T(8,128)(2,1)S(1)} %fusion.13), channel_id=1, source_target_pairs={{0,64},{8,72},{16,80},{24,88},{32,96},{40,104},{48,112},{56,120},{... | collective-permute-start | bytes 393224 | tf_op jit(solution)/shard_map/ppermute | solution.py:39
  145.7 7.7 %collective-permute-start.6 = (bf16[4,64,256]{2,1,0:T(8,128)(2,1)S(1)}, bf16[4,64,256]{2,1,0:T(8,128)(2,1)S(1)}, u32[]{:S(2)}, u32[]{:S(2)}) collective-permute-start(bf16[4,64,256]{2,1,0:T(8,128)(2,1)S(1)} %fusion.13), channel_id=1, source_target_pairs={{0,128},{8,136},{16,144},{24,152},{32,160},{40,168},{48,176},{56,1... | collective-permute-start | bytes 393224 | tf_op jit(solution)/shard_map/ppermute | solution.py:39
  147.0 12.7 %collective-permute-start.7 = (bf16[4,64,256]{2,1,0:T(8,128)(2,1)S(1)}, bf16[4,64,256]{2,1,0:T(8,128)(2,1)S(1)}, u32[]{:S(2)}, u32[]{:S(2)}) collective-permute-start(bf16[4,64,256]{2,1,0:T(8,128)(2,1)S(1)} %fusion.13), channel_id=1, source_target_pairs={{0,192},{8,200},{16,208},{24,216},{32,224},{40,232},{48,240},{56,2... | collective-permute-start | bytes 393224 | tf_op jit(solution)/shard_map/ppermute | solution.py:39
  160.8 8.2 %collective-permute-start.8 = (bf16[4,64,256]{2,1,0:T(8,128)(2,1)S(1)}, bf16[4,64,256]{2,1,0:T(8,128)(2,1)S(1)}, u32[]{:S(2)}, u32[]{:S(2)}) collective-permute-start(bf16[4,64,256]{2,1,0:T(8,128)(2,1)S(1)} %get-tuple-element.23), channel_id=1, source_target_pairs={{0,16},{8,24},{16,32},{24,40},{32,48},{40,56},{48,0},{56,8},{64,80... | collective-permute-start | bytes 393224 | tf_op jit(solution)/shard_map/ppermute | solution.py:39
  162.0 11.9 %collective-permute-start.9 = (bf16[4,64,256]{2,1,0:T(8,128)(2,1)S(1)}, bf16[4,64,256]{2,1,0:T(8,128)(2,1)S(1)}, u32[]{:S(2)}, u32[]{:S(2)}) collective-permute-start(bf16[4,64,256]{2,1,0:T(8,128)(2,1)S(1)} %get-tuple-element.22), channel_id=1, source_target_pairs={{0,32},{8,40},{16,48},{24,56},{32,0},{40,8},{48,16},{56,24},{64,96... | collective-permute-start | bytes 393224 | tf_op jit(solution)/shard_map/ppermute | solution.py:39
  164.5 9.3 %collective-permute-start.10 = (bf16[4,64,256]{2,1,0:T(8,128)(2,1)S(1)}, bf16[4,64,256]{2,1,0:T(8,128)(2,1)S(1)}, u32[]{:S(2)}, u32[]{:S(2)}) collective-permute-start(bf16[4,64,256]{2,1,0:T(8,128)(2,1)S(1)} %get-tuple-element.21), channel_id=1, source_target_pairs={{0,48},{8,56},{16,0},{24,8},{32,16},{40,24},{48,32},{56,40},{64,11... | collective-permute-start | bytes 393224 | tf_op jit(solution)/shard_map/ppermute | solution.py:39
  166.3 7.8 %copy-start.1 = (bf16[2048,256]{1,0:T(8,128)(2,1)S(1)}, bf16[2048,256]{1,0:T(8,128)(2,1)}, u32[]{:S(2)}) copy-start(bf16[2048,256]{1,0:T(8,128)(2,1)} %get-tuple-element.9) | copy-start | bytes 3145732
  166.3 11.8 %collective-permute-start.20 = (bf16[2,512,256]{2,1,0:T(8,128)(2,1)S(1)}, bf16[2,512,256]{2,1,0:T(8,128)(2,1)S(1)}, u32[]{:S(2)}, u32[]{:S(2)}) collective-permute-start(bf16[2,512,256]{2,1,0:T(8,128)(2,1)S(1)} %slice.144), channel_id=1, source_target_pairs={{0,64},{8,72},{16,80},{24,88},{32,96},{40,104},{48,112},{56,120},{... | collective-permute-start | bytes 1572872 | tf_op jit(solution)/shard_map/ppermute | solution.py:39
  167.6 14.1 %collective-permute-start.21 = (bf16[2,512,256]{2,1,0:T(8,128)(2,1)S(1)}, bf16[2,512,256]{2,1,0:T(8,128)(2,1)S(1)}, u32[]{:S(2)}, u32[]{:S(2)}) collective-permute-start(bf16[2,512,256]{2,1,0:T(8,128)(2,1)S(1)} %slice.145), channel_id=1, source_target_pairs={{0,192},{8,200},{16,208},{24,216},{32,224},{40,232},{48,240},{56,2... | collective-permute-start | bytes 1572872 | tf_op jit(solution)/shard_map/ppermute | solution.py:39
  175.2 9.6 %collective-permute-start.11 = (bf16[16,64,256]{2,1,0:T(8,128)(2,1)}, bf16[16,64,256]{2,1,0:T(8,128)(2,1)}, u32[]{:S(2)}, u32[]{:S(2)}) collective-permute-start(bf16[16,64,256]{2,1,0:T(8,128)(2,1)} %fusion.3), channel_id=1, source_target_pairs={{0,8},{8,0},{16,24},{24,16},{32,40},{40,32},{48,56},{56,48},{64,72... | collective-permute-start | bytes 1572872 | tf_op jit(solution)/shard_map/ppermute | solution.py:39
  177.5 17.1 %collective-permute-start.15 = (bf16[4,512,256]{2,1,0:T(8,128)(2,1)}, bf16[4,512,256]{2,1,0:T(8,128)(2,1)}, u32[]{:S(2)}, u32[]{:S(2)}) collective-permute-start(bf16[4,512,256]{2,1,0:T(8,128)(2,1)} %pad_maximum_fusion.1.refs_0_), channel_id=1, source_target_pairs={{0,8},{8,0},{16,24},{24,16},{32,40},{40,32},{48,56},{56,48},{64,72... | collective-permute-start | bytes 3145736 | tf_op jit(solution)/shard_map/ppermute | solution.py:39
  177.6 17.0 %collective-permute-start.17 = (bf16[4,512,256]{2,1,0:T(8,128)(2,1)}, bf16[4,512,256]{2,1,0:T(8,128)(2,1)}, u32[]{:S(2)}, u32[]{:S(2)}) collective-permute-start(bf16[4,512,256]{2,1,0:T(8,128)(2,1)} %collective-permute-done.16.refs_2_), channel_id=1, source_target_pairs={{0,8},{8,0},{16,24},{24,16},{32,40},{40,32},{48,56},{56,48},{64,72... | collective-permute-start | bytes 3145736 | tf_op jit(solution)/shard_map/ppermute | solution.py:39
  178.1 16.5 %collective-permute-start.19 = (bf16[4,512,256]{2,1,0:T(8,128)(2,1)}, bf16[4,512,256]{2,1,0:T(8,128)(2,1)}, u32[]{:S(2)}, u32[]{:S(2)}) collective-permute-start(bf16[4,512,256]{2,1,0:T(8,128)(2,1)} %collective-permute-done.18.refs_4_), channel_id=1, source_target_pairs={{0,8},{8,0},{16,24},{24,16},{32,40},{40,32},{48,56},{56,48},{64,72... | collective-permute-start | bytes 3145736 | tf_op jit(solution)/shard_map/ppermute | solution.py:39
  182.5 12.2 %collective-permute-start.22 = (bf16[4,512,256]{2,1,0:T(8,128)(2,1)}, bf16[4,512,256]{2,1,0:T(8,128)(2,1)}, u32[]{:S(2)}, u32[]{:S(2)}) collective-permute-start(bf16[4,512,256]{2,1,0:T(8,128)(2,1)} %constant_dynamic-update-slice_fusion.2.refs_6_), channel_id=1, source_target_pairs={{0,8},{8,0},{16,24},{24,16},{32,40},{40,32},{48,56},{56,48},{64,72... | collective-permute-start | bytes 3145736 | tf_op jit(solution)/shard_map/ppermute | solution.py:39

commit v2 on v1

v2 whole, which is shorter than its diff:
```python
import functools
import math

import jax
import jax.numpy as jnp
import numpy as np
from jax import lax
from jax.experimental import pallas as pl
from jax.experimental.pallas import tpu as pltpu
from jax.sharding import PartitionSpec as P

SPAN = 128
HD = 128
BF = jnp.bfloat16
F32 = jnp.float32
NX, NZ, NC = 4, 4, 2
HEADS, PSIZE, STATE = 32, 64, 256
CHAN = HEADS * PSIZE
TOK = 512
HB = 32
HBC = HB * PSIZE
CHUNK = 1024
VMEM_LIMIT = 58 << 20


def pairs_of(move):
    found = []
    for x in range(NX):
        for z in range(NZ):
            for c in range(NC):
                target = move(x, z, c)
                if target is not None:
                    tx, tz, tc = target
                    found.append(((x * NZ + z) * NC + c, (tx * NZ + tz) * NC + tc))
    return found


def send(value, move):
    return lax.ppermute(value, "ctx", pairs_of(move))


def swap_core(value):
    return send(value, lambda x, z, c: (x, z, 1 - c))


def along_z(value, steps):
    return send(value, lambda x, z, c: (x, (z + steps) % NZ, c))


def along_x(value, steps, wrap=False):
    def move(x, z, c):
        if wrap or 0 <= x + steps < NX:
            return ((x + steps) % NX, z, c)
        return None

    return send(value, move)


def shifted_rows(rows, tail, steps):
    if steps == 0:
        return rows
    rolled = pltpu.roll(rows, steps, 0)
    before = pltpu.roll(tail, steps, 0)
    at = lax.broadcasted_iota(jnp.int32, before.shape, 0)
    top = jnp.where(at < steps, before, rolled[:8])
    return jnp.concatenate([top, rolled[8:]], axis=0)


def conv_silu(rows, tail, taps):
    taps_count = taps.shape[0]
    total = None
    for k in range(taps_count):
        term = taps[k : k + 1] * shifted_rows(rows, tail, taps_count - 1 - k)
        total = term if total is None else total + term
    return (total * jax.nn.sigmoid(total)).astype(BF)


def two_parts(value):
    high = value.astype(BF).astype(F32)
    return [high, (value - high).astype(BF).astype(F32)]


def three_parts(value):
    high = value.astype(BF).astype(F32)
    return [high] + two_parts(value - high)


def states_kernel(
    core_ref,
    x_ref,
    before_ref,
    xtail_ref,
    pair_ref,
    pbefore_ref,
    ptail_ref,
    steps_ref,
    drop_ref,
    taps_ref,
    ptaps_ref,
    spread_ref,
    rows_ref,
    xin_ref,
    conv_ref,
    cum_ref,
    log_ref,
    start_ref,
    mine_ref,
    give_ref,
    b_s,
    ex_s,
    dec_s,
    log_s,
    state_s,
):
    span, block = pl.program_id(0), pl.program_id(1)

    @pl.when(block == 0)
    def _():
        @pl.when(span == 0)
        def _():
            log_s[...] = jnp.zeros_like(log_s)

        before = jnp.where(span == 0, ptail_ref[...], pbefore_ref[...]).astype(F32)[8:]
        pair = conv_silu(pair_ref[...].astype(F32), before, ptaps_ref[...])
        conv_ref[...] = pair
        b_s[...] = pair[:, :STATE]
        at_i = lax.broadcasted_iota(jnp.int32, (SPAN, SPAN), 0)
        at_j = lax.broadcasted_iota(jnp.int32, (SPAN, SPAN), 1)
        steps = steps_ref[...]
        upper = jnp.where(at_i <= at_j, 1.0, 0.0)
        cum = jnp.dot(
            drop_ref[...], upper, precision=lax.Precision.HIGHEST, preferred_element_type=F32
        )
        cum_ref[...] = cum
        last = cum[:, SPAN - 1 : SPAN]
        ex_s[...] = jnp.concatenate(
            two_parts(jnp.exp(last - cum) * steps) + [jnp.zeros((2 * HEADS, SPAN), F32)], axis=0
        ).T.astype(BF)
        dec_s[...] = jnp.broadcast_to(
            jnp.concatenate(two_parts(jnp.exp(last)), axis=0), dec_s.shape
        ).astype(BF)
        log_ref[...] = log_s[...] + cum
        log_s[...] = log_s[...] + last

    before = jnp.where(span == 0, xtail_ref[...], before_ref[...]).astype(F32)[8:]
    xin = conv_silu(x_ref[...].astype(F32), before, taps_ref[...])
    xin_ref[...] = xin
    spread = spread_ref[...]
    weight = jnp.dot(
        ex_s[...], jnp.concatenate([spread, jnp.zeros_like(spread)], axis=0), preferred_element_type=F32
    )
    weighted = (xin.astype(F32) * weight).astype(BF)
    gain = lax.dot_general(
        weighted, b_s[...], (((0,), (0,)), ((), ())), preferred_element_type=F32
    )
    decay = jnp.dot(rows_ref[...], dec_s[...], preferred_element_type=F32)
    state = jnp.where(span == 0, 0.0, state_s[block])
    start_ref[...] = state.astype(BF)
    state = state * decay + gain
    state_s[block] = state

    @pl.when(span == TOK // SPAN - 1)
    def _():
        low = state.astype(BF)
        first = core_ref[0] == 0
        mine_ref[...] = jnp.where(first, low[: CHAN // 2], low[CHAN // 2 :])
        give_ref[...] = jnp.where(first, low[CHAN // 2 :], low[: CHAN // 2])


def spread_rows():
    spread = np.zeros((2 * HEADS, CHAN), np.float32)
    for h in range(HEADS):
        for part in range(2):
            spread[part * HEADS + h, h * PSIZE : (h + 1) * PSIZE] = 1
    return spread


def own_states(core, ssm_in, tail, bc_in, steps, drop, conv_x, conv_bc):
    spread = spread_rows()
    blocks = HEADS // HB
    prior = lambda s, b: (jnp.maximum(s * (SPAN // 16) - 1, 0), b)
    prior0 = lambda s, b: (jnp.maximum(s * (SPAN // 16) - 1, 0), 0)
    return pl.pallas_call(
        states_kernel,
        grid=(TOK // SPAN, blocks),
        in_specs=[
            pl.BlockSpec(memory_space=pltpu.SMEM),
            pl.BlockSpec((SPAN, HBC), lambda s, b: (s, b)),
            pl.BlockSpec((16, HBC), prior),
            pl.BlockSpec((16, HBC), lambda s, b: (0, b)),
            pl.BlockSpec((SPAN, 2 * STATE), lambda s, b: (s, 0)),
            pl.BlockSpec((16, 2 * STATE), prior0),
            pl.BlockSpec((16, 2 * STATE), lambda s, b: (0, CHAN // (2 * STATE))),
            pl.BlockSpec((HEADS, SPAN), lambda s, b: (0, s)),
            pl.BlockSpec((HEADS, SPAN), lambda s, b: (0, s)),
            pl.BlockSpec((4, HBC), lambda s, b: (0, b)),
            pl.BlockSpec((4, 2 * STATE), lambda s, b: (0, 0)),
            pl.BlockSpec((2 * HEADS, HBC), lambda s, b: (0, b)),
            pl.BlockSpec((HBC, 2 * HEADS), lambda s, b: (b, 0)),
        ],
        out_specs=[
            pl.BlockSpec((SPAN, HBC), lambda s, b: (s, b)),
            pl.BlockSpec((SPAN, 2 * STATE), lambda s, b: (s, 0)),
            pl.BlockSpec((HEADS, SPAN), lambda s, b: (0, s)),
            pl.BlockSpec((HEADS, SPAN), lambda s, b: (0, s)),
            pl.BlockSpec((HBC, STATE), lambda s, b: (s * blocks + b, 0)),
            pl.BlockSpec((CHAN // 2, STATE), lambda s, b: (0, 0)),
            pl.BlockSpec((CHAN // 2, STATE), lambda s, b: (0, 0)),
        ],
        out_shape=[
            jax.ShapeDtypeStruct((TOK, CHAN), BF),
            jax.ShapeDtypeStruct((TOK, 2 * STATE), BF),
            jax.ShapeDtypeStruct((HEADS, TOK), F32),
            jax.ShapeDtypeStruct((HEADS, TOK), F32),
            jax.ShapeDtypeStruct((TOK // SPAN * CHAN, STATE), BF),
            jax.ShapeDtypeStruct((CHAN // 2, STATE), BF),
            jax.ShapeDtypeStruct((CHAN // 2, STATE), BF),
        ],
        scratch_shapes=[
            pltpu.VMEM((SPAN, STATE), BF),
            pltpu.VMEM((SPAN, 4 * HEADS), BF),
            pltpu.VMEM((2 * HEADS, STATE), BF),
            pltpu.VMEM((HEADS, SPAN), F32),
            pltpu.VMEM((blocks, HBC, STATE), F32),
        ],
        compiler_params=pltpu.CompilerParams(vmem_limit_bytes=VMEM_LIMIT),
        cost_estimate=pl.CostEstimate(flops=4 << 30, bytes_accessed=12 << 20, transcendentals=2 << 20),
    )(
        core,
        ssm_in,
        ssm_in,
        tail,
        bc_in,
        bc_in,
        tail,
        steps,
        drop,
        conv_x,
        conv_bc,
        jnp.asarray(spread, BF),
        jnp.asarray(spread.T, BF),
    )


def inside_kernel(
    xin_ref,
    pair_ref,
    cum_ref,
    steps_ref,
    start_ref,
    skip_ref,
    spread_ref,
    column_ref,
    y_ref,
    g_s,
    ci_s,
    ex_s,
):
    block = pl.program_id(1)
    cmat = pair_ref[:, STATE:]

    @pl.when(block == 0)
    def _():
        product = lax.dot_general(
            cmat, pair_ref[:, :STATE], (((1,), (1,)), ((), ())), preferred_element_type=F32
        )
        at_i = lax.broadcasted_iota(jnp.int32, (SPAN, SPAN), 0)
        at_j = lax.broadcasted_iota(jnp.int32, (SPAN, SPAN), 1)
        g_s[...] = jnp.where(at_j <= at_i, product, 0.0)
        cum = cum_ref[...]
        ci_s[...] = jnp.concatenate(three_parts(cum) + [jnp.zeros_like(cum)], axis=0).T.astype(BF)
        ex_s[...] = jnp.concatenate(
            two_parts(jnp.exp(cum)) + [jnp.zeros((2 * HEADS, SPAN), F32)], axis=0
        ).T.astype(BF)

    xf = xin_ref[...].astype(F32)
    spread = spread_ref[...]
    grown = jnp.dot(
        ex_s[...], jnp.concatenate([spread, jnp.zeros_like(spread)], axis=0), preferred_element_type=F32
    )
    rows_i = jnp.dot(ci_s[...], column_ref[...], preferred_element_type=F32)
    read = lax.dot_general(
        cmat, start_ref[...], (((1,), (1,)), ((), ())), preferred_element_type=F32
    )
    base = read * grown + skip_ref[...] * xf
    cum_rows = cum_ref[pl.ds(pl.multiple_of(block * HB, HB), HB), :]
    step_rows = steps_ref[pl.ds(pl.multiple_of(block * HB, HB), HB), :]
    masked = g_s[...]
    lane = lax.broadcasted_iota(jnp.int32, (SPAN, 2 * PSIZE), 1)
    for pair in range(HB // 2):
        mixes = []
        for h in (2 * pair, 2 * pair + 1):
            gap = rows_i[:, h * SPAN : (h + 1) * SPAN] - cum_rows[h : h + 1]
            mixes.append(
                (masked * jnp.exp(jnp.minimum(gap, 0.0)) * step_rows[h : h + 1]).astype(BF)
            )
        two = xf[:, pair * 128 : (pair + 1) * 128]
        left = jnp.where(lane < PSIZE, two, 0.0).astype(BF)
        right = jnp.where(lane < PSIZE, 0.0, two).astype(BF)
        intra = jnp.dot(
            jnp.concatenate(mixes, axis=1),
            jnp.concatenate([left, right], axis=0),
            preferred_element_type=F32,
        )
        y_ref[:, pair * 128 : (pair + 1) * 128] = base[:, pair * 128 : (pair + 1) * 128] + intra


def inside_blocks(xin, pair, cum, steps, starts, skip):
    column = np.zeros((4 * HEADS, HEADS * SPAN), np.float32)
    for h in range(HEADS):
        for part in range(3):
            column[part * HEADS + h, h * SPAN : (h + 1) * SPAN] = 1
    blocks = HEADS // HB
    return pl.pallas_call(
        inside_kernel,
        grid=(TOK // SPAN, blocks),
        in_specs=[
            pl.BlockSpec((SPAN, HBC), lambda s, b: (s, b)),
            pl.BlockSpec((SPAN, 2 * STATE), lambda s, b: (s, 0)),
            pl.BlockSpec((HEADS, SPAN), lambda s, b: (0, s)),
            pl.BlockSpec((HEADS, SPAN), lambda s, b: (0, s)),
            pl.BlockSpec((HBC, STATE), lambda s, b: (s * blocks + b, 0)),
            pl.BlockSpec((1, HBC), lambda s, b: (0, b)),
            pl.BlockSpec((2 * HEADS, HBC), lambda s, b: (0, b)),
            pl.BlockSpec((4 * HEADS, HB * SPAN), lambda s, b: (0, b)),
        ],
        out_specs=pl.BlockSpec((SPAN, HBC), lambda s, b: (s, b)),
        out_shape=jax.ShapeDtypeStruct((TOK, CHAN), F32),
        scratch_shapes=[
            pltpu.VMEM((SPAN, SPAN), F32),
            pltpu.VMEM((SPAN, 4 * HEADS), BF),
            pltpu.VMEM((SPAN, 4 * HEADS), BF),
        ],
        compiler_params=pltpu.CompilerParams(vmem_limit_bytes=VMEM_LIMIT),
        cost_estimate=pl.CostEstimate(flops=8 << 30, bytes_accessed=12 << 20, transcendentals=4 << 20),
    )(xin, pair, cum, steps, starts, skip, jnp.asarray(spread_rows(), BF), jnp.asarray(column, BF))


CHIPS = NX * NZ
SAME_CORE = [[2 * chip + core for chip in range(CHIPS)] for core in range(NC)]


def chain_kernel(decay_ref, from_ref, into_ref):
    carried = jnp.zeros(from_ref.shape[1:], F32)
    for chip in range(CHIPS):
        into_ref[chip] = carried.astype(BF)
        if chip < CHIPS - 1:
            carried = decay_ref[chip] * carried + from_ref[chip].astype(F32)


def chain(decays, states):
    return pl.pallas_call(
        chain_kernel,
        in_specs=[
            pl.BlockSpec(memory_space=pltpu.SMEM),
            pl.BlockSpec(memory_space=pltpu.VMEM),
        ],
        out_specs=pl.BlockSpec(memory_space=pltpu.VMEM),
        out_shape=jax.ShapeDtypeStruct(states.shape, BF),
        cost_estimate=pl.CostEstimate(flops=1 << 20, bytes_accessed=1 << 20, transcendentals=0),
    )(decays, states)


def exchanged(value):
    return lax.all_to_all(value, "ctx", 0, 0, tiled=True, axis_index_groups=SAME_CORE)


def decay_logs(total, mine):
    lead = total.reshape(2, 16).T.reshape(32, 1)
    rows = jnp.concatenate(
        [lead, jnp.broadcast_to(total[None], (32, HEADS)), jnp.zeros((32, 95), F32)], axis=1
    )
    got = lax.all_to_all(rows, "ctx", 0, 0, tiled=True)
    partner = lax.dynamic_index_in_dim(got, mine + 1 - 2 * (mine % NC), 0, False)[1 : 1 + HEADS]
    chip_decay = jnp.exp(jnp.sum(got[:, 0].reshape(CHIPS, NC), axis=1))
    return partner, chip_decay


def finish_kernel(
    core_ref, y_ref, c_ref, log_ref, in_ref, other_ref, gate_ref, gain_ref, spread_ref, out_ref
):
    grown = jnp.concatenate(
        two_parts(jnp.exp(log_ref[...])) + [jnp.zeros((2 * HEADS, SPAN), F32)], axis=0
    ).T.astype(BF)
    spread = spread_ref[...]
    scale = jnp.dot(
        grown, jnp.concatenate([spread, jnp.zeros_like(spread)], axis=0), preferred_element_type=F32
    )
    contract = (((1,), (1,)), ((), ()))
    kept = lax.dot_general(c_ref[...], in_ref[...], contract, preferred_element_type=F32)
    given = lax.dot_general(c_ref[...], other_ref[...], contract, preferred_element_type=F32)
    first = core_ref[0] == 0
    read = jnp.concatenate(
        [jnp.where(first, kept, given), jnp.where(first, given, kept)], axis=1
    )
    mixed = y_ref[...] + read * scale
    gate = gate_ref[...].astype(F32)
    gated = mixed * (gate * jax.nn.sigmoid(gate))
    mean = jnp.mean(gated * gated, axis=1, keepdims=True)
    out_ref[...] = (gated * lax.rsqrt(mean + 1e-05) * gain_ref[...]).astype(BF)


def finish(core, y, pair, logs, entering, other, gate, gain):
    return pl.pallas_call(
        finish_kernel,
        grid=(TOK // SPAN,),
        in_specs=[
            pl.BlockSpec(memory_space=pltpu.SMEM),
            pl.BlockSpec((SPAN, CHAN), lambda s: (s, 0)),
            pl.BlockSpec((SPAN, STATE), lambda s: (s, 1)),
            pl.BlockSpec((HEADS, SPAN), lambda s: (0, s)),
            pl.BlockSpec((CHAN // 2, STATE), lambda s: (0, 0)),
            pl.BlockSpec((CHAN // 2, STATE), lambda s: (0, 0)),
            pl.BlockSpec((SPAN, CHAN), lambda s: (s, 0)),
            pl.BlockSpec((1, CHAN), lambda s: (0, 0)),
            pl.BlockSpec((2 * HEADS, CHAN), lambda s: (0, 0)),
        ],
        out_specs=pl.BlockSpec((SPAN, CHAN), lambda s: (s, 0)),
        out_shape=jax.ShapeDtypeStruct((TOK, CHAN), BF),
        compiler_params=pltpu.CompilerParams(vmem_limit_bytes=VMEM_LIMIT),
        cost_estimate=pl.CostEstimate(flops=2 << 30, bytes_accessed=10 << 20, transcendentals=1 << 20),
    )(core, y, pair, logs, entering, other, gate, gain, jnp.asarray(spread_rows(), BF))


QHEADS = 4
SUB = 256


def attend_kernel(flag_ref, q_ref, near_ref, pair_ref, *refs, first, last):
    if first:
        carry_ref = None
        out_ref, kv, sums, top, qq, sa, sb, ma, mb, sems = refs
    else:
        carry_ref, out_ref, kv, sums, top, qq, sa, sb, ma, mb, sems = refs
    count = flag_ref[0]
    core = flag_ref[1]

    def copies():
        found = []
        for side, piece in enumerate((near_ref, pair_ref)):
            for slot in range(NZ):
                found.append(
                    pltpu.make_async_copy(
                        piece.at[slot], kv.at[slot, pl.ds(side * TOK, TOK)], sems.at[side * NZ + slot]
                    )
                )
        return found

    def score(head, at, s_ref, m_ref, masked=False):
        keys = kv[at, :, :HD]
        twice = jnp.concatenate([keys, keys], axis=1)
        for r in range(TOK // SUB):
            rows = slice(r * SUB, (r + 1) * SUB)
            s = lax.dot_general(
                qq[head, rows, :], twice, (((1,), (1,)), ((), ())), preferred_element_type=F32
            )
            if masked:
                row = lax.broadcasted_iota(jnp.int32, s.shape, 0) + r * SUB
                key = lax.broadcasted_iota(jnp.int32, s.shape, 1)
                limit = jnp.where(core == 1, 2 * TOK, TOK)
                seen = ((key < TOK) & (key <= row)) | ((key >= TOK) & (key < limit))
                s = jnp.where(seen, s, -1e30)
            s_ref[rows, :] = s
            m_ref[rows, :] = jnp.broadcast_to(jnp.max(s, axis=1, keepdims=True), (SUB, HD))

    def gather(head, at, s_ref, m_ref):
        values = jnp.concatenate([kv[at, :, HD:], jnp.ones((CHUNK, HD), BF)], axis=1)
        for r in range(TOK // SUB):
            rows = slice(r * SUB, (r + 1) * SUB)
            old = top[head, rows, :]
            new = jnp.maximum(old, m_ref[rows, :])
            weights = jnp.exp2(s_ref[rows, :] - new[:, :1]).astype(BF)
            factor = jnp.exp2(old - new)
            part = jnp.dot(weights, values, preferred_element_type=F32)
            sums[head, rows, :] = (
                sums[head, rows, :] * jnp.concatenate([factor, factor], axis=1) + part
            )
            top[head, rows, :] = new

    @pl.when(count > 0)
    def _():
        for copy in copies():
            copy.start()
        for head in range(QHEADS):
            scaled = q_ref[:, head * HD : (head + 1) * HD].astype(F32) * (HD**-0.5 * math.log2(math.e))
            high = scaled.astype(BF)
            low = (scaled - high.astype(F32)).astype(BF)
            qq[head] = jnp.concatenate([high, low], axis=1)
            if first:
                sums[head] = jnp.zeros((TOK, 2 * HD), F32)
                top[head] = jnp.full((TOK, HD), -1e30, F32)
            else:
                block = carry_ref[:, 2 * head * HD : 2 * (head + 1) * HD]
                sums[head] = jnp.concatenate(
                    [block[:, :HD], jnp.broadcast_to(block[:, HD : HD + 1], (TOK, HD))], axis=1
                )
                top[head] = jnp.broadcast_to(block[:, 2 * HD - 1 :], (TOK, HD))
        for copy in copies():
            copy.wait()

        if first:
            def chunk(i):
                return flag_ref[2 + jnp.minimum(i, count - 1)]

            def one_head(head, _):
                score(head, 0, sa, ma, masked=True)

                def body(j, _):
                    i = 2 * j
                    score(head, chunk(i + 1), sb, mb)
                    gather(head, chunk(i), sa, ma)
                    score(head, chunk(i + 2), sa, ma)
                    gather(head, chunk(i + 1), sb, mb)
                    return 0

                lax.fori_loop(0, count // 2, body, 0)

                @pl.when(count % 2 == 1)
                def _():
                    gather(head, chunk(count - 1), sa, ma)

                return 0

            lax.fori_loop(0, QHEADS, one_head, 0)
        else:
            score(0, 0, sa, ma)

            def one_head(head, _):
                score(head, 1, sb, mb)
                gather(head, 0, sa, ma)
                score(head, 2, sa, ma)
                gather(head, 1, sb, mb)
                score(head, 3, sb, mb)
                gather(head, 2, sa, ma)
                score(jnp.minimum(head + 1, QHEADS - 1), 0, sa, ma)
                gather(head, 3, sb, mb)
                return 0

            lax.fori_loop(0, QHEADS, one_head, 0)

        lane = lax.broadcasted_iota(jnp.int32, (TOK, HD), 1)
        for head in range(QHEADS):
            if last:
                out_ref[:, head * HD : (head + 1) * HD] = (
                    sums[head, :, :HD] / sums[head, :, HD:]
                ).astype(BF)
            else:
                out_ref[:, 2 * head * HD : (2 * head + 1) * HD] = sums[head, :, :HD]
                out_ref[:, (2 * head + 1) * HD : 2 * (head + 1) * HD] = jnp.where(
                    lane < HD // 2, sums[head, :, HD:], top[head]
                )

    if not first:

        @pl.when(count == 0)
        def _():
            if last:
                for head in range(QHEADS):
                    block = carry_ref[:, 2 * head * HD : 2 * (head + 1) * HD]
                    out_ref[:, head * HD : (head + 1) * HD] = (
                        block[:, :HD] / block[:, HD : HD + 1]
                    ).astype(BF)
            else:
                out_ref[...] = carry_ref[...]


def attend(flags, query, near, pair, carry=None, last=False):
    first = carry is None
    vmem = pl.BlockSpec(memory_space=pltpu.VMEM)
    hbm = pl.BlockSpec(memory_space=pl.ANY)
    out = (
        jax.ShapeDtypeStruct((TOK, QHEADS * HD), BF)
        if last
        else jax.ShapeDtypeStruct((TOK, 2 * QHEADS * HD), F32)
    )
    return pl.pallas_call(
        functools.partial(attend_kernel, first=first, last=last),
        in_specs=[pl.BlockSpec(memory_space=pltpu.SMEM), vmem, hbm, hbm] + ([] if first else [vmem]),
        out_specs=vmem,
        out_shape=out,
        scratch_shapes=[
            pltpu.VMEM((NZ, CHUNK, 2 * HD), BF),
            pltpu.VMEM((QHEADS, TOK, 2 * HD), F32),
            pltpu.VMEM((QHEADS, TOK, HD), F32),
            pltpu.VMEM((QHEADS, TOK, 2 * HD), BF),
            pltpu.VMEM((TOK, CHUNK), F32),
            pltpu.VMEM((TOK, CHUNK), F32),
            pltpu.VMEM((TOK, HD), F32),
            pltpu.VMEM((TOK, HD), F32),
            pltpu.SemaphoreType.DMA((2 * NZ,)),
        ],
        compiler_params=pltpu.CompilerParams(vmem_limit_bytes=40 << 20),
        cost_estimate=pl.CostEstimate(flops=14 << 30, bytes_accessed=8 << 20, transcendentals=8 << 20),
    )(flags, query, near, pair, *([] if first else [carry]))


def gathered_keys(key_heads, value_heads):
    own = jnp.concatenate([key_heads, value_heads], axis=1)
    up = along_z(own, 1)
    down = along_z(own, -1)
    two = along_z(up, 1)
    plane = jnp.stack([own, up, down, two])
    left = along_x(plane, 1, wrap=True)
    right = along_x(plane, -1, wrap=True)
    far = jnp.concatenate(
        [along_x(left[:2], 1, wrap=True), along_x(right[2:], -1, wrap=True)], axis=0
    )
    return [(part, swap_core(part)) for part in (plane, left, right, far)]


def plane_list(c, z):
    third = jnp.where(z == 3, 2, 3)
    return jnp.stack([z + 1, c, 0 * z, 0 * z + 1, third, 0 * z + 3]).astype(jnp.int32)


def local(
    hidden,
    dt_weight,
    dt_bias,
    decay_rate,
    skip_gain,
    ssm_in,
    bc_in,
    conv_x,
    conv_bc,
    gate_in,
    norm_gain,
    query_heads,
    key_heads,
    value_heads,
):
    mine = lax.axis_index("ctx")
    x, z, c = mine // (NZ * NC), (mine // NC) % NZ, mine % NC
    core = c.astype(jnp.int32)[None]
    bc = bc_in.reshape(TOK, 2 * STATE)
    ends = jnp.concatenate([ssm_in[TOK - 16 :], bc[TOK - 16 :]], axis=1)
    tail = lax.ppermute(ends, "ctx", [(i, i + 1) for i in range(31)])
    partial = lax.dot_general(
        dt_weight, hidden, (((0,), (1,)), ((), ())), preferred_element_type=F32
    )
    parts = lax.all_to_all(partial.reshape(8, HEADS, TOK), "head", 0, 0, tiled=True)
    steps = jax.nn.softplus(jnp.sum(parts, axis=0) + dt_bias[:, None])
    drop = -steps * decay_rate[:, None]
    total = jnp.sum(drop, axis=1)
    partner, chip_decay = decay_logs(total, mine)
    xin, pair, cum, logs, starts, keep, give = own_states(
        core, ssm_in, tail, bc, steps, drop, conv_x, conv_bc.reshape(4, 2 * STATE)
    )
    planes = gathered_keys(key_heads, value_heads)
    flags = [plane_list(c, z)] + [
        jnp.stack([4 * seen.astype(jnp.int32), c.astype(jnp.int32)])
        for seen in (x >= 1, x == 3, x >= 2)
    ]

    other = swap_core(give)
    by_half = lambda value: lax.dynamic_index_in_dim(value.reshape(2, 16), c, 0, False)
    shape = (16, PSIZE, STATE)
    log_first = by_half(jnp.where(c == 0, total, partner))
    log_second = by_half(jnp.where(c == 0, partner, total))
    early = jnp.where(c == 0, keep, other).reshape(shape).astype(F32)
    late = jnp.where(c == 0, other, keep).reshape(shape).astype(F32)
    both = (late + jnp.exp(log_second)[:, None, None] * early).astype(BF)
    collected = exchanged(both)
    both, xin, query = lax.optimization_barrier((both, xin, query_heads))
    y = inside_blocks(xin, pair, cum, steps, starts, jnp.repeat(skip_gain, PSIZE)[None])
    seen = attend(flags[0], query, *planes[0])
    collected, y, seen = lax.optimization_barrier((collected, y, seen))
    carried = chain(chip_decay, collected)
    chip_in = exchanged(carried)
    carried, seen = lax.optimization_barrier((carried, seen))
    seen = attend(flags[1], query, *planes[1], carry=seen)
    seen = attend(flags[2], query, *planes[2], carry=seen)
    chip_in, seen = lax.optimization_barrier((chip_in, seen))
    after = (early + jnp.exp(log_first)[:, None, None] * chip_in.astype(F32)).astype(BF)
    entering = jnp.where(c == 0, chip_in, after).reshape(CHAN // 2, STATE)
    sent = jnp.where(c == 0, after, chip_in).reshape(CHAN // 2, STATE)
    received = swap_core(sent)
    sent, seen = lax.optimization_barrier((sent, seen))
    attn_out = attend(flags[3], query, *planes[3], carry=seen, last=True)
    received, attn_out = lax.optimization_barrier((received, attn_out))
    mamba_out = finish(core, y, pair, logs, entering, received, gate_in, norm_gain[None])
    return (mamba_out, attn_out)


def solution(mesh):
    in_specs = (
        P("ctx", "head"),
        P("head", None),
        P("head"),
        P("head"),
        P("head"),
        P("ctx", "head"),
        P("ctx", "head", None),
        P(None, "head"),
        P(None, "head", None),
        P("ctx", "head"),
        P("head"),
        P("ctx", "head"),
        P("ctx", "head"),
        P("ctx", "head"),
    )
    out_specs = (P("ctx", "head"), P("ctx", "head"))
    return jax.shard_map(local, mesh=mesh, in_specs=in_specs, out_specs=out_specs, check_vma=False)
```

time: 248 us -> 182 us (0.73)
  the two profiles are of different devices: /device:TPU:199 before, /device:TPU:23 now
where the time goes in v2:
time: 182 us; the launch traced here: 181 us
  Pallas kernels  77.8 us (43%)
  starting transfers between devices  59.3 us (33%)
  waiting for transfers between devices  16.5 us (9%)
  local copies, waits for them, and re-layouts  15.1 us (8%)
  other arithmetic  8.76 us (5%)
  matrix products  2.32 us (1%)
    pallas_call x4, Pallas kernels, attend(): pl.pallas_call(functools.partial(attend_kernel, first=first, last=last),...  48.2 us
    all_to_all x2, starting transfers between devices, exchanged(): lax.all_to_all(value, 'ctx', 0, 0, tiled=True, axis_index_groups=SAME_CORE)  22 us
    ppermute x13, starting transfers between devices, send(): return lax.ppermute(value, 'ctx', pairs_of(move))  19.6 us
    ppermute x13, waiting for transfers between devices, send(): return lax.ppermute(value, 'ctx', pairs_of(move))  15.7 us
    pallas_call x1, Pallas kernels, own_states(): pl.pallas_call(states_kernel, grid=(TOK // SPAN, blocks), in_specs=[pl.Bl...  11.3 us
    unnamed x31, local copies, waits for them, and re-layouts  10.1 us
    pallas_call x1, Pallas kernels, inside_blocks(): pl.pallas_call(inside_kernel, grid=(TOK // SPAN, blocks), in_specs=[pl.Bl...  8.84 us
    all_to_all x1, starting transfers between devices, decay_logs(): got = lax.all_to_all(rows, 'ctx', 0, 0, tiled=True)  8.47 us
  transfers between devices with their start and end apart: 18, of which 5 were waited for; matrix products, arithmetic and copies ran while one was open for 9% of the time, Pallas kernels for 39%

profile of v2, /device:TPU:23, one launch (start us, length us, event | category | flops | bytes accessed | tf_op | source)
XLA Modules:
  0.0 180.7 jit_solution(17377751963961687766)
XLA Ops:
  0.7 1.0 constant_dynamic-update-slice_fusion.1
  1.7 0.9 constant_dynamic-update-slice_fusion
  2.6 3.1 %collective-permute-start.2 = (bf16[512,256]{1,0:T(8,128)(2,1)S(1)}, bf16[512,256]{1,0:T(8,128)(2,1)S(1)}, u32[]{:S(2)}, u32[]{:S(2)}) collective-permute-start(bf16[512,256]{1,0:T(8,128)(2,1)S(1)} %constant_dynamic-update-slice_fusion), channel_id=1, source_target_pairs={{0,16},{8,24},{16,32},{24,40},{32,48},{40,56},{48,0},{56,8},{64,80... | collective-permute-start | bytes 786440 | tf_op jit(solution)/shard_map/ppermute | solution.py:39
  5.7 3.1 %collective-permute-start.3 = (bf16[512,256]{1,0:T(8,128)(2,1)S(1)}, bf16[512,256]{1,0:T(8,128)(2,1)S(1)}, u32[]{:S(2)}, u32[]{:S(2)}) collective-permute-start(bf16[512,256]{1,0:T(8,128)(2,1)S(1)} %constant_dynamic-update-slice_fusion), channel_id=1, source_target_pairs={{0,48},{8,56},{16,0},{24,8},{32,16},{40,24},{48,32},{56,40},{64,11... | collective-permute-start | bytes 786440 | tf_op jit(solution)/shard_map/ppermute | solution.py:39
  8.8 2.3 %fusion.11 = f32[256,512]{1,0:T(8,128)} fusion(bf16[1024,256]{1,0:T(8,128)(2,1)} %param.20, bf16[512,1024]{1,0:T(8,128)(2,1)S(1)} %copy-done), kind=kOutput, calls=%fused_computation.36 | convolution fusion | flops 268435456 | bytes 2097152 | tf_op jit(solution)/shard_map/dot_general | solution.py:638
  11.2 4.8 %all-to-all-start = ((f32[8,32,512]{2,1,0:T(8,128)}), f32[8,32,512]{2,1,0:T(8,128)}, u32[]{:S(2)}, u32[]{:S(2)}) async-start(f32[8,32,512]{2,1,0:T(8,128)} %bitcast.3), calls=%async_computation | async-start | bytes 1048576 | tf_op jit(solution)/shard_map/all_to_all | solution.py:641
  16.0 0.7 slice_bitcast_fusion
  16.7 0.6 pad_maximum_fusion.1
  17.3 4.4 %collective-permute-start = (bf16[16,2560]{1,0:T(8,128)(2,1)}, bf16[16,2560]{1,0:T(8,128)(2,1)}, u32[]{:S(2)}, u32[]{:S(2)}) collective-permute-start(bf16[16,2560]{1,0:T(8,128)(2,1)} %pad_maximum_fusion.1), channel_id=1, source_target_pairs={{0,8},{8,16},{16,24},{24,32},{32,40},{40,48},{48,56},{56,64},{64,7... | collective-permute-start | bytes 245768 | tf_op jit(solution)/shard_map/ppermute | solution.py:637
  21.8 3.9 %collective-permute-start.4 = (bf16[512,256]{1,0:T(8,128)(2,1)S(1)}, bf16[512,256]{1,0:T(8,128)(2,1)S(1)}, u32[]{:S(2)}, u32[]{:S(2)}) collective-permute-start(bf16[512,256]{1,0:T(8,128)(2,1)S(1)} %collective-permute-done.2), channel_id=1, source_target_pairs={{0,16},{8,24},{16,32},{24,40},{32,48},{40,56},{48,0},{56,8},{64,80... | collective-permute-start | bytes 786440 | tf_op jit(solution)/shard_map/ppermute | solution.py:39
  25.7 0.1 pad_add_fusion.flag_ref
  25.8 0.6 copy.27
  26.5 0.7 broadcast_in_dim_reshape.3.skip_ref
  27.1 0.1 pad.12.clone
  27.2 0.1 stack.48.flag_ref
  27.4 0.1 pad_add_fusion.2.flag_ref
  27.5 12.6 %collective-permute-done.4 = bf16[512,256]{1,0:T(8,128)(2,1)S(1)} collective-permute-done((bf16[512,256]{1,0:T(8,128)(2,1)S(1)}, bf16[512,256]{1,0:T(8,128)(2,1)S(1)}, u32[]{:S(2)}, u32[]{:S(2)}) %collective-permute-start.4) | collective-permute-done | bytes 262176 | tf_op jit(solution)/shard_map/ppermute | solution.py:39
  40.1 0.1 pad_maximum_fusion.near_ref
  40.2 0.6 collective-permute-start.5
  40.8 0.8 collective-permute-start.6
  41.6 1.9 %collective-permute-start.8 = (bf16[4,512,256]{2,1,0:T(8,128)(2,1)S(1)}, bf16[4,512,256]{2,1,0:T(8,128)(2,1)}, u32[]{:S(2)}, u32[]{:S(2)}) collective-permute-start(bf16[4,512,256]{2,1,0:T(8,128)(2,1)S(1)} %pad_maximum_fusion.near_ref), channel_id=1, source_target_pairs={{0,64},{8,72},{16,80},{24,88},{32,96},{40,104},{48,112},{56,120},{... | collective-permute-start | bytes 3145736 | tf_op jit(solution)/shard_map/ppermute | solution.py:39
  43.5 1.1 reduce_sum.27
  44.6 0.9 fusion.10
  45.5 0.1 reshape.60
  45.6 0.1 copy.23
  45.8 0.6 maximum_maximum_fusion
  46.4 8.5 %all-to-all-start.1 = ((f32[32,1,128]{2,1,0:T(1,128)}), f32[32,1,128]{2,1,0:T(1,128)S(1)}, u32[]{:S(2)}, u32[]{:S(2)}) async-start(f32[32,1,128]{2,1,0:T(1,128)} %bitcast.6), calls=%async_computation.1 | async-start | bytes 32768 | tf_op jit(solution)/shard_map/all_to_all | solution.py:373
  54.9 11.3 %shard_map.194 = (bf16[512,2048]{1,0:T(8,128)(2,1)}, bf16[512,512]{1,0:T(8,128)(2,1)}, f32[32,512]{1,0:T(8,128)}, f32[32,512]{1,0:T(8,128)}, bf16[8192,256]{1,0:...) custom-call(s32[1]{0:T(128)} %bitcast.core_ref, bf16[512,2048]{1,0:T(8,128)(2,1)} %before_ref.1, ...), custom_call_target="tpu_custom_call" | custom-call | flops 4294967296 | bytes 12582912 | tf_op jit(solution)/shard_map/pallas_call | solution.py:183
  66.1 0.4 collective-permute-start.1
  66.6 0.7 all-to-all-done.1
  67.3 0.1 slice_reduce_fusion.1
  67.4 0.1 slice.28
  67.5 0.1 slice_reduce_fusion
  67.6 0.1 reshape_squeeze.3
  67.7 0.1 reduce_sum.29
  67.8 0.5 exp.30.decay_ref
  68.4 0.1 collective-permute-done.1
  68.5 1.3 broadcast_select_fusion.1
  69.8 0.8 copy-done.8
  70.5 1.0 fusion.1
  71.6 9.0 %all-to-all-start.2 = ((bf16[16,64,256]{2,1,0:T(8,128)(2,1)}), bf16[16,64,256]{2,1,0:T(8,128)(2,1)}, u32[]{:S(2)}, u32[]{:S(2)}) async-start(bf16[16,64,256]{2,1,0:T(8,128)(2,1)} %fusion.1), calls=%async_computation.2 | async-start | bytes 1048576 | tf_op jit(solution)/shard_map/all_to_all | solution.py:365
  80.6 8.8 %shard_map.195.y_ref = f32[512,2048]{1,0:T(8,128)} custom-call(bf16[512,2048]{1,0:T(8,128)(2,1)} %get-tuple-element.23.xin_ref, bf16[512,512]{1,0:T(8,128)(2,1)} %get-tuple-element.24.pair_ref.c_ref, f32[32,512]{1,0:T(8,128)} %get-tuple-element.25.cum_ref, f32[32,512]{1,0:T(8,128)} %get-tuple-element.40.steps_ref, ...), custom_call_target="tpu_custom_call" | custom-call | flops 8589934592 | bytes 12582912 | tf_op jit(solution)/shard_map/pallas_call | solution.py:314
  89.4 1.1 slice.33
  90.6 0.2 collective-permute-start.11
  90.9 1.6 collective-permute-start.12
  92.4 1.5 collective-permute-start.7
  93.9 6.5 %shard_map.196.refs_0_ = f32[512,1024]{1,0:T(8,128)S(1)} custom-call(s32[6]{0:T(128)S(1)} %stack.48.flag_ref, bf16[512,512]{1,0:T(8,128)(2,1)S(1)} %copy-done.1, bf16[4,512,256]{2,1,0:T(8,128)(2,1)S(1)} %pad_maximum_fusion.near_ref, bf16[4,512,256]{2,1,0:T(8,128)(2,1)} %collective-permute-done.5.pair_ref), custom_call_target="tpu_custom_call" | custom-call | flops 15032385536 | bytes 8388608 | tf_op jit(solution)/shard_map/pallas_call | solution.py:576
  100.5 1.3 copy-done.4
  101.8 2.4 %collective-permute-done.11 = bf16[2,512,256]{2,1,0:T(8,128)(2,1)S(1)} collective-permute-done((bf16[2,512,256]{2,1,0:T(8,128)(2,1)S(1)}, bf16[2,512,256]{2,1,0:T(8,128)(2,1)S(1)}, u32[]{:S(2)}, u32[]{:S(2)}) %collective-permute-start.11) | collective-permute-done | bytes 524320 | tf_op jit(solution)/shard_map/ppermute | solution.py:39
  104.3 0.6 collective-permute-done.12
  104.9 1.9 %collective-permute-start.13 = (bf16[4,512,256]{2,1,0:T(8,128)(2,1)S(1)}, bf16[4,512,256]{2,1,0:T(8,128)(2,1)}, u32[]{:S(2)}, u32[]{:S(2)}) collective-permute-start(bf16[4,512,256]{2,1,0:T(8,128)(2,1)S(1)} %constant_dynamic-update-slice_fusion.2.near_ref), channel_id=1, source_target_pairs={{0,8},{8,0},{16,24},{24,16},{32,40},{40,32},{48,56},{56,48},{64,72... | collective-permute-start | bytes 3145736 | tf_op jit(solution)/shard_map/ppermute | solution.py:39
  106.8 2.0 %shard_map.197 = bf16[16,64,256]{2,1,0:T(8,128)(2,1)} custom-call(f32[16]{0:T(128)} %exp.30.decay_ref, bf16[16,64,256]{2,1,0:T(8,128)(2,1)} %all-to-all-done.2.from_ref), custom_call_target="tpu_custom_call" | custom-call | flops 1048576 | bytes 1048576 | tf_op jit(solution)/shard_map/pallas_call | solution.py:352
  108.8 13.0 %all-to-all-start.3 = ((bf16[16,64,256]{2,1,0:T(8,128)(2,1)}), bf16[16,64,256]{2,1,0:T(8,128)(2,1)}, u32[]{:S(2)}, u32[]{:S(2)}) async-start(bf16[16,64,256]{2,1,0:T(8,128)(2,1)} %shard_map.197), calls=%async_computation.3 | async-start | bytes 1048576 | tf_op jit(solution)/shard_map/all_to_all | solution.py:365
  121.8 1.0 copy-done.2
  122.8 1.6 copy-done.5
  124.4 13.8 %shard_map.198.refs_0_ = f32[512,1024]{1,0:T(8,128)S(1)} custom-call(s32[2]{0:T(128)S(1)} %pad_add_fusion.1.flag_ref, bf16[512,512]{1,0:T(8,128)(2,1)S(1)} %copy-done.2, bf16[4,512,256]{2,1,0:T(8,128)(2,1)} %collective-permute-done.8.near_ref, bf16[4,512,256]{2,1,0:T(8,128)(2,1)} %collective-permute-done.9.pair_ref, f32[512,1024]{1,0:T(8,128)S(1)} %copy-done.5), custom_call_target="tpu_custom_call" | custom-call | flops 15032385536 | bytes 8388608 | tf_op jit(solution)/shard_map/pallas_call | solution.py:576
  138.2 13.8 %shard_map.199.refs_0_ = f32[512,1024]{1,0:T(8,128)S(1)} custom-call(s32[2]{0:T(128)S(1)} %pad_add_fusion.flag_ref, bf16[512,512]{1,0:T(8,128)(2,1)S(1)} %copy-done.2, bf16[4,512,256]{2,1,0:T(8,128)(2,1)S(1)} %collective-permute-done.6.near_ref, bf16[4,512,256]{2,1,0:T(8,128)(2,1)} %collective-permute-done.7.pair_ref, f32[512,1024]{1,0:T(8,128)S(1)} %shard_map.198.refs_0_), custom_call_target="tpu_custom_call" | custom-call | flops 15032385536 | bytes 8388608 | tf_op jit(solution)/shard_map/pallas_call | solution.py:576
  151.9 1.3 copy-done.6
  153.3 2.8 %fusion.3 = (bf16[16,64,256]{2,1,0:T(8,128)(2,1)S(1)}, bf16[16,64,256]{2,1,0:T(8,128)(2,1)}) fusion(bf16[16,64,256]{2,1,0:T(8,128)(2,1)} %all-to-all-done.3, bf16[16,64,256]{2,1,0:T(8,128)(2,1)} %bitcast.36, f32[16]{0:T(128)S(1)} %fusion.9, pred[]{:T(512)S(6)} %eq.18), kind=kLoop, calls=%fused_computation.6 | loop fusion | flops 1835008 | bytes 2097217 | tf_op jit(solution)/shard_map/jit(_where)/select_n | solution.py:676
  156.0 0.6 collective-permute-start.10
  156.6 1.6 copy-done.7
  158.2 14.2 %shard_map.200 = bf16[512,512]{1,0:T(8,128)(2,1)} custom-call(s32[2]{0:T(128)S(1)} %pad_add_fusion.2.flag_ref, bf16[512,512]{1,0:T(8,128)(2,1)S(1)} %copy-done.3, bf16[4,512,256]{2,1,0:T(8,128)(2,1)S(1)} %constant_dynamic-update-slice_fusion.2.near_ref, bf16[4,512,256]{2,1,0:T(8,128)(2,1)} %collective-permute-done.13.pair_ref, f32[512,1024]{1,0:T(8,128)S(1)} %copy-done.7), custom_call_target="tpu_custom_call" | custom-call | flops 15032385536 | bytes 8388608 | tf_op jit(solution)/shard_map/pallas_call | solution.py:576
  172.4 0.8 copy-done.9
  173.2 7.5 %shard_map.201 = bf16[512,2048]{1,0:T(8,128)(2,1)} custom-call(s32[1]{0:T(128)} %bitcast.core_ref, f32[512,2048]{1,0:T(8,128)} %shard_map.195.y_ref, bf16[512,512]{1,0:T(8,128)(2,1)} %get-tuple-element.24.pair_ref.c_ref, f32[32,512]{1,0:T(8,128)} %get-tuple-element.29.log_ref, bf16[1024,256]{1,0:T(8,128)(2,1)} %bitcast.38, bf16[1024,256]{1,0:T(8,128)(2,1)} %copy-done.9, ...), custom_call_target="tpu_custom_call" | custom-call | flops 2147483648 | bytes 10485760 | tf_op jit(solution)/shard_map/pallas_call | solution.py:404
  (49 shorter events, 0.5 us)
Async XLA Ops:
  0.6 8.2 %copy-start = (bf16[512,1024]{1,0:T(8,128)(2,1)S(1)}, bf16[512,1024]{1,0:T(8,128)(2,1)}, u32[]{:S(2)}) copy-start(bf16[512,1024]{1,0:T(8,128)(2,1)} %param.19) | copy-start | bytes 3145732
  0.6 16.1 %slice-start = ((bf16[512,2048]{1,0:T(8,128)(2,1)}), bf16[16,2048]{1,0:T(8,128)(2,1)S(1)}, s32[]{:S(2)}) async-start(bf16[512,2048]{1,0:T(8,128)(2,1)} %before_ref.1), calls=%async_computation.4 | async-start | bytes 131072 | tf_op jit(solution)/shard_map/slice | solution.py:636
  0.7 25.1 %copy-start.10 = (f32[4,1,512]{2,1,0:T(1,128)S(1)}, f32[4,1,512]{2,1,0:T(1,128)}, u32[]{:S(2)}) copy-start(f32[4,1,512]{2,1,0:T(1,128)} %param.27) | copy-start | bytes 24580
  0.7 25.7 %copy-start.13 = (f32[32]{0:T(128)S(1)}, f32[32]{0:T(128)}, u32[]{:S(2)}) copy-start(f32[32]{0:T(128)} %param.23) | copy-start | bytes 388
  2.6 19.1 %collective-permute-start.2 = (bf16[512,256]{1,0:T(8,128)(2,1)S(1)}, bf16[512,256]{1,0:T(8,128)(2,1)S(1)}, u32[]{:S(2)}, u32[]{:S(2)}) collective-permute-start(bf16[512,256]{1,0:T(8,128)(2,1)S(1)} %constant_dynamic-update-slice_fusion), channel_id=1, source_target_pairs={{0,16},{8,24},{16,32},{24,40},{32,48},{40,56},{48,0},{56,8},{64,80... | collective-permute-start | bytes 786440 | tf_op jit(solution)/shard_map/ppermute | solution.py:39
  5.7 21.7 %collective-permute-start.3 = (bf16[512,256]{1,0:T(8,128)(2,1)S(1)}, bf16[512,256]{1,0:T(8,128)(2,1)S(1)}, u32[]{:S(2)}, u32[]{:S(2)}) collective-permute-start(bf16[512,256]{1,0:T(8,128)(2,1)S(1)} %constant_dynamic-update-slice_fusion), channel_id=1, source_target_pairs={{0,48},{8,56},{16,0},{24,8},{32,16},{40,24},{48,32},{56,40},{64,11... | collective-permute-start | bytes 786440 | tf_op jit(solution)/shard_map/ppermute | solution.py:39
  11.1 33.4 %copy-start.11 = (f32[32]{0:T(128)S(1)}, f32[32]{0:T(128)}, u32[]{:S(2)}) copy-start(f32[32]{0:T(128)} %param.22) | copy-start | bytes 388
  11.1 33.4 %copy-start.12 = (f32[32]{0:T(128)S(1)}, f32[32]{0:T(128)}, u32[]{:S(2)}) copy-start(f32[32]{0:T(128)} %param.21) | copy-start | bytes 388
  11.2 32.3 %all-to-all-start = ((f32[8,32,512]{2,1,0:T(8,128)}), f32[8,32,512]{2,1,0:T(8,128)}, u32[]{:S(2)}, u32[]{:S(2)}) async-start(f32[8,32,512]{2,1,0:T(8,128)} %bitcast.3), calls=%async_computation | async-start | bytes 1048576 | tf_op jit(solution)/shard_map/all_to_all | solution.py:641
  17.3 37.5 %collective-permute-start = (bf16[16,2560]{1,0:T(8,128)(2,1)}, bf16[16,2560]{1,0:T(8,128)(2,1)}, u32[]{:S(2)}, u32[]{:S(2)}) collective-permute-start(bf16[16,2560]{1,0:T(8,128)(2,1)} %pad_maximum_fusion.1), channel_id=1, source_target_pairs={{0,8},{8,16},{16,24},{24,32},{32,40},{40,48},{48,56},{56,64},{64,7... | collective-permute-start | bytes 245768 | tf_op jit(solution)/shard_map/ppermute | solution.py:637
  21.8 18.3 %collective-permute-start.4 = (bf16[512,256]{1,0:T(8,128)(2,1)S(1)}, bf16[512,256]{1,0:T(8,128)(2,1)S(1)}, u32[]{:S(2)}, u32[]{:S(2)}) collective-permute-start(bf16[512,256]{1,0:T(8,128)(2,1)S(1)} %collective-permute-done.2), channel_id=1, source_target_pairs={{0,16},{8,24},{16,32},{24,40},{32,48},{40,56},{48,0},{56,8},{64,80... | collective-permute-start | bytes 786440 | tf_op jit(solution)/shard_map/ppermute | solution.py:39
  40.2 53.7 %collective-permute-start.5 = (bf16[4,512,256]{2,1,0:T(8,128)(2,1)S(1)}, bf16[4,512,256]{2,1,0:T(8,128)(2,1)}, u32[]{:S(2)}, u32[]{:S(2)}) collective-permute-start(bf16[4,512,256]{2,1,0:T(8,128)(2,1)S(1)} %pad_maximum_fusion.near_ref), channel_id=1, source_target_pairs={{0,8},{8,0},{16,24},{24,16},{32,40},{40,32},{48,56},{56,48},{64,72... | collective-permute-start | bytes 3145736 | tf_op jit(solution)/shard_map/ppermute | solution.py:39
  40.8 50.0 %collective-permute-start.6 = (bf16[4,512,256]{2,1,0:T(8,128)(2,1)S(1)}, bf16[4,512,256]{2,1,0:T(8,128)(2,1)S(1)}, u32[]{:S(2)}, u32[]{:S(2)}) collective-permute-start(bf16[4,512,256]{2,1,0:T(8,128)(2,1)S(1)} %pad_maximum_fusion.near_ref), channel_id=1, source_target_pairs={{0,192},{8,200},{16,208},{24,216},{32,224},{40,232},{48,240},{56,2... | collective-permute-start | bytes 3145736 | tf_op jit(solution)/shard_map/ppermute | solution.py:39
  41.6 47.8 %collective-permute-start.8 = (bf16[4,512,256]{2,1,0:T(8,128)(2,1)S(1)}, bf16[4,512,256]{2,1,0:T(8,128)(2,1)}, u32[]{:S(2)}, u32[]{:S(2)}) collective-permute-start(bf16[4,512,256]{2,1,0:T(8,128)(2,1)S(1)} %pad_maximum_fusion.near_ref), channel_id=1, source_target_pairs={{0,64},{8,72},{16,80},{24,88},{32,96},{40,104},{48,112},{56,120},{... | collective-permute-start | bytes 3145736 | tf_op jit(solution)/shard_map/ppermute | solution.py:39
  46.4 20.9 %all-to-all-start.1 = ((f32[32,1,128]{2,1,0:T(1,128)}), f32[32,1,128]{2,1,0:T(1,128)S(1)}, u32[]{:S(2)}, u32[]{:S(2)}) async-start(f32[32,1,128]{2,1,0:T(1,128)} %bitcast.6), calls=%async_computation.1 | async-start | bytes 32768 | tf_op jit(solution)/shard_map/all_to_all | solution.py:373
  66.1 2.3 %collective-permute-start.1 = (bf16[1024,256]{1,0:T(8,128)(2,1)}, bf16[1024,256]{1,0:T(8,128)(2,1)}, u32[]{:S(2)}, u32[]{:S(2)}) collective-permute-start(bf16[1024,256]{1,0:T(8,128)(2,1)} %get-tuple-element.20), channel_id=1, source_target_pairs={{0,8},{8,0},{16,24},{24,16},{32,40},{40,32},{48,56},{56,48},{64,72... | collective-permute-start | bytes 1572872 | tf_op jit(solution)/shard_map/ppermute | solution.py:39
  69.8 0.8 copy-start.8
  71.6 35.2 %all-to-all-start.2 = ((bf16[16,64,256]{2,1,0:T(8,128)(2,1)}), bf16[16,64,256]{2,1,0:T(8,128)(2,1)}, u32[]{:S(2)}, u32[]{:S(2)}) async-start(bf16[16,64,256]{2,1,0:T(8,128)(2,1)} %fusion.1), calls=%async_computation.2 | async-start | bytes 1048576 | tf_op jit(solution)/shard_map/all_to_all | solution.py:365
  89.4 4.5 %copy-start.1 = (bf16[512,512]{1,0:T(8,128)(2,1)S(1)}, bf16[512,512]{1,0:T(8,128)(2,1)}, u32[]{:S(2)}) copy-start(bf16[512,512]{1,0:T(8,128)(2,1)} %q_ref.3) | copy-start | bytes 1572868
  90.6 13.6 %collective-permute-start.11 = (bf16[2,512,256]{2,1,0:T(8,128)(2,1)S(1)}, bf16[2,512,256]{2,1,0:T(8,128)(2,1)S(1)}, u32[]{:S(2)}, u32[]{:S(2)}) collective-permute-start(bf16[2,512,256]{2,1,0:T(8,128)(2,1)S(1)} %slice.33), channel_id=1, source_target_pairs={{0,64},{8,72},{16,80},{24,88},{32,96},{40,104},{48,112},{56,120},{... | collective-permute-start | bytes 1572872 | tf_op jit(solution)/shard_map/ppermute | solution.py:39
  90.9 14.0 %collective-permute-start.12 = (bf16[2,512,256]{2,1,0:T(8,128)(2,1)S(1)}, bf16[2,512,256]{2,1,0:T(8,128)(2,1)S(1)}, u32[]{:S(2)}, u32[]{:S(2)}) collective-permute-start(bf16[2,512,256]{2,1,0:T(8,128)(2,1)S(1)} %slice.34), channel_id=1, source_target_pairs={{0,192},{8,200},{16,208},{24,216},{32,224},{40,232},{48,240},{56,2... | collective-permute-start | bytes 1572872 | tf_op jit(solution)/shard_map/ppermute | solution.py:39
  92.4 45.7 %collective-permute-start.7 = (bf16[4,512,256]{2,1,0:T(8,128)(2,1)S(1)}, bf16[4,512,256]{2,1,0:T(8,128)(2,1)}, u32[]{:S(2)}, u32[]{:S(2)}) collective-permute-start(bf16[4,512,256]{2,1,0:T(8,128)(2,1)S(1)} %collective-permute-done.6.near_ref), channel_id=1, source_target_pairs={{0,8},{8,0},{16,24},{24,16},{32,40},{40,32},{48,56},{56,48},{64,72... | collective-permute-start | bytes 3145736 | tf_op jit(solution)/shard_map/ppermute | solution.py:39
  93.9 27.8 %collective-permute-start.9 = (bf16[4,512,256]{2,1,0:T(8,128)(2,1)}, bf16[4,512,256]{2,1,0:T(8,128)(2,1)}, u32[]{:S(2)}, u32[]{:S(2)}) collective-permute-start(bf16[4,512,256]{2,1,0:T(8,128)(2,1)} %collective-permute-done.8.near_ref), channel_id=1, source_target_pairs={{0,8},{8,0},{16,24},{24,16},{32,40},{40,32},{48,56},{56,48},{64,72... | collective-permute-start | bytes 3145736 | tf_op jit(solution)/shard_map/ppermute | solution.py:39
  100.5 1.3 copy-start.4
  104.9 51.7 %collective-permute-start.13 = (bf16[4,512,256]{2,1,0:T(8,128)(2,1)S(1)}, bf16[4,512,256]{2,1,0:T(8,128)(2,1)}, u32[]{:S(2)}, u32[]{:S(2)}) collective-permute-start(bf16[4,512,256]{2,1,0:T(8,128)(2,1)S(1)} %constant_dynamic-update-slice_fusion.2.near_ref), channel_id=1, source_target_pairs={{0,8},{8,0},{16,24},{24,16},{32,40},{40,32},{48,56},{56,48},{64,72... | collective-permute-start | bytes 3145736 | tf_op jit(solution)/shard_map/ppermute | solution.py:39
  108.8 44.5 %all-to-all-start.3 = ((bf16[16,64,256]{2,1,0:T(8,128)(2,1)}), bf16[16,64,256]{2,1,0:T(8,128)(2,1)}, u32[]{:S(2)}, u32[]{:S(2)}) async-start(bf16[16,64,256]{2,1,0:T(8,128)(2,1)} %shard_map.197), calls=%async_computation.3 | async-start | bytes 1048576 | tf_op jit(solution)/shard_map/all_to_all | solution.py:365
  121.7 1.0 copy-start.2
  122.8 1.6 copy-start.5
  151.9 1.3 copy-start.6
  153.2 3.4 %copy-start.3 = (bf16[512,512]{1,0:T(8,128)(2,1)S(1)}, bf16[512,512]{1,0:T(8,128)(2,1)}, u32[]{:S(2)}) copy-start(bf16[512,512]{1,0:T(8,128)(2,1)} %q_ref.3) | copy-start | bytes 1572868
  156.0 16.3 %collective-permute-start.10 = (bf16[1024,256]{1,0:T(8,128)(2,1)S(1)}, bf16[1024,256]{1,0:T(8,128)(2,1)S(1)}, u32[]{:S(2)}, u32[]{:S(2)}) collective-permute-start(bf16[1024,256]{1,0:T(8,128)(2,1)S(1)} %bitcast.40), channel_id=1, source_target_pairs={{0,8},{8,0},{16,24},{24,16},{32,40},{40,32},{48,56},{56,48},{64,72... | collective-permute-start | bytes 1572872 | tf_op jit(solution)/shard_map/ppermute | solution.py:39
  156.6 1.6 copy-start.7
  172.4 0.8 copy-start.9

commit v3 on v2

v3 whole, which is shorter than its diff:
```python
import functools
import math

import jax
import jax.numpy as jnp
import numpy as np
from jax import lax
from jax.experimental import pallas as pl
from jax.experimental.pallas import tpu as pltpu
from jax.sharding import PartitionSpec as P

SPAN = 128
HD = 128
BF = jnp.bfloat16
F32 = jnp.float32
NX, NZ, NC = 4, 4, 2
HEADS, PSIZE, STATE = 32, 64, 256
CHAN = HEADS * PSIZE
TOK = 512
HB = 32
HBC = HB * PSIZE
CHUNK = 1024
VMEM_LIMIT = 58 << 20


def pairs_of(move):
    found = []
    for x in range(NX):
        for z in range(NZ):
            for c in range(NC):
                target = move(x, z, c)
                if target is not None:
                    tx, tz, tc = target
                    found.append(((x * NZ + z) * NC + c, (tx * NZ + tz) * NC + tc))
    return found


def send(value, move):
    return lax.ppermute(value, "ctx", pairs_of(move))


def swap_core(value):
    return send(value, lambda x, z, c: (x, z, 1 - c))


def along_z(value, steps):
    return send(value, lambda x, z, c: (x, (z + steps) % NZ, c))


def along_x(value, steps, wrap=False):
    def move(x, z, c):
        if wrap or 0 <= x + steps < NX:
            return ((x + steps) % NX, z, c)
        return None

    return send(value, move)


def shifted_rows(rows, tail, steps):
    if steps == 0:
        return rows
    rolled = pltpu.roll(rows, steps, 0)
    before = pltpu.roll(tail, steps, 0)
    at = lax.broadcasted_iota(jnp.int32, before.shape, 0)
    top = jnp.where(at < steps, before, rolled[:8])
    return jnp.concatenate([top, rolled[8:]], axis=0)


def conv_silu(rows, tail, taps):
    taps_count = taps.shape[0]
    total = None
    for k in range(taps_count):
        term = taps[k : k + 1] * shifted_rows(rows, tail, taps_count - 1 - k)
        total = term if total is None else total + term
    return (total * jax.nn.sigmoid(total)).astype(BF)


def two_parts(value):
    high = value.astype(BF).astype(F32)
    return [high, (value - high).astype(BF).astype(F32)]


def three_parts(value):
    high = value.astype(BF).astype(F32)
    return [high] + two_parts(value - high)


def conv_kernel(
    x_ref, before_ref, xtail_ref, pair_ref, pbefore_ref, ptail_ref, taps_ref, ptaps_ref, xin_ref, conv_ref
):
    first = pl.program_id(0) == 0
    before = jnp.where(first, ptail_ref[...], pbefore_ref[...]).astype(F32)[8:]
    conv_ref[...] = conv_silu(pair_ref[...].astype(F32), before, ptaps_ref[...])
    before = jnp.where(first, xtail_ref[...], before_ref[...]).astype(F32)[8:]
    xin_ref[...] = conv_silu(x_ref[...].astype(F32), before, taps_ref[...])


def convolved(ssm_in, tail, bc_in, conv_x, conv_bc):
    prior = lambda s: (jnp.maximum(s * (SPAN // 16) - 1, 0), 0)
    return pl.pallas_call(
        conv_kernel,
        grid=(TOK // SPAN,),
        in_specs=[
            pl.BlockSpec((SPAN, CHAN), lambda s: (s, 0)),
            pl.BlockSpec((16, CHAN), prior),
            pl.BlockSpec((16, CHAN), lambda s: (0, 0)),
            pl.BlockSpec((SPAN, 2 * STATE), lambda s: (s, 0)),
            pl.BlockSpec((16, 2 * STATE), prior),
            pl.BlockSpec((16, 2 * STATE), lambda s: (0, CHAN // (2 * STATE))),
            pl.BlockSpec((4, CHAN), lambda s: (0, 0)),
            pl.BlockSpec((4, 2 * STATE), lambda s: (0, 0)),
        ],
        out_specs=[
            pl.BlockSpec((SPAN, CHAN), lambda s: (s, 0)),
            pl.BlockSpec((SPAN, 2 * STATE), lambda s: (s, 0)),
        ],
        out_shape=[
            jax.ShapeDtypeStruct((TOK, CHAN), BF),
            jax.ShapeDtypeStruct((TOK, 2 * STATE), BF),
        ],
        compiler_params=pltpu.CompilerParams(vmem_limit_bytes=VMEM_LIMIT),
        cost_estimate=pl.CostEstimate(flops=1 << 20, bytes_accessed=1 << 16, transcendentals=0),
    )(ssm_in, ssm_in, tail, bc_in, bc_in, tail, conv_x, conv_bc)


def states_kernel(
    core_ref,
    xin_ref,
    pair_ref,
    steps_ref,
    drop_ref,
    spread_ref,
    rows_ref,
    cum_ref,
    log_ref,
    start_ref,
    mine_ref,
    give_ref,
    log_s,
    state_s,
):
    span = pl.program_id(0)

    @pl.when(span == 0)
    def _():
        log_s[...] = jnp.zeros_like(log_s)
        state_s[...] = jnp.zeros_like(state_s)

    at_i = lax.broadcasted_iota(jnp.int32, (SPAN, SPAN), 0)
    at_j = lax.broadcasted_iota(jnp.int32, (SPAN, SPAN), 1)
    upper = jnp.where(at_i <= at_j, 1.0, 0.0)
    cum = jnp.dot(
        drop_ref[...], upper, precision=lax.Precision.HIGHEST, preferred_element_type=F32
    )
    cum_ref[...] = cum
    last = cum[:, SPAN - 1 : SPAN]
    scales = jnp.concatenate(
        two_parts(jnp.exp(last - cum) * steps_ref[...]) + [jnp.zeros((2 * HEADS, SPAN), F32)], axis=0
    ).T.astype(BF)
    decays = jnp.broadcast_to(
        jnp.concatenate(two_parts(jnp.exp(last)), axis=0), (2 * HEADS, STATE)
    ).astype(BF)
    log_ref[...] = log_s[...] + cum
    log_s[...] = log_s[...] + last
    spread = spread_ref[...]
    weight = jnp.dot(
        scales, jnp.concatenate([spread, jnp.zeros_like(spread)], axis=0), preferred_element_type=F32
    )
    weighted = (xin_ref[...].astype(F32) * weight).astype(BF)
    gain = lax.dot_general(
        weighted, pair_ref[...], (((0,), (0,)), ((), ())), preferred_element_type=F32
    )
    decay = jnp.dot(rows_ref[...], decays, preferred_element_type=F32)
    state = state_s[...]
    start_ref[...] = state.astype(BF)
    state = state * decay + gain
    state_s[...] = state

    @pl.when(span == TOK // SPAN - 1)
    def _():
        low = state.astype(BF)
        first = core_ref[0] == 0
        mine_ref[...] = jnp.where(first, low[: CHAN // 2], low[CHAN // 2 :])
        give_ref[: CHAN // 2, :] = jnp.where(first, low[CHAN // 2 :], low[: CHAN // 2])
        parts = three_parts(log_s[...]) + [jnp.zeros((HEADS, SPAN), F32)]
        rows = jnp.concatenate(parts, axis=0).T[:16].astype(BF)
        give_ref[CHAN // 2 :, :] = jnp.concatenate([rows, jnp.zeros_like(rows)], axis=1)


def spread_rows():
    spread = np.zeros((2 * HEADS, CHAN), np.float32)
    for h in range(HEADS):
        for part in range(2):
            spread[part * HEADS + h, h * PSIZE : (h + 1) * PSIZE] = 1
    return spread


def own_states(core, xin, pair, steps, drop):
    spread = spread_rows()
    return pl.pallas_call(
        states_kernel,
        grid=(TOK // SPAN,),
        in_specs=[
            pl.BlockSpec(memory_space=pltpu.SMEM),
            pl.BlockSpec((SPAN, CHAN), lambda s: (s, 0)),
            pl.BlockSpec((SPAN, STATE), lambda s: (s, 0)),
            pl.BlockSpec((HEADS, SPAN), lambda s: (0, s)),
            pl.BlockSpec((HEADS, SPAN), lambda s: (0, s)),
            pl.BlockSpec((2 * HEADS, CHAN), lambda s: (0, 0)),
            pl.BlockSpec((CHAN, 2 * HEADS), lambda s: (0, 0)),
        ],
        out_specs=[
            pl.BlockSpec((HEADS, SPAN), lambda s: (0, s)),
            pl.BlockSpec((HEADS, SPAN), lambda s: (0, s)),
            pl.BlockSpec((CHAN, STATE), lambda s: (s, 0)),
            pl.BlockSpec((CHAN // 2, STATE), lambda s: (0, 0)),
            pl.BlockSpec((CHAN // 2 + 16, STATE), lambda s: (0, 0)),
        ],
        out_shape=[
            jax.ShapeDtypeStruct((HEADS, TOK), F32),
            jax.ShapeDtypeStruct((HEADS, TOK), F32),
            jax.ShapeDtypeStruct((TOK // SPAN * CHAN, STATE), BF),
            jax.ShapeDtypeStruct((CHAN // 2, STATE), BF),
            jax.ShapeDtypeStruct((CHAN // 2 + 16, STATE), BF),
        ],
        scratch_shapes=[
            pltpu.VMEM((HEADS, SPAN), F32),
            pltpu.VMEM((CHAN, STATE), F32),
        ],
        compiler_params=pltpu.CompilerParams(vmem_limit_bytes=VMEM_LIMIT),
        cost_estimate=pl.CostEstimate(flops=1 << 20, bytes_accessed=1 << 16, transcendentals=0),
    )(core, xin, pair, steps, drop, jnp.asarray(spread, BF), jnp.asarray(spread.T, BF))


def inside_kernel(
    xin_ref,
    pair_ref,
    cum_ref,
    steps_ref,
    start_ref,
    skip_ref,
    spread_ref,
    column_ref,
    y_ref,
    g_s,
    ci_s,
    ex_s,
):
    block = pl.program_id(1)
    cmat = pair_ref[:, STATE:]

    @pl.when(block == 0)
    def _():
        product = lax.dot_general(
            cmat, pair_ref[:, :STATE], (((1,), (1,)), ((), ())), preferred_element_type=F32
        )
        at_i = lax.broadcasted_iota(jnp.int32, (SPAN, SPAN), 0)
        at_j = lax.broadcasted_iota(jnp.int32, (SPAN, SPAN), 1)
        g_s[...] = jnp.where(at_j <= at_i, product, 0.0)
        cum = cum_ref[...]
        ci_s[...] = jnp.concatenate(three_parts(cum) + [jnp.zeros_like(cum)], axis=0).T.astype(BF)
        ex_s[...] = jnp.concatenate(
            two_parts(jnp.exp(cum)) + [jnp.zeros((2 * HEADS, SPAN), F32)], axis=0
        ).T.astype(BF)

    xf = xin_ref[...].astype(F32)
    spread = spread_ref[...]
    grown = jnp.dot(
        ex_s[...], jnp.concatenate([spread, jnp.zeros_like(spread)], axis=0), preferred_element_type=F32
    )
    rows_i = jnp.dot(ci_s[...], column_ref[...], preferred_element_type=F32)
    read = lax.dot_general(
        cmat, start_ref[...], (((1,), (1,)), ((), ())), preferred_element_type=F32
    )
    base = read * grown + skip_ref[...] * xf
    cum_rows = cum_ref[pl.ds(pl.multiple_of(block * HB, HB), HB), :]
    step_rows = steps_ref[pl.ds(pl.multiple_of(block * HB, HB), HB), :]
    masked = g_s[...]
    lane = lax.broadcasted_iota(jnp.int32, (SPAN, 2 * PSIZE), 1)
    for pair in range(HB // 2):
        mixes = []
        for h in (2 * pair, 2 * pair + 1):
            gap = rows_i[:, h * SPAN : (h + 1) * SPAN] - cum_rows[h : h + 1]
            mixes.append(
                (masked * jnp.exp(jnp.minimum(gap, 0.0)) * step_rows[h : h + 1]).astype(BF)
            )
        two = xf[:, pair * 128 : (pair + 1) * 128]
        left = jnp.where(lane < PSIZE, two, 0.0).astype(BF)
        right = jnp.where(lane < PSIZE, 0.0, two).astype(BF)
        intra = jnp.dot(
            jnp.concatenate(mixes, axis=1),
            jnp.concatenate([left, right], axis=0),
            preferred_element_type=F32,
        )
        y_ref[:, pair * 128 : (pair + 1) * 128] = (
            base[:, pair * 128 : (pair + 1) * 128] + intra
        ).astype(BF)


def inside_blocks(xin, pair, cum, steps, starts, skip):
    column = np.zeros((4 * HEADS, HEADS * SPAN), np.float32)
    for h in range(HEADS):
        for part in range(3):
            column[part * HEADS + h, h * SPAN : (h + 1) * SPAN] = 1
    blocks = HEADS // HB
    return pl.pallas_call(
        inside_kernel,
        grid=(TOK // SPAN, blocks),
        in_specs=[
            pl.BlockSpec((SPAN, HBC), lambda s, b: (s, b)),
            pl.BlockSpec((SPAN, 2 * STATE), lambda s, b: (s, 0)),
            pl.BlockSpec((HEADS, SPAN), lambda s, b: (0, s)),
            pl.BlockSpec((HEADS, SPAN), lambda s, b: (0, s)),
            pl.BlockSpec((HBC, STATE), lambda s, b: (s * blocks + b, 0)),
            pl.BlockSpec((1, HBC), lambda s, b: (0, b)),
            pl.BlockSpec((2 * HEADS, HBC), lambda s, b: (0, b)),
            pl.BlockSpec((4 * HEADS, HB * SPAN), lambda s, b: (0, b)),
        ],
        out_specs=pl.BlockSpec((SPAN, HBC), lambda s, b: (s, b)),
        out_shape=jax.ShapeDtypeStruct((TOK, CHAN), BF),
        scratch_shapes=[
            pltpu.VMEM((SPAN, SPAN), F32),
            pltpu.VMEM((SPAN, 4 * HEADS), BF),
            pltpu.VMEM((SPAN, 4 * HEADS), BF),
        ],
        compiler_params=pltpu.CompilerParams(vmem_limit_bytes=VMEM_LIMIT),
        cost_estimate=pl.CostEstimate(flops=1 << 34, bytes_accessed=1 << 16, transcendentals=0),
    )(xin, pair, cum, steps, starts, skip, jnp.asarray(spread_rows(), BF), jnp.asarray(column, BF))


CHIPS = NX * NZ
SAME_CORE = [[2 * chip + core for chip in range(CHIPS)] for core in range(NC)]


def chain_kernel(from_ref, into_ref):
    carried = jnp.zeros((PSIZE, STATE), F32)
    for chip in range(CHIPS):
        into_ref[chip] = carried.astype(BF)
        if chip < CHIPS - 1:
            parts = from_ref[chip, PSIZE:, :].astype(F32)
            decay = jnp.exp(parts[0:1] + parts[1:2] + parts[2:3])
            carried = decay * carried + from_ref[chip, :PSIZE, :].astype(F32)


def chain(states):
    return pl.pallas_call(
        chain_kernel,
        in_specs=[pl.BlockSpec(memory_space=pltpu.VMEM)],
        out_specs=pl.BlockSpec(memory_space=pltpu.VMEM),
        out_shape=jax.ShapeDtypeStruct((CHIPS, PSIZE, STATE), BF),
        cost_estimate=pl.CostEstimate(flops=1 << 20, bytes_accessed=1 << 16, transcendentals=0),
    )(states)


def with_logs(states, logs):
    parts = [part[:, None, None] for part in three_parts(logs)]
    row = lax.broadcasted_iota(jnp.int32, (16, 16, STATE), 1)
    extra = jnp.where(
        row == 0, parts[0], jnp.where(row == 1, parts[1], jnp.where(row == 2, parts[2], 0.0))
    )
    return jnp.concatenate([states, extra], axis=1).astype(BF)


def exchanged(value):
    return lax.all_to_all(value, "ctx", 0, 0, tiled=True, axis_index_groups=SAME_CORE)


def finish_kernel(
    core_ref, y_ref, c_ref, log_ref, in_ref, other_ref, gate_ref, gain_ref, spread_ref, out_ref
):
    grown = jnp.concatenate(
        two_parts(jnp.exp(log_ref[...])) + [jnp.zeros((2 * HEADS, SPAN), F32)], axis=0
    ).T.astype(BF)
    spread = spread_ref[...]
    scale = jnp.dot(
        grown, jnp.concatenate([spread, jnp.zeros_like(spread)], axis=0), preferred_element_type=F32
    )
    contract = (((1,), (1,)), ((), ()))
    kept = lax.dot_general(c_ref[...], in_ref[...], contract, preferred_element_type=F32)
    given = lax.dot_general(c_ref[...], other_ref[...], contract, preferred_element_type=F32)
    first = core_ref[0] == 0
    read = jnp.concatenate(
        [jnp.where(first, kept, given), jnp.where(first, given, kept)], axis=1
    )
    mixed = y_ref[...].astype(F32) + read * scale
    gate = gate_ref[...].astype(F32)
    gated = mixed * (gate * jax.nn.sigmoid(gate))
    mean = jnp.mean(gated * gated, axis=1, keepdims=True)
    out_ref[...] = (gated * lax.rsqrt(mean + 1e-05) * gain_ref[...]).astype(BF)


def finish(core, y, pair, logs, entering, other, gate, gain):
    return pl.pallas_call(
        finish_kernel,
        grid=(TOK // SPAN,),
        in_specs=[
            pl.BlockSpec(memory_space=pltpu.SMEM),
            pl.BlockSpec((SPAN, CHAN), lambda s: (s, 0)),
            pl.BlockSpec((SPAN, STATE), lambda s: (s, 1)),
            pl.BlockSpec((HEADS, SPAN), lambda s: (0, s)),
            pl.BlockSpec((CHAN // 2, STATE), lambda s: (0, 0)),
            pl.BlockSpec((CHAN // 2, STATE), lambda s: (0, 0)),
            pl.BlockSpec((SPAN, CHAN), lambda s: (s, 0)),
            pl.BlockSpec((1, CHAN), lambda s: (0, 0)),
            pl.BlockSpec((2 * HEADS, CHAN), lambda s: (0, 0)),
        ],
        out_specs=pl.BlockSpec((SPAN, CHAN), lambda s: (s, 0)),
        out_shape=jax.ShapeDtypeStruct((TOK, CHAN), BF),
        compiler_params=pltpu.CompilerParams(vmem_limit_bytes=VMEM_LIMIT),
        cost_estimate=pl.CostEstimate(flops=1 << 20, bytes_accessed=1 << 16, transcendentals=0),
    )(core, y, pair, logs, entering, other, gate, gain, jnp.asarray(spread_rows(), BF))


QHEADS = 4
SUB = 256


def attend_kernel(flag_ref, q_ref, *refs, planes, own, fresh):
    pieces, refs = refs[: 2 * planes], refs[2 * planes :]
    if not fresh:
        in_sums, in_top, *refs = refs
    if own:
        out_sums, out_top, *refs = refs
    else:
        part_ref, *refs = refs
    kv, sums, top, qq, sa, sb, ma, mb, key_sem, in_sem, out_sem = refs
    count = flag_ref[0]
    third = flag_ref[1]
    core = flag_ref[2]

    def carried(head):
        return (
            pltpu.make_async_copy(in_sums.at[head], sums.at[head], in_sem.at[0, head]),
            pltpu.make_async_copy(in_top.at[head], top.at[head], in_sem.at[1, head]),
        )

    def leaving(head):
        return (
            pltpu.make_async_copy(sums.at[head], out_sums.at[head], out_sem.at[0, head]),
            pltpu.make_async_copy(top.at[head], out_top.at[head], out_sem.at[1, head]),
        )

    def keys(p):
        slots = pl.ds(p * NZ, NZ)
        return (
            pltpu.make_async_copy(pieces[2 * p], kv.at[slots, 0], key_sem.at[p, 0]),
            pltpu.make_async_copy(pieces[2 * p + 1], kv.at[slots, 1], key_sem.at[p, 1]),
        )

    def score(head, at, s_ref, m_ref, masked=False):
        rows_in = kv[at, :, :, :HD].reshape(CHUNK, HD)
        twice = jnp.concatenate([rows_in, rows_in], axis=1)
        for r in range(TOK // SUB):
            rows = slice(r * SUB, (r + 1) * SUB)
            s = lax.dot_general(
                qq[head, rows, :], twice, (((1,), (1,)), ((), ())), preferred_element_type=F32
            )
            if masked:
                row = lax.broadcasted_iota(jnp.int32, s.shape, 0) + r * SUB
                key = lax.broadcasted_iota(jnp.int32, s.shape, 1)
                limit = jnp.where(core == 1, 2 * TOK, TOK)
                seen = ((key < TOK) & (key <= row)) | ((key >= TOK) & (key < limit))
                s = jnp.where(seen, s, -1e30)
            s_ref[rows, :] = s
            m_ref[rows, :] = jnp.broadcast_to(jnp.max(s, axis=1, keepdims=True), (SUB, HD))

    def gather(head, at, s_ref, m_ref):
        values = kv[at, :, :, HD:].reshape(CHUNK, HD)
        values = jnp.concatenate([values, jnp.ones((CHUNK, HD), BF)], axis=1)
        for r in range(TOK // SUB):
            rows = slice(r * SUB, (r + 1) * SUB)
            old = top[head, rows, :]
            new = jnp.maximum(old, m_ref[rows, :])
            weights = jnp.exp2(s_ref[rows, :] - new[:, :1]).astype(BF)
            factor = jnp.exp2(old - new)
            part = jnp.dot(weights, values, preferred_element_type=F32)
            sums[head, rows, :] = (
                sums[head, rows, :] * jnp.concatenate([factor, factor], axis=1) + part
            )
            top[head, rows, :] = new

    if not fresh:
        for head in range(QHEADS):
            for copy in carried(head):
                copy.start()

    @pl.when(count > 0)
    def _():
        for p in range(planes):

            @pl.when(own | (p < count))
            def _():
                for copy in keys(p):
                    copy.start()

        for head in range(QHEADS):
            scaled = q_ref[:, head * HD : (head + 1) * HD].astype(F32) * (HD**-0.5 * math.log2(math.e))
            high = scaled.astype(BF)
            low = (scaled - high.astype(F32)).astype(BF)
            qq[head] = jnp.concatenate([high, low], axis=1)
            if fresh:
                sums[head] = jnp.zeros((TOK, 2 * HD), F32)
                top[head] = jnp.full((TOK, HD), -1e30, F32)
        for p in range(planes):

            @pl.when(own | (p < count))
            def _():
                for copy in keys(p):
                    copy.wait()

        if own:
            def chunk(i):
                return jnp.where(i == 2, third, jnp.minimum(i, NZ - 1))

            def one_head(head, _):
                score(head, 0, sa, ma, masked=True)

                def body(j, _):
                    i = 2 * j
                    score(head, chunk(i + 1), sb, mb)
                    gather(head, chunk(i), sa, ma)
                    score(head, chunk(i + 2), sa, ma)
                    gather(head, chunk(i + 1), sb, mb)
                    return 0

                lax.fori_loop(0, count // 2, body, 0)

                @pl.when(count % 2 == 1)
                def _():
                    gather(head, chunk(count - 1), sa, ma)

                for copy in leaving(head):
                    copy.start()
                return 0

            def full_head(head, _):
                score(head, 1, sb, mb)
                gather(head, 0, sa, ma)
                score(head, 2, sa, ma)
                gather(head, 1, sb, mb)
                score(head, 3, sb, mb)
                gather(head, 2, sa, ma)
                score(jnp.minimum(head + 1, QHEADS - 1), 0, sa, ma, masked=True)
                gather(head, 3, sb, mb)
                for copy in leaving(head):
                    copy.start()
                return 0

            @pl.when(count == NZ)
            def _():
                score(0, 0, sa, ma, masked=True)
                lax.fori_loop(0, QHEADS, full_head, 0)

            @pl.when(count < NZ)
            def _():
                lax.fori_loop(0, QHEADS, one_head, 0)

            for head in range(QHEADS):
                for copy in leaving(head):
                    copy.wait()
        else:
            steps = 2 * count

            def where_at(step):
                head = step // steps
                return jnp.minimum(head, QHEADS - 1), 2 * (step - head * steps)

            score(0, 0, sa, ma)

            def body(step, _):
                head, at = where_at(step)
                if not fresh:

                    @pl.when(at == 0)
                    def _():
                        for copy in carried(head):
                            copy.wait()

                score(head, at + 1, sb, mb)
                gather(head, at, sa, ma)
                score(*where_at(step + 1), sa, ma)
                gather(head, at + 1, sb, mb)
                return 0

            lax.fori_loop(0, QHEADS * steps, body, 0)

    if not own:
        if not fresh:

            @pl.when(count == 0)
            def _():
                for head in range(QHEADS):
                    for copy in carried(head):
                        copy.wait()

        @pl.when(jnp.logical_or(count > 0, not fresh))
        def _():
            lane = lax.broadcasted_iota(jnp.int32, (TOK, HD), 1)
            log = jnp.zeros((TOK, HD), F32)
            for head in range(QHEADS):
                total = sums[head, :, HD:]
                part_ref[:, head * HD : (head + 1) * HD] = (sums[head, :, :HD] / total).astype(BF)
                for at, part in enumerate(three_parts(top[head] + jnp.log2(total))):
                    log = jnp.where(lane == 32 * head + at, part, log)
            part_ref[:, QHEADS * HD :] = log.astype(BF)


def attend(flags, query, *pieces, carry=None, own=False):
    fresh = carry is None
    planes = len(pieces) // 2
    vmem = pl.BlockSpec(memory_space=pltpu.VMEM)
    hbm = pl.BlockSpec(memory_space=pl.ANY)
    if own:
        out = [
            jax.ShapeDtypeStruct((QHEADS, TOK, 2 * HD), F32),
            jax.ShapeDtypeStruct((QHEADS, TOK, HD), F32),
        ]
        out_specs = [hbm, hbm]
    else:
        out, out_specs = jax.ShapeDtypeStruct((TOK, (QHEADS + 1) * HD), BF), vmem
    return pl.pallas_call(
        functools.partial(attend_kernel, planes=planes, own=own, fresh=fresh),
        in_specs=[pl.BlockSpec(memory_space=pltpu.SMEM), vmem]
        + [hbm] * len(pieces)
        + ([] if fresh else [hbm, hbm]),
        out_specs=out_specs,
        out_shape=out,
        scratch_shapes=[
            pltpu.VMEM((planes * NZ, NC, TOK, 2 * HD), BF),
            pltpu.VMEM((QHEADS, TOK, 2 * HD), F32),
            pltpu.VMEM((QHEADS, TOK, HD), F32),
            pltpu.VMEM((QHEADS, TOK, 2 * HD), BF),
            pltpu.VMEM((TOK, CHUNK), F32),
            pltpu.VMEM((TOK, CHUNK), F32),
            pltpu.VMEM((TOK, HD), F32),
            pltpu.VMEM((TOK, HD), F32),
            pltpu.SemaphoreType.DMA((planes, 2)),
            pltpu.SemaphoreType.DMA((2, QHEADS)),
            pltpu.SemaphoreType.DMA((2, QHEADS)),
        ],
        compiler_params=pltpu.CompilerParams(vmem_limit_bytes=VMEM_LIMIT),
        cost_estimate=pl.CostEstimate(
            flops=1 << 35 if fresh and not own else 1 << 20, bytes_accessed=1 << 16, transcendentals=0
        ),
    )(flags, query, *pieces, *([] if fresh else carry))


def merge_kernel(flag_ref, mine_ref, other_ref, out_ref):
    row = lax.broadcasted_iota(jnp.int32, (HD, HD), 0)
    with_other = flag_ref[0] > 0
    logs = [ref[:, QHEADS * HD :] for ref in (mine_ref, other_ref)]
    for head in range(QHEADS):
        pick = jnp.where((row >= 32 * head) & (row < 32 * head + 3), 1.0, 0.0).astype(BF)
        mine, other = [jnp.dot(log, pick, preferred_element_type=F32) for log in logs]
        other = jnp.where(with_other, other, -1e30)
        new = jnp.maximum(mine, other)
        mine, other = jnp.exp2(mine - new), jnp.exp2(other - new)
        columns = slice(head * HD, (head + 1) * HD)
        joint = mine_ref[:, columns].astype(F32) * mine + other_ref[:, columns].astype(F32) * other
        out_ref[:, columns] = (joint / (mine + other)).astype(BF)


def merge(flags, part, other):
    rows = TOK // 2
    wide = pl.BlockSpec((rows, (QHEADS + 1) * HD), lambda r: (r, 0))
    return pl.pallas_call(
        merge_kernel,
        grid=(TOK // rows,),
        in_specs=[pl.BlockSpec(memory_space=pltpu.SMEM), wide, wide],
        out_specs=pl.BlockSpec((rows, QHEADS * HD), lambda r: (r, 0)),
        out_shape=jax.ShapeDtypeStruct((TOK, QHEADS * HD), BF),
        compiler_params=pltpu.CompilerParams(vmem_limit_bytes=VMEM_LIMIT),
        cost_estimate=pl.CostEstimate(flops=1 << 20, bytes_accessed=1 << 16, transcendentals=0),
    )(flags, part, other)


def local(
    hidden,
    dt_weight,
    dt_bias,
    decay_rate,
    skip_gain,
    ssm_in,
    bc_in,
    conv_x,
    conv_bc,
    gate_in,
    norm_gain,
    query_heads,
    key_heads,
    value_heads,
):
    mine = lax.axis_index("ctx")
    x, z, c = mine // (NZ * NC), (mine // NC) % NZ, mine % NC
    core = c.astype(jnp.int32)[None]

    def flags(count):
        return jnp.stack([count, jnp.where(z == NZ - 1, 2, 3), c]).astype(jnp.int32)

    bc = bc_in.reshape(TOK, 2 * STATE)
    ends = jnp.concatenate([ssm_in[TOK - 16 :], bc[TOK - 16 :]], axis=1)
    tail = lax.ppermute(ends, "ctx", [(i, i + 1) for i in range(31)])
    partial = lax.dot_general(
        dt_weight, hidden, (((0,), (1,)), ((), ())), preferred_element_type=F32
    )
    partial, tail, keys, query = lax.optimization_barrier((partial, tail, key_heads, query_heads))
    parts = lax.all_to_all(partial.reshape(8, HEADS, TOK), "head", 0, 0, tiled=True)
    xin, pair = convolved(ssm_in, tail, bc, conv_x, conv_bc.reshape(4, 2 * STATE))
    rows = jnp.concatenate([keys, value_heads], axis=1)
    up, down = along_z(rows, 1), along_z(rows, -1)
    visitor = send(query, lambda x, z, c: (x - 1, z, c) if x >= 2 else None)
    parts, xin, pair = lax.optimization_barrier((parts, xin, pair))
    steps = jax.nn.softplus(jnp.sum(parts, axis=0) + dt_bias[:, None])
    drop = -steps * decay_rate[:, None]
    total = jnp.sum(drop, axis=1)
    cum, logs, starts, keep, give = own_states(core, xin, pair, steps, drop)

    keep, give, up, down, visitor = lax.optimization_barrier((keep, give, up, down, visitor))
    other = swap_core(give)
    partner = jnp.sum(other[CHAN // 2, : 3 * HEADS].astype(F32).reshape(3, HEADS), axis=0)
    other = other[: CHAN // 2]
    by_half = lambda value: lax.dynamic_index_in_dim(value.reshape(2, 16), c, 0, False)
    shape = (16, PSIZE, STATE)
    log_first = by_half(jnp.where(c == 0, total, partner))
    log_second = by_half(jnp.where(c == 0, partner, total))
    early = jnp.where(c == 0, keep, other).reshape(shape).astype(F32)
    late = jnp.where(c == 0, other, keep).reshape(shape).astype(F32)
    both = with_logs(
        late + jnp.exp(log_second)[:, None, None] * early, log_first + log_second
    )
    collected = exchanged(both)
    both, xin, rows, up, down, visitor = lax.optimization_barrier(
        (both, xin, rows, up, down, visitor)
    )
    middle = TOK // 2
    two = [along_z(up[:middle], 1), along_z(down[middle:], -1)]
    visitor = send(visitor, lambda x, z, c: (x - 1, z, c) if x in (1, 2) else None)
    y = inside_blocks(xin, pair, cum, steps, starts, jnp.repeat(skip_gain, PSIZE)[None])
    plane = jnp.stack([rows, up, down, jnp.concatenate(two, axis=0)])
    plane_pair = swap_core(plane)
    left = along_x(plane, 1)
    right = send(plane, lambda x, z, c: (NX - 1, z, c) if x == 0 else None)
    seen = attend(flags(z + 1), query, plane, plane_pair, own=True)
    collected, y, seen = lax.optimization_barrier((collected, y, seen))
    carried = chain(collected)
    chip_in = exchanged(carried)
    planes_seen = jnp.where(x == 0, 0, jnp.where(x == NX - 1, 2, 1))
    carried, to_visit, to_see, visitor, left, right = lax.optimization_barrier(
        (carried, flags(jnp.where(x <= 1, 1, 0)), flags(planes_seen), visitor, left, right)
    )
    left_pair = swap_core(left)
    right_pair = swap_core(right)
    part = attend(to_visit, visitor, plane, plane_pair)
    part, to_see = lax.optimization_barrier((part, to_see))
    part = send(part, lambda x, z, c: (x + 2, z, c) if x <= 1 else None)
    seen = attend(to_see, query, left, left_pair, right, right_pair, carry=seen)
    chip_in, seen = lax.optimization_barrier((chip_in, seen))
    after = (early + jnp.exp(log_first)[:, None, None] * chip_in.astype(F32)).astype(BF)
    entering = jnp.where(c == 0, chip_in, after).reshape(CHAN // 2, STATE)
    sent = jnp.where(c == 0, after, chip_in).reshape(CHAN // 2, STATE)
    received = swap_core(sent)
    sent, seen = lax.optimization_barrier((sent, seen))
    attn_out = merge(flags(jnp.where(x >= 2, 1, 0)), seen, part)
    received, attn_out = lax.optimization_barrier((received, attn_out))
    mamba_out = finish(core, y, pair, logs, entering, received, gate_in, norm_gain[None])
    return (mamba_out, attn_out)


def solution(mesh):
    in_specs = (
        P("ctx", "head"),
        P("head", None),
        P("head"),
        P("head"),
        P("head"),
        P("ctx", "head"),
        P("ctx", "head", None),
        P(None, "head"),
        P(None, "head", None),
        P("ctx", "head"),
        P("head"),
        P("ctx", "head"),
        P("ctx", "head"),
        P("ctx", "head"),
    )
    out_specs = (P("ctx", "head"), P("ctx", "head"))
    return jax.shard_map(local, mesh=mesh, in_specs=in_specs, out_specs=out_specs, check_vma=False)
```

time: 182 us -> 157 us (0.86)
  the two profiles are of different devices: /device:TPU:23 before, /device:TPU:35 now
where the time goes in v3:
time: 157 us; the launch traced here: 154 us
  Pallas kernels  74.9 us (48%)
  starting transfers between devices  56.9 us (36%)
  local copies, waits for them, and re-layouts  8.81 us (6%)
  other arithmetic  7.61 us (5%)
  waiting for transfers between devices  2.37 us (2%)
  matrix products  2.32 us (1%)
    pallas_call x3, Pallas kernels, attend(): pl.pallas_call(functools.partial(attend_kernel, planes=planes, own=own, f...  40.2 us
    ppermute x14, starting transfers between devices, send(): return lax.ppermute(value, 'ctx', pairs_of(move))  25.5 us
    all_to_all x2, starting transfers between devices, exchanged(): lax.all_to_all(value, 'ctx', 0, 0, tiled=True, axis_index_groups=SAME_CORE)  20.6 us
    pallas_call x1, Pallas kernels, inside_blocks(): pl.pallas_call(inside_kernel, grid=(TOK // SPAN, blocks), in_specs=[pl.Bl...  8.46 us
    pallas_call x1, Pallas kernels, own_states(): pl.pallas_call(states_kernel, grid=(TOK // SPAN,), in_specs=[pl.BlockSpec...  8.38 us
    pallas_call x1, Pallas kernels, finish(): pl.pallas_call(finish_kernel, grid=(TOK // SPAN,), in_specs=[pl.BlockSpec...  7.26 us
    unnamed x38, local copies, waits for them, and re-layouts  6.06 us
    pallas_call x1, Pallas kernels, convolved(): pl.pallas_call(conv_kernel, grid=(TOK // SPAN,), in_specs=[pl.BlockSpec((...  6.01 us
  transfers between devices with their start and end apart: 18, of which 2 were waited for; matrix products, arithmetic and copies ran while one was open for 6% of the time, Pallas kernels for 44%

profile of v3, /device:TPU:35, one launch (start us, length us, event | category | flops | bytes accessed | tf_op | source)
XLA Modules:
  0.0 153.9 jit_solution(17315476682550759475)
XLA Ops:
  0.6 0.0 copy-start
  0.7 0.0 copy-start.3
  0.7 0.8 slice_bitcast_fusion
  1.5 0.8 slice.21
  2.4 5.5 %collective-permute-start = (bf16[16,2560]{1,0:T(8,128)(2,1)S(1)}, bf16[16,2560]{1,0:T(8,128)(2,1)S(1)}, u32[]{:S(2)}, u32[]{:S(2)}) collective-permute-start(bf16[16,2560]{1,0:T(8,128)(2,1)S(1)} %pad_maximum_fusion.2), channel_id=1, source_target_pairs={{0,8},{8,16},{16,24},{24,32},{32,40},{40,48},{48,56},{56,64},{64,7... | collective-permute-start | bytes 245768 | tf_op jit(solution)/shard_map/ppermute | solution.py:702
  7.9 2.3 %fusion.10 = f32[256,512]{1,0:T(8,128)} fusion(bf16[1024,256]{1,0:T(8,128)(2,1)} %param.20, bf16[512,1024]{1,0:T(8,128)(2,1)S(1)} %copy-done), kind=kOutput, calls=%fused_computation.42 | convolution fusion | flops 268435456 | bytes 2097152 | tf_op jit(solution)/shard_map/dot_general | solution.py:703
  10.2 0.0 collective-permute-done.xtail_ref.ptail_ref
  10.2 5.4 %all-to-all-start = ((f32[8,32,512]{2,1,0:T(8,128)}), f32[8,32,512]{2,1,0:T(8,128)S(1)}, u32[]{:S(2)}, u32[]{:S(2)}) async-start(f32[8,32,512]{2,1,0:T(8,128)} %bitcast.2), calls=%async_computation | async-start | bytes 1048576 | tf_op jit(solution)/shard_map/all_to_all | solution.py:707
  15.6 1.3 collective-permute-start.3
  17.0 1.7 %collective-permute-start.2 = (bf16[512,256]{1,0:T(8,128)(2,1)S(1)}, bf16[512,256]{1,0:T(8,128)(2,1)S(1)}, u32[]{:S(2)}, u32[]{:S(2)}) collective-permute-start(bf16[512,256]{1,0:T(8,128)(2,1)S(1)} %constant_dynamic-update-slice_fusion), channel_id=1, source_target_pairs={{0,48},{8,56},{16,0},{24,8},{32,16},{40,24},{48,32},{56,40},{64,11... | collective-permute-start | bytes 786440 | tf_op jit(solution)/shard_map/ppermute | solution.py:39
  18.6 1.8 %collective-permute-start.1 = (bf16[512,256]{1,0:T(8,128)(2,1)S(1)}, bf16[512,256]{1,0:T(8,128)(2,1)S(1)}, u32[]{:S(2)}, u32[]{:S(2)}) collective-permute-start(bf16[512,256]{1,0:T(8,128)(2,1)S(1)} %constant_dynamic-update-slice_fusion), channel_id=1, source_target_pairs={{0,16},{8,24},{16,32},{24,40},{32,48},{40,56},{48,0},{56,8},{64,80... | collective-permute-start | bytes 786440 | tf_op jit(solution)/shard_map/ppermute | solution.py:39
  20.4 0.6 copy.23
  21.0 6.0 %shard_map.194 = (bf16[512,2048]{1,0:T(8,128)(2,1)}, bf16[512,512]{1,0:T(8,128)(2,1)}) custom-call(bf16[512,2048]{1,0:T(8,128)(2,1)} %before_ref.1, bf16[512,2048]{1,0:T(8,128)(2,1)} %before_ref.1, bf16[16,2560]{1,0:T(8,128)(2,1)} %copy-done.11, bf16[512,512]{1,0:T(8,128)(2,1)} %bitcast.44, bf16[512,512]{1,0:T(8,128)(2,1)} %bitcast.45, ...), custom_call_target="tpu_custom_call" | custom-call | flops 1048576 | bytes 65536 | tf_op jit(solution)/shard_map/pallas_call | solution.py:100
  27.0 0.0 all-to-all-done
  27.1 0.9 fusion.9
  28.0 8.4 %shard_map.195 = (f32[32,512]{1,0:T(8,128)}, f32[32,512]{1,0:T(8,128)}, bf16[8192,256]{1,0:T(8,128)(2,1)}, bf16[1024,256]{1,0:T(8,128)(2,1)}, bf16[1040,256]{1,0:T(8,128)(2,1)}) custom-call(s32[1]{0:T(128)} %bitcast.core_ref, bf16[512,2048]{1,0:T(8,128)(2,1)} %get-tuple-element.60.xin_ref, bf16[512,512]{1,0:T(8,128)(2,1)} %get-tuple-element.49.pair_ref.c_ref, ...), custom_call_target="tpu_custom_call" | custom-call | flops 1048576 | bytes 65536 | tf_op jit(solution)/shard_map/pallas_call | solution.py:200
  36.4 0.6 collective-permute-done.2
  37.0 0.0 collective-permute-done.1
  37.0 0.0 collective-permute-done.3
  37.0 3.3 %collective-permute-start.4 = (bf16[1040,256]{1,0:T(8,128)(2,1)}, bf16[1040,256]{1,0:T(8,128)(2,1)S(1)}, u32[]{:S(2)}, u32[]{:S(2)}) collective-permute-start(bf16[1040,256]{1,0:T(8,128)(2,1)} %get-tuple-element.55), channel_id=1, source_target_pairs={{0,8},{8,0},{16,24},{24,16},{32,40},{40,32},{48,56},{56,48},{64,72... | collective-permute-start | bytes 1597448 | tf_op jit(solution)/shard_map/ppermute | solution.py:39
  40.3 1.7 %collective-permute-done.4 = bf16[1040,256]{1,0:T(8,128)(2,1)S(1)} collective-permute-done((bf16[1040,256]{1,0:T(8,128)(2,1)}, bf16[1040,256]{1,0:T(8,128)(2,1)S(1)}, u32[]{:S(2)}, u32[]{:S(2)}) %collective-permute-start.4) | collective-permute-done | bytes 532512 | tf_op jit(solution)/shard_map/ppermute | solution.py:39
  42.1 0.1 reshape.90
  42.2 0.1 select_n.112
  42.3 0.1 select_n.108
  42.4 1.1 broadcast_select_fusion.1
  43.5 0.0 copy-start.17
  43.5 0.2 fusion.1
  43.7 0.1 select_convert_fusion
  43.9 0.9 pad_maximum_fusion.1
  44.8 5.0 %collective-permute-start.6 = (bf16[256,256]{1,0:T(8,128)(2,1)S(1)}, bf16[256,256]{1,0:T(8,128)(2,1)S(1)}, u32[]{:S(2)}, u32[]{:S(2)}) collective-permute-start(bf16[256,256]{1,0:T(8,128)(2,1)S(1)} %slice.27), channel_id=1, source_target_pairs={{0,48},{8,56},{16,0},{24,8},{32,16},{40,24},{48,32},{56,40},{64,11... | collective-permute-start | bytes 393224 | tf_op jit(solution)/shard_map/ppermute | solution.py:39
  49.8 0.0 collective-permute-start.5
  49.8 0.7 add_add_fusion.flag_ref
  50.4 0.1 broadcast_in_dim.46
  50.5 0.7 broadcast_in_dim_reshape.3.skip_ref
  51.2 0.7 add_add_fusion.1
  51.9 7.6 %all-to-all-start.1 = ((bf16[16,80,256]{2,1,0:T(8,128)(2,1)}), bf16[16,80,256]{2,1,0:T(8,128)(2,1)S(1)}, u32[]{:S(2)}, u32[]{:S(2)}) async-start(bf16[16,80,256]{2,1,0:T(8,128)(2,1)} %pad_maximum_fusion.1), calls=%async_computation.1 | async-start | bytes 1310720 | tf_op jit(solution)/shard_map/all_to_all | solution.py:365
  59.5 2.0 %collective-permute-start.8 = (bf16[512,512]{1,0:T(8,128)(2,1)}, bf16[512,512]{1,0:T(8,128)(2,1)}, u32[]{:S(2)}, u32[]{:S(2)}) collective-permute-start(bf16[512,512]{1,0:T(8,128)(2,1)} %collective-permute-done.3), channel_id=1, source_target_pairs={{64,0},{72,8},{80,16},{88,24},{96,32},{104,40},{112,48},{120,56},{... | collective-permute-start | bytes 1572872 | tf_op jit(solution)/shard_map/ppermute | solution.py:39
  61.6 1.2 pad_maximum_fusion.refs_0_
  62.8 1.7 %collective-permute-start.10 = (bf16[4,512,256]{2,1,0:T(8,128)(2,1)S(1)}, bf16[4,512,256]{2,1,0:T(8,128)(2,1)}, u32[]{:S(2)}, u32[]{:S(2)}) collective-permute-start(bf16[4,512,256]{2,1,0:T(8,128)(2,1)S(1)} %pad_maximum_fusion.refs_0_), channel_id=1, source_target_pairs={{0,192},{8,200},{16,208},{24,216},{32,224},{40,232},{48,240},{56,2... | collective-permute-start | bytes 3145736 | tf_op jit(solution)/shard_map/ppermute | solution.py:39
  64.5 4.0 %collective-permute-start.9 = (bf16[4,512,256]{2,1,0:T(8,128)(2,1)S(1)}, bf16[4,512,256]{2,1,0:T(8,128)(2,1)}, u32[]{:S(2)}, u32[]{:S(2)}) collective-permute-start(bf16[4,512,256]{2,1,0:T(8,128)(2,1)S(1)} %pad_maximum_fusion.refs_0_), channel_id=1, source_target_pairs={{0,64},{8,72},{16,80},{24,88},{32,96},{40,104},{48,112},{56,120},{... | collective-permute-start | bytes 3145736 | tf_op jit(solution)/shard_map/ppermute | solution.py:39
  68.5 2.1 %collective-permute-start.7 = (bf16[4,512,256]{2,1,0:T(8,128)(2,1)S(1)}, bf16[4,512,256]{2,1,0:T(8,128)(2,1)S(1)}, u32[]{:S(2)}, u32[]{:S(2)}) collective-permute-start(bf16[4,512,256]{2,1,0:T(8,128)(2,1)S(1)} %pad_maximum_fusion.refs_0_), channel_id=1, source_target_pairs={{0,8},{8,0},{16,24},{24,16},{32,40},{40,32},{48,56},{56,48},{64,72... | collective-permute-start | bytes 3145736 | tf_op jit(solution)/shard_map/ppermute | solution.py:39
  70.7 8.5 %shard_map.196.y_ref = bf16[512,2048]{1,0:T(8,128)(2,1)} custom-call(bf16[512,2048]{1,0:T(8,128)(2,1)} %get-tuple-element.60.xin_ref, bf16[512,512]{1,0:T(8,128)(2,1)} %get-tuple-element.49.pair_ref.c_ref, f32[32,512]{1,0:T(8,128)} %get-tuple-element.61.cum_ref, f32[32,512]{1,0:T(8,128)} %get-tuple-element.90.steps_ref, ...), custom_call_target="tpu_custom_call" | custom-call | flops 17179869184 | bytes 65536 | tf_op jit(solution)/shard_map/pallas_call | solution.py:306
  79.2 1.0 copy-done.6
  80.1 7.8 %shard_map.197 = (f32[4,512,256]{2,1,0:T(8,128)}, f32[4,512,128]{2,1,0:T(8,128)}) custom-call(s32[3]{0:T(128)} %add_add_fusion.flag_ref, bf16[512,512]{1,0:T(8,128)(2,1)} %q_ref.1, bf16[4,512,256]{2,1,0:T(8,128)(2,1)} %copy-done.1, bf16[4,512,256]{2,1,0:T(8,128)(2,1)} %copy-done.6), custom_call_target="tpu_custom_call" | custom-call | flops 1048576 | bytes 65536 | tf_op jit(solution)/shard_map/pallas_call | solution.py:621
  88.0 0.0 all-to-all-done.1.from_ref
  88.0 0.8 copy-done.2
  88.8 2.0 %shard_map.198 = bf16[16,64,256]{2,1,0:T(8,128)(2,1)} custom-call(bf16[16,80,256]{2,1,0:T(8,128)(2,1)} %copy-done.2), custom_call_target="tpu_custom_call" | custom-call | flops 1048576 | bytes 65536 | tf_op jit(solution)/shard_map/pallas_call | solution.py:346
  90.9 12.9 %all-to-all-start.2 = ((bf16[16,64,256]{2,1,0:T(8,128)(2,1)}), bf16[16,64,256]{2,1,0:T(8,128)(2,1)S(1)}, u32[]{:S(2)}, u32[]{:S(2)}) async-start(bf16[16,64,256]{2,1,0:T(8,128)(2,1)} %shard_map.198), calls=%async_computation.2 | async-start | bytes 1048576 | tf_op jit(solution)/shard_map/all_to_all | solution.py:365
  103.8 0.0 collective-permute-done.10.refs_2_
  103.8 0.7 collective-permute-start.11
  104.5 0.1 collective-permute-start.12
  104.6 15.6 %shard_map.199 = bf16[512,640]{1,0:T(8,128)(2,1)} custom-call(s32[3]{0:T(128)} %get-tuple-element.72.flag_ref, bf16[512,512]{1,0:T(8,128)(2,1)} %collective-permute-done.8.q_ref, bf16[4,512,256]{2,1,0:T(8,128)(2,1)} %copy-done.1, bf16[4,512,256]{2,1,0:T(8,128)(2,1)} %copy-done.6), custom_call_target="tpu_custom_call" | custom-call | flops 34359738368 | bytes 65536 | tf_op jit(solution)/shard_map/pallas_call | solution.py:621
  120.2 1.3 collective-permute-start.14
  121.6 0.0 collective-permute-done.12.refs_3_
  121.6 1.0 copy-done.4
  122.6 1.0 copy-done.5
  123.6 16.7 %shard_map.200.mine_ref = bf16[512,640]{1,0:T(8,128)(2,1)} custom-call(s32[3]{0:T(128)} %get-tuple-element.75.flag_ref, bf16[512,512]{1,0:T(8,128)(2,1)} %q_ref.1, bf16[4,512,256]{2,1,0:T(8,128)(2,1)} %collective-permute-done.9.refs_0_, bf16[4,512,256]{2,1,0:T(8,128)(2,1)} %copy-done.4, bf16[4,512,256]{2,1,0:T(8,128)(2,1)} %collective-permute-done.10.refs_2_, ...), custom_call_target="tpu_custom_call" | custom-call | flops 1048576 | bytes 65536 | tf_op jit(solution)/shard_map/pallas_call | solution.py:621
  140.2 1.2 fusion.3
  141.4 0.4 collective-permute-start.13
  141.8 0.6 add_add_fusion.3.flag_ref
  142.4 0.8 copy-done.7
  143.3 2.6 %shard_map.201 = bf16[512,512]{1,0:T(8,128)(2,1)} custom-call(s32[3]{0:T(128)} %add_add_fusion.3.flag_ref, bf16[512,640]{1,0:T(8,128)(2,1)} %shard_map.200.mine_ref, bf16[512,640]{1,0:T(8,128)(2,1)} %copy-done.7), custom_call_target="tpu_custom_call" | custom-call | flops 1048576 | bytes 65536 | tf_op jit(solution)/shard_map/pallas_call | solution.py:666
  145.9 0.8 copy-done.10
  146.7 7.3 %shard_map.202 = bf16[512,2048]{1,0:T(8,128)(2,1)} custom-call(s32[1]{0:T(128)} %bitcast.core_ref, bf16[512,2048]{1,0:T(8,128)(2,1)} %shard_map.196.y_ref, bf16[512,512]{1,0:T(8,128)(2,1)} %get-tuple-element.49.pair_ref.c_ref, f32[32,512]{1,0:T(8,128)} %get-tuple-element.69.log_ref, bf16[1024,256]{1,0:T(8,128)(2,1)} %bitcast.47, ...), custom_call_target="tpu_custom_call" | custom-call | flops 1048576 | bytes 65536 | tf_op jit(solution)/shard_map/pallas_call | solution.py:393
  (50 shorter events, 0.3 us)
Async XLA Ops:
  0.6 7.2 %copy-start = (bf16[512,1024]{1,0:T(8,128)(2,1)S(1)}, bf16[512,1024]{1,0:T(8,128)(2,1)}, u32[]{:S(2)}) copy-start(bf16[512,1024]{1,0:T(8,128)(2,1)} %param.19) | copy-start | bytes 3145732
  0.6 16.2 %copy-start.12 = (bf16[512,128]{1,0:T(8,128)(2,1)S(1)}, bf16[512,128]{1,0:T(8,128)(2,1)}, u32[]{:S(2)}) copy-start(bf16[512,128]{1,0:T(8,128)(2,1)} %param.31) | copy-start | bytes 393220
  0.7 14.9 %copy-start.3 = (bf16[512,512]{1,0:T(8,128)(2,1)S(1)}, bf16[512,512]{1,0:T(8,128)(2,1)}, u32[]{:S(2)}) copy-start(bf16[512,512]{1,0:T(8,128)(2,1)} %q_ref.1) | copy-start | bytes 1572868
  0.7 16.2 %copy-start.13 = (bf16[512,128]{1,0:T(8,128)(2,1)S(1)}, bf16[512,128]{1,0:T(8,128)(2,1)}, u32[]{:S(2)}) copy-start(bf16[512,128]{1,0:T(8,128)(2,1)} %param.32) | copy-start | bytes 393220
  0.7 19.8 %copy-start.14 = (f32[4,1,512]{2,1,0:T(1,128)S(1)}, f32[4,1,512]{2,1,0:T(1,128)}, u32[]{:S(2)}) copy-start(f32[4,1,512]{2,1,0:T(1,128)} %param.27) | copy-start | bytes 24580
  2.4 7.8 %collective-permute-start = (bf16[16,2560]{1,0:T(8,128)(2,1)S(1)}, bf16[16,2560]{1,0:T(8,128)(2,1)S(1)}, u32[]{:S(2)}, u32[]{:S(2)}) collective-permute-start(bf16[16,2560]{1,0:T(8,128)(2,1)S(1)} %pad_maximum_fusion.2), channel_id=1, source_target_pairs={{0,8},{8,16},{16,24},{24,32},{32,40},{40,48},{48,56},{56,64},{64,7... | collective-permute-start | bytes 245768 | tf_op jit(solution)/shard_map/ppermute | solution.py:702
  10.2 10.8 %copy-start.11 = (bf16[16,2560]{1,0:T(8,128)(2,1)}, bf16[16,2560]{1,0:T(8,128)(2,1)S(1)}, u32[]{:S(2)}) copy-start(bf16[16,2560]{1,0:T(8,128)(2,1)S(1)} %collective-permute-done.xtail_ref.ptail_ref) | copy-start | bytes 245764
  10.2 16.9 %all-to-all-start = ((f32[8,32,512]{2,1,0:T(8,128)}), f32[8,32,512]{2,1,0:T(8,128)S(1)}, u32[]{:S(2)}, u32[]{:S(2)}) async-start(f32[8,32,512]{2,1,0:T(8,128)} %bitcast.2), calls=%async_computation | async-start | bytes 1048576 | tf_op jit(solution)/shard_map/all_to_all | solution.py:707
  15.6 21.4 %collective-permute-start.3 = (bf16[512,512]{1,0:T(8,128)(2,1)S(1)}, bf16[512,512]{1,0:T(8,128)(2,1)}, u32[]{:S(2)}, u32[]{:S(2)}) collective-permute-start(bf16[512,512]{1,0:T(8,128)(2,1)S(1)} %copy-done.3), channel_id=1, source_target_pairs={{128,64},{136,72},{144,80},{152,88},{160,96},{168,104},{176,112},{... | collective-permute-start | bytes 1572872 | tf_op jit(solution)/shard_map/ppermute | solution.py:39
  16.9 26.8 %copy-start.9 = (bf16[512,256]{1,0:T(8,128)(2,1)}, bf16[512,256]{1,0:T(8,128)(2,1)S(1)}, u32[]{:S(2)}) copy-start(bf16[512,256]{1,0:T(8,128)(2,1)S(1)} %constant_dynamic-update-slice_fusion) | copy-start | bytes 786436
  17.0 20.0 %collective-permute-start.2 = (bf16[512,256]{1,0:T(8,128)(2,1)S(1)}, bf16[512,256]{1,0:T(8,128)(2,1)S(1)}, u32[]{:S(2)}, u32[]{:S(2)}) collective-permute-start(bf16[512,256]{1,0:T(8,128)(2,1)S(1)} %constant_dynamic-update-slice_fusion), channel_id=1, source_target_pairs={{0,48},{8,56},{16,0},{24,8},{32,16},{40,24},{48,32},{56,40},{64,11... | collective-permute-start | bytes 786440 | tf_op jit(solution)/shard_map/ppermute | solution.py:39
  18.6 18.3 %collective-permute-start.1 = (bf16[512,256]{1,0:T(8,128)(2,1)S(1)}, bf16[512,256]{1,0:T(8,128)(2,1)S(1)}, u32[]{:S(2)}, u32[]{:S(2)}) collective-permute-start(bf16[512,256]{1,0:T(8,128)(2,1)S(1)} %constant_dynamic-update-slice_fusion), channel_id=1, source_target_pairs={{0,16},{8,24},{16,32},{24,40},{32,48},{40,56},{48,0},{56,8},{64,80... | collective-permute-start | bytes 786440 | tf_op jit(solution)/shard_map/ppermute | solution.py:39
  21.0 6.1 %copy-start.15 = (f32[32]{0:T(128)S(1)}, f32[32]{0:T(128)}, u32[]{:S(2)}) copy-start(f32[32]{0:T(128)} %param.22) | copy-start | bytes 388
  21.0 6.1 %copy-start.16 = (f32[32]{0:T(128)S(1)}, f32[32]{0:T(128)}, u32[]{:S(2)}) copy-start(f32[32]{0:T(128)} %param.21) | copy-start | bytes 388
  37.0 24.6 %copy-start.8 = (bf16[512,256]{1,0:T(8,128)(2,1)}, bf16[512,256]{1,0:T(8,128)(2,1)S(1)}, u32[]{:S(2)}) copy-start(bf16[512,256]{1,0:T(8,128)(2,1)S(1)} %collective-permute-done.1) | copy-start | bytes 786436
  37.0 5.1 %collective-permute-start.4 = (bf16[1040,256]{1,0:T(8,128)(2,1)}, bf16[1040,256]{1,0:T(8,128)(2,1)S(1)}, u32[]{:S(2)}, u32[]{:S(2)}) collective-permute-start(bf16[1040,256]{1,0:T(8,128)(2,1)} %get-tuple-element.55), channel_id=1, source_target_pairs={{0,8},{8,0},{16,24},{24,16},{32,40},{40,32},{48,56},{56,48},{64,72... | collective-permute-start | bytes 1597448 | tf_op jit(solution)/shard_map/ppermute | solution.py:39
  43.5 6.9 %copy-start.17 = (f32[32]{0:T(128)S(1)}, f32[32]{0:T(128)}, u32[]{:S(2)}) copy-start(f32[32]{0:T(128)} %param.23) | copy-start | bytes 388
  44.8 16.7 %collective-permute-start.6 = (bf16[256,256]{1,0:T(8,128)(2,1)S(1)}, bf16[256,256]{1,0:T(8,128)(2,1)S(1)}, u32[]{:S(2)}, u32[]{:S(2)}) collective-permute-start(bf16[256,256]{1,0:T(8,128)(2,1)S(1)} %slice.27), channel_id=1, source_target_pairs={{0,48},{8,56},{16,0},{24,8},{32,16},{40,24},{48,32},{56,40},{64,11... | collective-permute-start | bytes 393224 | tf_op jit(solution)/shard_map/ppermute | solution.py:39
  49.8 11.8 %collective-permute-start.5 = (bf16[256,256]{1,0:T(8,128)(2,1)S(1)}, bf16[256,256]{1,0:T(8,128)(2,1)S(1)}, u32[]{:S(2)}, u32[]{:S(2)}) collective-permute-start(bf16[256,256]{1,0:T(8,128)(2,1)S(1)} %slice.26), channel_id=1, source_target_pairs={{0,16},{8,24},{16,32},{24,40},{32,48},{40,56},{48,0},{56,8},{64,80... | collective-permute-start | bytes 393224 | tf_op jit(solution)/shard_map/ppermute | solution.py:39
  51.9 36.1 %all-to-all-start.1 = ((bf16[16,80,256]{2,1,0:T(8,128)(2,1)}), bf16[16,80,256]{2,1,0:T(8,128)(2,1)S(1)}, u32[]{:S(2)}, u32[]{:S(2)}) async-start(bf16[16,80,256]{2,1,0:T(8,128)(2,1)} %pad_maximum_fusion.1), calls=%async_computation.1 | async-start | bytes 1310720 | tf_op jit(solution)/shard_map/all_to_all | solution.py:365
  59.5 44.3 %collective-permute-start.8 = (bf16[512,512]{1,0:T(8,128)(2,1)}, bf16[512,512]{1,0:T(8,128)(2,1)}, u32[]{:S(2)}, u32[]{:S(2)}) collective-permute-start(bf16[512,512]{1,0:T(8,128)(2,1)} %collective-permute-done.3), channel_id=1, source_target_pairs={{64,0},{72,8},{80,16},{88,24},{96,32},{104,40},{112,48},{120,56},{... | collective-permute-start | bytes 1572872 | tf_op jit(solution)/shard_map/ppermute | solution.py:39
  62.7 16.4 %copy-start.1 = (bf16[4,512,256]{2,1,0:T(8,128)(2,1)}, bf16[4,512,256]{2,1,0:T(8,128)(2,1)S(1)}, u32[]{:S(2)}) copy-start(bf16[4,512,256]{2,1,0:T(8,128)(2,1)S(1)} %pad_maximum_fusion.refs_0_) | copy-start | bytes 3145732
  62.8 41.0 %collective-permute-start.10 = (bf16[4,512,256]{2,1,0:T(8,128)(2,1)S(1)}, bf16[4,512,256]{2,1,0:T(8,128)(2,1)}, u32[]{:S(2)}, u32[]{:S(2)}) collective-permute-start(bf16[4,512,256]{2,1,0:T(8,128)(2,1)S(1)} %pad_maximum_fusion.refs_0_), channel_id=1, source_target_pairs={{0,192},{8,200},{16,208},{24,216},{32,224},{40,232},{48,240},{56,2... | collective-permute-start | bytes 3145736 | tf_op jit(solution)/shard_map/ppermute | solution.py:39
  64.5 39.3 %collective-permute-start.9 = (bf16[4,512,256]{2,1,0:T(8,128)(2,1)S(1)}, bf16[4,512,256]{2,1,0:T(8,128)(2,1)}, u32[]{:S(2)}, u32[]{:S(2)}) collective-permute-start(bf16[4,512,256]{2,1,0:T(8,128)(2,1)S(1)} %pad_maximum_fusion.refs_0_), channel_id=1, source_target_pairs={{0,64},{8,72},{16,80},{24,88},{32,96},{40,104},{48,112},{56,120},{... | collective-permute-start | bytes 3145736 | tf_op jit(solution)/shard_map/ppermute | solution.py:39
  68.5 10.6 %collective-permute-start.7 = (bf16[4,512,256]{2,1,0:T(8,128)(2,1)S(1)}, bf16[4,512,256]{2,1,0:T(8,128)(2,1)S(1)}, u32[]{:S(2)}, u32[]{:S(2)}) collective-permute-start(bf16[4,512,256]{2,1,0:T(8,128)(2,1)S(1)} %pad_maximum_fusion.refs_0_), channel_id=1, source_target_pairs={{0,8},{8,0},{16,24},{24,16},{32,40},{40,32},{48,56},{56,48},{64,72... | collective-permute-start | bytes 3145736 | tf_op jit(solution)/shard_map/ppermute | solution.py:39
  79.1 1.0 copy-start.6
  88.0 0.8 copy-start.2
  90.9 49.4 %all-to-all-start.2 = ((bf16[16,64,256]{2,1,0:T(8,128)(2,1)}), bf16[16,64,256]{2,1,0:T(8,128)(2,1)S(1)}, u32[]{:S(2)}, u32[]{:S(2)}) async-start(bf16[16,64,256]{2,1,0:T(8,128)(2,1)} %shard_map.198), calls=%async_computation.2 | async-start | bytes 1048576 | tf_op jit(solution)/shard_map/all_to_all | solution.py:365
  103.8 17.8 %collective-permute-start.11 = (bf16[4,512,256]{2,1,0:T(8,128)(2,1)}, bf16[4,512,256]{2,1,0:T(8,128)(2,1)S(1)}, u32[]{:S(2)}, u32[]{:S(2)}) collective-permute-start(bf16[4,512,256]{2,1,0:T(8,128)(2,1)} %collective-permute-done.9.refs_0_), channel_id=1, source_target_pairs={{0,8},{8,0},{16,24},{24,16},{32,40},{40,32},{48,56},{56,48},{64,72... | collective-permute-start | bytes 3145736 | tf_op jit(solution)/shard_map/ppermute | solution.py:39
  104.5 17.1 %collective-permute-start.12 = (bf16[4,512,256]{2,1,0:T(8,128)(2,1)}, bf16[4,512,256]{2,1,0:T(8,128)(2,1)S(1)}, u32[]{:S(2)}, u32[]{:S(2)}) collective-permute-start(bf16[4,512,256]{2,1,0:T(8,128)(2,1)} %collective-permute-done.10.refs_2_), channel_id=1, source_target_pairs={{0,8},{8,0},{16,24},{24,16},{32,40},{40,32},{48,56},{56,48},{64,72... | collective-permute-start | bytes 3145736 | tf_op jit(solution)/shard_map/ppermute | solution.py:39
  120.2 22.2 %collective-permute-start.14 = (bf16[512,640]{1,0:T(8,128)(2,1)}, bf16[512,640]{1,0:T(8,128)(2,1)S(1)}, u32[]{:S(2)}, u32[]{:S(2)}) collective-permute-start(bf16[512,640]{1,0:T(8,128)(2,1)} %shard_map.199), channel_id=1, source_target_pairs={{0,128},{8,136},{16,144},{24,152},{32,160},{40,168},{48,176},{56,1... | collective-permute-start | bytes 1966088 | tf_op jit(solution)/shard_map/ppermute | solution.py:39
  121.6 1.0 copy-start.4
  122.6 1.0 copy-start.5
  141.4 4.5 %collective-permute-start.13 = (bf16[1024,256]{1,0:T(8,128)(2,1)S(1)}, bf16[1024,256]{1,0:T(8,128)(2,1)S(1)}, u32[]{:S(2)}, u32[]{:S(2)}) collective-permute-start(bf16[1024,256]{1,0:T(8,128)(2,1)S(1)} %bitcast.51), channel_id=1, source_target_pairs={{0,8},{8,0},{16,24},{24,16},{32,40},{40,32},{48,56},{56,48},{64,72... | collective-permute-start | bytes 1572872 | tf_op jit(solution)/shard_map/ppermute | solution.py:39
  142.4 0.8 copy-start.7
  145.9 0.8 copy-start.10

commit v4 on v3

--- a/solution.py
+++ b/solution.py
@@ -3,7 +3,6 @@
 
 import jax
 import jax.numpy as jnp
-import numpy as np
 from jax import lax
 from jax.experimental import pallas as pl
 from jax.experimental.pallas import tpu as pltpu
@@ -21,6 +20,9 @@
 HBC = HB * PSIZE
 CHUNK = 1024
 VMEM_LIMIT = 58 << 20
+ATTEND_LIMIT = 28 << 20
+CONV_ROWS = 256
+END_ROWS = 256
 
 
 def pairs_of(move):
@@ -96,23 +98,23 @@
 
 
 def convolved(ssm_in, tail, bc_in, conv_x, conv_bc):
-    prior = lambda s: (jnp.maximum(s * (SPAN // 16) - 1, 0), 0)
+    prior = lambda s: (jnp.maximum(s * (CONV_ROWS // 16) - 1, 0), 0)
     return pl.pallas_call(
         conv_kernel,
-        grid=(TOK // SPAN,),
+        grid=(TOK // CONV_ROWS,),
         in_specs=[
-            pl.BlockSpec((SPAN, CHAN), lambda s: (s, 0)),
+            pl.BlockSpec((CONV_ROWS, CHAN), lambda s: (s, 0)),
             pl.BlockSpec((16, CHAN), prior),
             pl.BlockSpec((16, CHAN), lambda s: (0, 0)),
-            pl.BlockSpec((SPAN, 2 * STATE), lambda s: (s, 0)),
+            pl.BlockSpec((CONV_ROWS, 2 * STATE), lambda s: (s, 0)),
             pl.BlockSpec((16, 2 * STATE), prior),
             pl.BlockSpec((16, 2 * STATE), lambda s: (0, CHAN // (2 * STATE))),
             pl.BlockSpec((4, CHAN), lambda s: (0, 0)),
             pl.BlockSpec((4, 2 * STATE), lambda s: (0, 0)),
         ],
         out_specs=[
-            pl.BlockSpec((SPAN, CHAN), lambda s: (s, 0)),
-            pl.BlockSpec((SPAN, 2 * STATE), lambda s: (s, 0)),
+            pl.BlockSpec((CONV_ROWS, CHAN), lambda s: (s, 0)),
+            pl.BlockSpec((CONV_ROWS, 2 * STATE), lambda s: (s, 0)),
         ],
         out_shape=[
             jax.ShapeDtypeStruct((TOK, CHAN), BF),
@@ -129,15 +131,15 @@
     pair_ref,
     steps_ref,
     drop_ref,
-    spread_ref,
-    rows_ref,
     cum_ref,
     log_ref,
-    start_ref,
+    read_ref,
     mine_ref,
     give_ref,
     log_s,
     state_s,
+    spread_s,
+    rows_s,
 ):
     span = pl.program_id(0)
 
@@ -145,6 +147,11 @@
     def _():
         log_s[...] = jnp.zeros_like(log_s)
         state_s[...] = jnp.zeros_like(state_s)
+        spread_s[...] = spread_heads()
+        channel = lax.broadcasted_iota(jnp.int32, (CHAN, 4 * HEADS), 0)
+        column = lax.broadcasted_iota(jnp.int32, (CHAN, 4 * HEADS), 1)
+        hit = (column < 2 * HEADS) & (column % HEADS == channel // PSIZE)
+        rows_s[...] = jnp.where(hit, 1.0, 0.0).astype(BF)
 
     at_i = lax.broadcasted_iota(jnp.int32, (SPAN, SPAN), 0)
     at_j = lax.broadcasted_iota(jnp.int32, (SPAN, SPAN), 1)
@@ -158,21 +165,21 @@
         two_parts(jnp.exp(last - cum) * steps_ref[...]) + [jnp.zeros((2 * HEADS, SPAN), F32)], axis=0
     ).T.astype(BF)
     decays = jnp.broadcast_to(
-        jnp.concatenate(two_parts(jnp.exp(last)), axis=0), (2 * HEADS, STATE)
+        jnp.concatenate(two_parts(jnp.exp(last)) + [jnp.zeros((2 * HEADS, 1), F32)], axis=0),
+        (4 * HEADS, STATE),
     ).astype(BF)
     log_ref[...] = log_s[...] + cum
     log_s[...] = log_s[...] + last
-    spread = spread_ref[...]
-    weight = jnp.dot(
-        scales, jnp.concatenate([spread, jnp.zeros_like(spread)], axis=0), preferred_element_type=F32
-    )
+    weight = jnp.dot(scales, spread_s[...], preferred_element_type=F32)
     weighted = (xin_ref[...].astype(F32) * weight).astype(BF)
     gain = lax.dot_general(
-        weighted, pair_ref[...], (((0,), (0,)), ((), ())), preferred_element_type=F32
-    )
-    decay = jnp.dot(rows_ref[...], decays, preferred_element_type=F32)
+        weighted, pair_ref[:, :STATE], (((0,), (0,)), ((), ())), preferred_element_type=F32
+    )
+    decay = jnp.dot(rows_s[...], decays, preferred_element_type=F32)
     state = state_s[...]
-    start_ref[...] = state.astype(BF)
+    read_ref[...] = lax.dot_general(
+        pair_ref[:, STATE:], state.astype(BF), (((1,), (1,)), ((), ())), preferred_element_type=F32
+    ).astype(BF)
     state = state * decay + gain
     state_s[...] = state
 
@@ -187,49 +194,54 @@
         give_ref[CHAN // 2 :, :] = jnp.concatenate([rows, jnp.zeros_like(rows)], axis=1)
 
 
-def spread_rows():
-    spread = np.zeros((2 * HEADS, CHAN), np.float32)
-    for h in range(HEADS):
-        for part in range(2):
-            spread[part * HEADS + h, h * PSIZE : (h + 1) * PSIZE] = 1
-    return spread
+def spread_heads():
+    row = lax.broadcasted_iota(jnp.int32, (4 * HEADS, CHAN), 0)
+    channel = lax.broadcasted_iota(jnp.int32, (4 * HEADS, CHAN), 1)
+    hit = (row < 2 * HEADS) & (row % HEADS == channel // PSIZE)
+    return jnp.where(hit, 1.0, 0.0).astype(BF)
+
+
+def spread_columns():
+    row = lax.broadcasted_iota(jnp.int32, (4 * HEADS, HEADS * SPAN), 0)
+    column = lax.broadcasted_iota(jnp.int32, (4 * HEADS, HEADS * SPAN), 1)
+    hit = (row < 3 * HEADS) & (row % HEADS == column // SPAN)
+    return jnp.where(hit, 1.0, 0.0).astype(BF)
 
 
 def own_states(core, xin, pair, steps, drop):
-    spread = spread_rows()
     return pl.pallas_call(
         states_kernel,
         grid=(TOK // SPAN,),
         in_specs=[
             pl.BlockSpec(memory_space=pltpu.SMEM),
             pl.BlockSpec((SPAN, CHAN), lambda s: (s, 0)),
-            pl.BlockSpec((SPAN, STATE), lambda s: (s, 0)),
+            pl.BlockSpec((SPAN, 2 * STATE), lambda s: (s, 0)),
             pl.BlockSpec((HEADS, SPAN), lambda s: (0, s)),
             pl.BlockSpec((HEADS, SPAN), lambda s: (0, s)),
-            pl.BlockSpec((2 * HEADS, CHAN), lambda s: (0, 0)),
-            pl.BlockSpec((CHAN, 2 * HEADS), lambda s: (0, 0)),
         ],
         out_specs=[
             pl.BlockSpec((HEADS, SPAN), lambda s: (0, s)),
             pl.BlockSpec((HEADS, SPAN), lambda s: (0, s)),
-            pl.BlockSpec((CHAN, STATE), lambda s: (s, 0)),
+            pl.BlockSpec((SPAN, CHAN), lambda s: (s, 0)),
             pl.BlockSpec((CHAN // 2, STATE), lambda s: (0, 0)),
             pl.BlockSpec((CHAN // 2 + 16, STATE), lambda s: (0, 0)),
         ],
         out_shape=[
             jax.ShapeDtypeStruct((HEADS, TOK), F32),
             jax.ShapeDtypeStruct((HEADS, TOK), F32),
-            jax.ShapeDtypeStruct((TOK // SPAN * CHAN, STATE), BF),
+            jax.ShapeDtypeStruct((TOK, CHAN), BF),
             jax.ShapeDtypeStruct((CHAN // 2, STATE), BF),
             jax.ShapeDtypeStruct((CHAN // 2 + 16, STATE), BF),
         ],
         scratch_shapes=[
             pltpu.VMEM((HEADS, SPAN), F32),
             pltpu.VMEM((CHAN, STATE), F32),
+            pltpu.VMEM((4 * HEADS, CHAN), BF),
+            pltpu.VMEM((CHAN, 4 * HEADS), BF),
         ],
         compiler_params=pltpu.CompilerParams(vmem_limit_bytes=VMEM_LIMIT),
         cost_estimate=pl.CostEstimate(flops=1 << 20, bytes_accessed=1 << 16, transcendentals=0),
-    )(core, xin, pair, steps, drop, jnp.asarray(spread, BF), jnp.asarray(spread.T, BF))
+    )(core, xin, pair, steps, drop)
 
 
 def inside_kernel(
@@ -237,17 +249,23 @@
     pair_ref,
     cum_ref,
     steps_ref,
-    start_ref,
+    read_ref,
     skip_ref,
-    spread_ref,
-    column_ref,
     y_ref,
     g_s,
     ci_s,
     ex_s,
+    log_s,
+    spread_s,
+    column_s,
 ):
     block = pl.program_id(1)
     cmat = pair_ref[:, STATE:]
+
+    @pl.when((block == 0) & (pl.program_id(0) == 0))
+    def _():
+        spread_s[...] = spread_heads()
+        column_s[...] = spread_columns()
 
     @pl.when(block == 0)
     def _():
@@ -258,32 +276,26 @@
         at_j = lax.broadcasted_iota(jnp.int32, (SPAN, SPAN), 1)
         g_s[...] = jnp.where(at_j <= at_i, product, 0.0)
         cum = cum_ref[...]
+        log_s[...] = jnp.log(steps_ref[...])
         ci_s[...] = jnp.concatenate(three_parts(cum) + [jnp.zeros_like(cum)], axis=0).T.astype(BF)
         ex_s[...] = jnp.concatenate(
             two_parts(jnp.exp(cum)) + [jnp.zeros((2 * HEADS, SPAN), F32)], axis=0
         ).T.astype(BF)
 
     xf = xin_ref[...].astype(F32)
-    spread = spread_ref[...]
-    grown = jnp.dot(
-        ex_s[...], jnp.concatenate([spread, jnp.zeros_like(spread)], axis=0), preferred_element_type=F32
-    )
-    rows_i = jnp.dot(ci_s[...], column_ref[...], preferred_element_type=F32)
-    read = lax.dot_general(
-        cmat, start_ref[...], (((1,), (1,)), ((), ())), preferred_element_type=F32
-    )
-    base = read * grown + skip_ref[...] * xf
+    grown = jnp.dot(ex_s[...], spread_s[...], preferred_element_type=F32)
+    rows_i = jnp.dot(ci_s[...], column_s[...], preferred_element_type=F32)
+    base = read_ref[...].astype(F32) * grown + skip_ref[...] * xf
     cum_rows = cum_ref[pl.ds(pl.multiple_of(block * HB, HB), HB), :]
-    step_rows = steps_ref[pl.ds(pl.multiple_of(block * HB, HB), HB), :]
+    log_rows = log_s[pl.ds(pl.multiple_of(block * HB, HB), HB), :]
+    cum_rows = cum_rows - log_rows
     masked = g_s[...]
     lane = lax.broadcasted_iota(jnp.int32, (SPAN, 2 * PSIZE), 1)
     for pair in range(HB // 2):
         mixes = []
         for h in (2 * pair, 2 * pair + 1):
             gap = rows_i[:, h * SPAN : (h + 1) * SPAN] - cum_rows[h : h + 1]
-            mixes.append(
-                (masked * jnp.exp(jnp.minimum(gap, 0.0)) * step_rows[h : h + 1]).astype(BF)
-            )
+            mixes.append((masked * jnp.exp(jnp.minimum(gap, log_rows[h : h + 1]))).astype(BF))
         two = xf[:, pair * 128 : (pair + 1) * 128]
         left = jnp.where(lane < PSIZE, two, 0.0).astype(BF)
         right = jnp.where(lane < PSIZE, 0.0, two).astype(BF)
@@ -297,11 +309,7 @@
         ).astype(BF)
 
 
-def inside_blocks(xin, pair, cum, steps, starts, skip):
-    column = np.zeros((4 * HEADS, HEADS * SPAN), np.float32)
-    for h in range(HEADS):
-        for part in range(3):
-            column[part * HEADS + h, h * SPAN : (h + 1) * SPAN] = 1
+def inside_blocks(xin, pair, cum, steps, read, skip):
     blocks = HEADS // HB
     return pl.pallas_call(
         inside_kernel,
@@ -311,10 +319,8 @@
             pl.BlockSpec((SPAN, 2 * STATE), lambda s, b: (s, 0)),
             pl.BlockSpec((HEADS, SPAN), lambda s, b: (0, s)),
             pl.BlockSpec((HEADS, SPAN), lambda s, b: (0, s)),
-            pl.BlockSpec((HBC, STATE), lambda s, b: (s * blocks + b, 0)),
+            pl.BlockSpec((SPAN, HBC), lambda s, b: (s, b)),
             pl.BlockSpec((1, HBC), lambda s, b: (0, b)),
-            pl.BlockSpec((2 * HEADS, HBC), lambda s, b: (0, b)),
-            pl.BlockSpec((4 * HEADS, HB * SPAN), lambda s, b: (0, b)),
         ],
         out_specs=pl.BlockSpec((SPAN, HBC), lambda s, b: (s, b)),
         out_shape=jax.ShapeDtypeStruct((TOK, CHAN), BF),
@@ -322,10 +328,13 @@
             pltpu.VMEM((SPAN, SPAN), F32),
             pltpu.VMEM((SPAN, 4 * HEADS), BF),
             pltpu.VMEM((SPAN, 4 * HEADS), BF),
+            pltpu.VMEM((HEADS, SPAN), F32),
+            pltpu.VMEM((4 * HEADS, CHAN), BF),
+            pltpu.VMEM((4 * HEADS, HEADS * SPAN), BF),
         ],
         compiler_params=pltpu.CompilerParams(vmem_limit_bytes=VMEM_LIMIT),
         cost_estimate=pl.CostEstimate(flops=1 << 34, bytes_accessed=1 << 16, transcendentals=0),
-    )(xin, pair, cum, steps, starts, skip, jnp.asarray(spread_rows(), BF), jnp.asarray(column, BF))
+    )(xin, pair, cum, steps, read, skip)
 
 
 CHIPS = NX * NZ
@@ -366,15 +375,17 @@
 
 
 def finish_kernel(
-    core_ref, y_ref, c_ref, log_ref, in_ref, other_ref, gate_ref, gain_ref, spread_ref, out_ref
+    core_ref, y_ref, c_ref, log_ref, in_ref, other_ref, gate_ref, gain_ref, out_ref, spread_s
 ):
     grown = jnp.concatenate(
-        two_parts(jnp.exp(log_ref[...])) + [jnp.zeros((2 * HEADS, SPAN), F32)], axis=0
+        two_parts(jnp.exp(log_ref[...])) + [jnp.zeros((2 * HEADS, END_ROWS), F32)], axis=0
     ).T.astype(BF)
-    spread = spread_ref[...]
-    scale = jnp.dot(
-        grown, jnp.concatenate([spread, jnp.zeros_like(spread)], axis=0), preferred_element_type=F32
-    )
+
+    @pl.when(pl.program_id(0) == 0)
+    def _():
+        spread_s[...] = spread_heads()
+
+    scale = jnp.dot(grown, spread_s[...], preferred_element_type=F32)
     contract = (((1,), (1,)), ((), ()))
     kept = lax.dot_general(c_ref[...], in_ref[...], contract, preferred_element_type=F32)
     given = lax.dot_general(c_ref[...], other_ref[...], contract, preferred_element_type=F32)
@@ -392,23 +403,23 @@
 def finish(core, y, pair, logs, entering, other, gate, gain):
     return pl.pallas_call(
         finish_kernel,
-        grid=(TOK // SPAN,),
+        grid=(TOK // END_ROWS,),
         in_specs=[
             pl.BlockSpec(memory_space=pltpu.SMEM),
-            pl.BlockSpec((SPAN, CHAN), lambda s: (s, 0)),
-            pl.BlockSpec((SPAN, STATE), lambda s: (s, 1)),
-            pl.BlockSpec((HEADS, SPAN), lambda s: (0, s)),
+            pl.BlockSpec((END_ROWS, CHAN), lambda s: (s, 0)),
+            pl.BlockSpec((END_ROWS, STATE), lambda s: (s, 1)),
+            pl.BlockSpec((HEADS, END_ROWS), lambda s: (0, s)),
             pl.BlockSpec((CHAN // 2, STATE), lambda s: (0, 0)),
             pl.BlockSpec((CHAN // 2, STATE), lambda s: (0, 0)),
-            pl.BlockSpec((SPAN, CHAN), lambda s: (s, 0)),
+            pl.BlockSpec((END_ROWS, CHAN), lambda s: (s, 0)),
             pl.BlockSpec((1, CHAN), lambda s: (0, 0)),
-            pl.BlockSpec((2 * HEADS, CHAN), lambda s: (0, 0)),
-        ],
-        out_specs=pl.BlockSpec((SPAN, CHAN), lambda s: (s, 0)),
+        ],
+        out_specs=pl.BlockSpec((END_ROWS, CHAN), lambda s: (s, 0)),
         out_shape=jax.ShapeDtypeStruct((TOK, CHAN), BF),
+        scratch_shapes=[pltpu.VMEM((4 * HEADS, CHAN), BF)],
         compiler_params=pltpu.CompilerParams(vmem_limit_bytes=VMEM_LIMIT),
         cost_estimate=pl.CostEstimate(flops=1 << 20, bytes_accessed=1 << 16, transcendentals=0),
-    )(core, y, pair, logs, entering, other, gate, gain, jnp.asarray(spread_rows(), BF))
+    )(core, y, pair, logs, entering, other, gate, gain)
 
 
 QHEADS = 4
@@ -638,7 +649,7 @@
             pltpu.SemaphoreType.DMA((2, QHEADS)),
             pltpu.SemaphoreType.DMA((2, QHEADS)),
         ],
-        compiler_params=pltpu.CompilerParams(vmem_limit_bytes=VMEM_LIMIT),
+        compiler_params=pltpu.CompilerParams(vmem_limit_bytes=ATTEND_LIMIT),
         cost_estimate=pl.CostEstimate(
             flops=1 << 35 if fresh and not own else 1 << 20, bytes_accessed=1 << 16, transcendentals=0
         ),
@@ -698,24 +709,25 @@
         return jnp.stack([count, jnp.where(z == NZ - 1, 2, 3), c]).astype(jnp.int32)
 
     bc = bc_in.reshape(TOK, 2 * STATE)
-    ends = jnp.concatenate([ssm_in[TOK - 16 :], bc[TOK - 16 :]], axis=1)
-    tail = lax.ppermute(ends, "ctx", [(i, i + 1) for i in range(31)])
     partial = lax.dot_general(
         dt_weight, hidden, (((0,), (1,)), ((), ())), preferred_element_type=F32
     )
-    partial, tail, keys, query = lax.optimization_barrier((partial, tail, key_heads, query_heads))
+    partial, keys, ends_x, ends_bc = lax.optimization_barrier(
+        (partial, key_heads, ssm_in[TOK - 16 :], bc[TOK - 16 :])
+    )
+    ends = jnp.concatenate([ends_x, ends_bc], axis=1)
+    tail = lax.ppermute(ends, "ctx", [(i, i + 1) for i in range(31)])
     parts = lax.all_to_all(partial.reshape(8, HEADS, TOK), "head", 0, 0, tiled=True)
     xin, pair = convolved(ssm_in, tail, bc, conv_x, conv_bc.reshape(4, 2 * STATE))
     rows = jnp.concatenate([keys, value_heads], axis=1)
-    up, down = along_z(rows, 1), along_z(rows, -1)
-    visitor = send(query, lambda x, z, c: (x - 1, z, c) if x >= 2 else None)
+    up, down, two = along_z(rows, 1), along_z(rows, -1), along_z(rows, 2)
     parts, xin, pair = lax.optimization_barrier((parts, xin, pair))
     steps = jax.nn.softplus(jnp.sum(parts, axis=0) + dt_bias[:, None])
     drop = -steps * decay_rate[:, None]
     total = jnp.sum(drop, axis=1)
-    cum, logs, starts, keep, give = own_states(core, xin, pair, steps, drop)
-
-    keep, give, up, down, visitor = lax.optimization_barrier((keep, give, up, down, visitor))
+    cum, logs, read, keep, give = own_states(core, xin, pair, steps, drop)
+
+    keep, give, up, down = lax.optimization_barrier((keep, give, up, down))
     other = swap_core(give)
     partner = jnp.sum(other[CHAN // 2, : 3 * HEADS].astype(F32).reshape(3, HEADS), axis=0)
     other = other[: CHAN // 2]
@@ -729,14 +741,12 @@
         late + jnp.exp(log_second)[:, None, None] * early, log_first + log_second
     )
     collected = exchanged(both)
-    both, xin, rows, up, down, visitor = lax.optimization_barrier(
-        (both, xin, rows, up, down, visitor)
-    )
-    middle = TOK // 2
-    two = [along_z(up[:middle], 1), along_z(down[middle:], -1)]
-    visitor = send(visitor, lambda x, z, c: (x - 1, z, c) if x in (1, 2) else None)
-    y = inside_blocks(xin, pair, cum, steps, starts, jnp.repeat(skip_gain, PSIZE)[None])
-    plane = jnp.stack([rows, up, down, jnp.concatenate(two, axis=0)])
+    both, xin, rows, up, down, two, query = lax.optimization_barrier(
+        (both, xin, rows, up, down, two, query_heads)
+    )
+    visitor = send(query, lambda x, z, c: (x - 2, z, c) if x >= 2 else None)
+    y = inside_blocks(xin, pair, cum, steps, read, jnp.repeat(skip_gain, PSIZE)[None])
+    plane = jnp.stack([rows, up, down, two])
     plane_pair = swap_core(plane)
     left = along_x(plane, 1)
     right = send(plane, lambda x, z, c: (NX - 1, z, c) if x == 0 else None)

time: 157 us -> 151 us (0.962); the launches traced: 154 us -> 151 us
  Pallas kernels: 74.9 us -> 67 us
  local copies, waits for them, and re-layouts: 8.81 us -> 11.5 us
  starting transfers between devices: 56.9 us -> 59.2 us
    pallas_call x3, Pallas kernels: 40.2 us -> 33.6 us  [attend(): pl.pallas_call(functools.partial(attend_kernel, planes=planes, own=own, f...]
    unnamed x38 -> x52, local copies, waits for them, and re-layouts: 6.06 us -> 9.64 us
    all_to_all x2, starting transfers between devices: 20.6 us -> 23.7 us  [exchanged(): lax.all_to_all(value, 'ctx', 0, 0, tiled=True, axis_index_groups=SAME_CORE)]
    ppermute x14 -> x12, starting transfers between devices: 25.5 us -> 24.1 us  [send(): return lax.ppermute(value, 'ctx', pairs_of(move))]
  transfers between devices with their start and end apart: 18 -> 16, of which waited for: 2 -> 1; matrix products, arithmetic and copies ran while one was open for 6% -> 6% of each run, Pallas kernels for 44% -> 40%
where the time goes in v4:
time: 151 us
  Pallas kernels  67 us (44%)
  starting transfers between devices  59.2 us (39%)
  local copies, waits for them, and re-layouts  11.5 us (8%)
  other arithmetic  7.87 us (5%)
  matrix products  2.31 us (2%)
  waiting for transfers between devices  1.69 us (1%)
    pallas_call x3, Pallas kernels, attend(): pl.pallas_call(functools.partial(attend_kernel, planes=planes, own=own, f...  33.6 us
    ppermute x12, starting transfers between devices, send(): return lax.ppermute(value, 'ctx', pairs_of(move))  24.1 us
    all_to_all x2, starting transfers between devices, exchanged(): lax.all_to_all(value, 'ctx', 0, 0, tiled=True, axis_index_groups=SAME_CORE)  23.7 us
    unnamed x52, local copies, waits for them, and re-layouts  9.64 us
    pallas_call x1, Pallas kernels, own_states(): pl.pallas_call(states_kernel, grid=(TOK // SPAN,), in_specs=[pl.BlockSpec...  9.12 us
    pallas_call x1, Pallas kernels, inside_blocks(): pl.pallas_call(inside_kernel, grid=(TOK // SPAN, blocks), in_specs=[pl.Bl...  7.23 us
    pallas_call x1, Pallas kernels, finish(): pl.pallas_call(finish_kernel, grid=(TOK // END_ROWS,), in_specs=[pl.Block...  6.27 us
    pallas_call x1, Pallas kernels, convolved(): pl.pallas_call(conv_kernel, grid=(TOK // CONV_ROWS,), in_specs=[pl.BlockS...  6.07 us
  transfers between devices with their start and end apart: 16, of which 1 were waited for; matrix products, arithmetic and copies ran while one was open for 6% of the time, Pallas kernels for 40%

profile of v4, /device:TPU:35, one launch (start us, length us, event | category | flops | bytes accessed | tf_op | source)
XLA Modules:
  0.0 150.5 jit_solution(3402681675244694072)
XLA Ops:
  0.6 0.0 copy-start
  0.6 0.0 slice-start
  0.7 0.8 slice_bitcast_fusion
  1.5 0.4 copy-done
  1.9 2.3 %fusion.10 = f32[256,512]{1,0:T(8,128)} fusion(bf16[1024,256]{1,0:T(8,128)(2,1)} %param.15, bf16[512,1024]{1,0:T(8,128)(2,1)S(1)} %copy-done), kind=kOutput, calls=%fused_computation.41 | convolution fusion | flops 268435456 | bytes 2097152 | tf_op jit(solution)/shard_map/dot_general | solution.py:712
  4.2 5.4 %all-to-all-start = ((f32[8,32,512]{2,1,0:T(8,128)}), f32[8,32,512]{2,1,0:T(8,128)S(1)}, u32[]{:S(2)}, u32[]{:S(2)}) async-start(f32[8,32,512]{2,1,0:T(8,128)} %bitcast.2), calls=%async_computation | async-start | bytes 1048576 | tf_op jit(solution)/shard_map/all_to_all | solution.py:720
  9.6 6.0 %collective-permute-start = (bf16[16,2560]{1,0:T(8,128)(2,1)S(1)}, bf16[16,2560]{1,0:T(8,128)(2,1)S(1)}, u32[]{:S(2)}, u32[]{:S(2)}) collective-permute-start(bf16[16,2560]{1,0:T(8,128)(2,1)S(1)} %pad_maximum_fusion.2), channel_id=1, source_target_pairs={{0,8},{8,16},{16,24},{24,32},{32,40},{40,48},{48,56},{56,64},{64,7... | collective-permute-start | bytes 245768 | tf_op jit(solution)/shard_map/ppermute | solution.py:719
  15.7 1.6 %collective-permute-start.2 = (bf16[512,256]{1,0:T(8,128)(2,1)S(1)}, bf16[512,256]{1,0:T(8,128)(2,1)S(1)}, u32[]{:S(2)}, u32[]{:S(2)}) collective-permute-start(bf16[512,256]{1,0:T(8,128)(2,1)S(1)} %constant_dynamic-update-slice_fusion), channel_id=1, source_target_pairs={{0,48},{8,56},{16,0},{24,8},{32,16},{40,24},{48,32},{56,40},{64,11... | collective-permute-start | bytes 786440 | tf_op jit(solution)/shard_map/ppermute | solution.py:41
  17.3 1.9 %collective-permute-start.1 = (bf16[512,256]{1,0:T(8,128)(2,1)S(1)}, bf16[512,256]{1,0:T(8,128)(2,1)S(1)}, u32[]{:S(2)}, u32[]{:S(2)}) collective-permute-start(bf16[512,256]{1,0:T(8,128)(2,1)S(1)} %constant_dynamic-update-slice_fusion), channel_id=1, source_target_pairs={{0,16},{8,24},{16,32},{24,40},{32,48},{40,56},{48,0},{56,8},{64,80... | collective-permute-start | bytes 786440 | tf_op jit(solution)/shard_map/ppermute | solution.py:41
  19.2 0.6 copy.18
  19.8 0.0 collective-permute-done.xtail_ref.ptail_ref
  19.8 0.6 copy-done.14
  20.4 6.1 %shard_map.149 = (bf16[512,2048]{1,0:T(8,128)(2,1)}, bf16[512,512]{1,0:T(8,128)(2,1)}) custom-call(bf16[512,2048]{1,0:T(8,128)(2,1)} %before_ref.1, bf16[512,2048]{1,0:T(8,128)(2,1)} %before_ref.1, bf16[16,2560]{1,0:T(8,128)(2,1)} %copy-done.14, bf16[512,512]{1,0:T(8,128)(2,1)} %bitcast.43, bf16[512,512]{1,0:T(8,128)(2,1)} %bitcast.44, ...), custom_call_target="tpu_custom_call" | custom-call | flops 1048576 | bytes 65536 | tf_op jit(solution)/shard_map/pallas_call | solution.py:102
  26.5 0.0 all-to-all-done
  26.6 0.9 fusion.9
  27.4 9.1 %shard_map.150 = (f32[32,512]{1,0:T(8,128)}, f32[32,512]{1,0:T(8,128)}, bf16[512,2048]{1,0:T(8,128)(2,1)}, bf16[1024,256]{1,0:T(8,128)(2,1)}, bf16[1040,256]{1,0:T(8,128)(2,1)}) custom-call(s32[1]{0:T(128)} %bitcast.core_ref, bf16[512,2048]{1,0:T(8,128)(2,1)} %get-tuple-element.59.xin_ref, bf16[512,512]{1,0:T(8,128)(2,1)} %get-tuple-element.50.pair_ref.c_ref, ...), custom_call_target="tpu_custom_call" | custom-call | flops 1048576 | bytes 65536 | tf_op jit(solution)/shard_map/pallas_call | solution.py:212
  36.6 0.1 collective-permute-start.3
  36.7 9.7 %collective-permute-start.4 = (bf16[512,256]{1,0:T(8,128)(2,1)S(1)}, bf16[512,256]{1,0:T(8,128)(2,1)}, u32[]{:S(2)}, u32[]{:S(2)}) collective-permute-start(bf16[512,256]{1,0:T(8,128)(2,1)S(1)} %constant_dynamic-update-slice_fusion), channel_id=1, source_target_pairs={{0,32},{8,40},{16,48},{24,56},{32,0},{40,8},{48,16},{56,24},{64,96... | collective-permute-start | bytes 786440 | tf_op jit(solution)/shard_map/ppermute | solution.py:41
  46.4 0.1 broadcast_in_dim.46
  46.4 0.7 broadcast_in_dim_reshape.3.skip_ref
  47.1 0.1 add_add_fusion.flag_ref
  47.2 0.1 add_add_fusion.1
  47.3 0.1 reshape.90
  47.4 0.1 select_n.112
  47.5 0.1 select_n.108
  47.6 1.2 broadcast_select_fusion.1
  48.8 0.2 fusion.1
  49.1 0.1 select_convert_fusion
  49.2 0.0 copy-start.2
  49.2 0.9 pad_maximum_fusion.1
  50.1 6.9 %all-to-all-start.1 = ((bf16[16,80,256]{2,1,0:T(8,128)(2,1)}), bf16[16,80,256]{2,1,0:T(8,128)(2,1)}, u32[]{:S(2)}, u32[]{:S(2)}) async-start(bf16[16,80,256]{2,1,0:T(8,128)(2,1)} %pad_maximum_fusion.1), calls=%async_computation.1 | async-start | bytes 1310720 | tf_op jit(solution)/shard_map/all_to_all | solution.py:374
  57.0 1.7 %collective-permute-done.4 = bf16[512,256]{1,0:T(8,128)(2,1)} collective-permute-done((bf16[512,256]{1,0:T(8,128)(2,1)S(1)}, bf16[512,256]{1,0:T(8,128)(2,1)}, u32[]{:S(2)}, u32[]{:S(2)}) %collective-permute-start.4) | collective-permute-done | bytes 262176 | tf_op jit(solution)/shard_map/ppermute | solution.py:41
  58.7 1.1 pad_maximum_fusion.refs_0_
  59.7 1.7 %collective-permute-start.8 = (bf16[4,512,256]{2,1,0:T(8,128)(2,1)S(1)}, bf16[4,512,256]{2,1,0:T(8,128)(2,1)}, u32[]{:S(2)}, u32[]{:S(2)}) collective-permute-start(bf16[4,512,256]{2,1,0:T(8,128)(2,1)S(1)} %pad_maximum_fusion.refs_0_), channel_id=1, source_target_pairs={{0,192},{8,200},{16,208},{24,216},{32,224},{40,232},{48,240},{56,2... | collective-permute-start | bytes 3145736 | tf_op jit(solution)/shard_map/ppermute | solution.py:41
  61.4 2.8 %collective-permute-start.7 = (bf16[4,512,256]{2,1,0:T(8,128)(2,1)S(1)}, bf16[4,512,256]{2,1,0:T(8,128)(2,1)}, u32[]{:S(2)}, u32[]{:S(2)}) collective-permute-start(bf16[4,512,256]{2,1,0:T(8,128)(2,1)S(1)} %pad_maximum_fusion.refs_0_), channel_id=1, source_target_pairs={{0,64},{8,72},{16,80},{24,88},{32,96},{40,104},{48,112},{56,120},{... | collective-permute-start | bytes 3145736 | tf_op jit(solution)/shard_map/ppermute | solution.py:41
  64.2 1.1 collective-permute-start.5
  65.4 1.3 collective-permute-start.6
  66.7 7.2 %shard_map.151.y_ref = bf16[512,2048]{1,0:T(8,128)(2,1)} custom-call(bf16[512,2048]{1,0:T(8,128)(2,1)} %get-tuple-element.59.xin_ref, bf16[512,512]{1,0:T(8,128)(2,1)} %get-tuple-element.50.pair_ref.c_ref, f32[32,512]{1,0:T(8,128)} %get-tuple-element.60.cum_ref, f32[32,512]{1,0:T(8,128)} %get-tuple-element.90.steps_ref, ...), custom_call_target="tpu_custom_call" | custom-call | flops 17179869184 | bytes 65536 | tf_op jit(solution)/shard_map/pallas_call | solution.py:314
  73.9 6.1 %shard_map.152 = (f32[4,512,256]{2,1,0:T(8,128)S(1)}, f32[4,512,128]{2,1,0:T(8,128)S(1)}) custom-call(s32[3]{0:T(128)S(1)} %add_add_fusion.flag_ref, bf16[512,512]{1,0:T(8,128)(2,1)S(1)} %copy-done.2, bf16[4,512,256]{2,1,0:T(8,128)(2,1)S(1)} %pad_maximum_fusion.refs_0_, bf16[4,512,256]{2,1,0:T(8,128)(2,1)S(1)} %collective-permute-done.5.refs_1_), custom_call_target="tpu_custom_call" | custom-call | flops 1048576 | bytes 65536 | tf_op jit(solution)/shard_map/pallas_call | solution.py:632
  80.0 0.0 copy-start.3
  80.0 1.3 copy-done.3
  81.3 1.0 copy-done.5
  82.3 1.0 copy-done.7
  83.3 0.0 all-to-all-done.1.from_ref
  83.3 2.0 %shard_map.153 = bf16[16,64,256]{2,1,0:T(8,128)(2,1)} custom-call(bf16[16,80,256]{2,1,0:T(8,128)(2,1)} %all-to-all-done.1.from_ref), custom_call_target="tpu_custom_call" | custom-call | flops 1048576 | bytes 65536 | tf_op jit(solution)/shard_map/pallas_call | solution.py:355
  85.3 16.8 %all-to-all-start.2 = ((bf16[16,64,256]{2,1,0:T(8,128)(2,1)}), bf16[16,64,256]{2,1,0:T(8,128)(2,1)}, u32[]{:S(2)}, u32[]{:S(2)}) async-start(bf16[16,64,256]{2,1,0:T(8,128)(2,1)} %shard_map.153), calls=%async_computation.2 | async-start | bytes 1048576 | tf_op jit(solution)/shard_map/all_to_all | solution.py:374
  102.1 0.8 copy-done.9
  102.9 0.9 collective-permute-start.9
  103.9 0.1 collective-permute-start.10
  104.0 1.2 copy-done.8
  105.2 1.0 copy-done.10
  106.2 13.3 %shard_map.154 = bf16[512,640]{1,0:T(8,128)(2,1)S(1)} custom-call(s32[3]{0:T(128)S(1)} %get-tuple-element.72.flag_ref, bf16[512,512]{1,0:T(8,128)(2,1)S(1)} %copy-done.10, bf16[4,512,256]{2,1,0:T(8,128)(2,1)S(1)} %pad_maximum_fusion.refs_0_, bf16[4,512,256]{2,1,0:T(8,128)(2,1)S(1)} %copy-done.8), custom_call_target="tpu_custom_call" | custom-call | flops 34359738368 | bytes 65536 | tf_op jit(solution)/shard_map/pallas_call | solution.py:632
  119.5 2.3 %collective-permute-start.12 = (bf16[512,640]{1,0:T(8,128)(2,1)S(1)}, bf16[512,640]{1,0:T(8,128)(2,1)}, u32[]{:S(2)}, u32[]{:S(2)}) collective-permute-start(bf16[512,640]{1,0:T(8,128)(2,1)S(1)} %shard_map.154), channel_id=1, source_target_pairs={{0,128},{8,136},{16,144},{24,152},{32,160},{40,168},{48,176},{56,1... | collective-permute-start | bytes 1966088 | tf_op jit(solution)/shard_map/ppermute | solution.py:41
  121.8 0.0 collective-permute-done.9.refs_1_
  121.8 0.0 collective-permute-done.10.refs_3_
  121.8 14.2 %shard_map.155.mine_ref = bf16[512,640]{1,0:T(8,128)(2,1)S(1)} custom-call(s32[3]{0:T(128)S(1)} %get-tuple-element.75.flag_ref, bf16[512,512]{1,0:T(8,128)(2,1)S(1)} %copy-done.2, bf16[4,512,256]{2,1,0:T(8,128)(2,1)} %collective-permute-done.7.refs_0_, bf16[4,512,256]{2,1,0:T(8,128)(2,1)S(1)} %collective-permute-done.9.refs_1_, ...), custom_call_target="tpu_custom_call" | custom-call | flops 1048576 | bytes 65536 | tf_op jit(solution)/shard_map/pallas_call | solution.py:632
  136.0 0.0 copy-start.1
  136.1 0.8 copy-done.1
  136.9 2.6 %fusion.3 = (bf16[16,64,256]{2,1,0:T(8,128)(2,1)S(1)}, bf16[16,64,256]{2,1,0:T(8,128)(2,1)}) fusion(bf16[16,64,256]{2,1,0:T(8,128)(2,1)} %all-to-all-done.2, bf16[16,64,256]{2,1,0:T(8,128)(2,1)S(1)} %bitcast.42, f32[16]{0:T(128)S(1)} %get-tuple-element.95, pred[]{:T(512)S(6)} %eq.44), kind=kLoop, calls=%fused_computation.6 | loop fusion | flops 1835008 | bytes 2097217 | tf_op jit(solution)/shard_map/jit(_where)/select_n | solution.py:770
  139.5 0.7 collective-permute-start.11
  140.2 0.7 add_add_fusion.3.flag_ref
  140.8 2.6 %shard_map.156 = bf16[512,512]{1,0:T(8,128)(2,1)} custom-call(s32[3]{0:T(128)} %add_add_fusion.3.flag_ref, bf16[512,640]{1,0:T(8,128)(2,1)} %copy-done.1, bf16[512,640]{1,0:T(8,128)(2,1)} %collective-permute-done.12.other_ref), custom_call_target="tpu_custom_call" | custom-call | flops 1048576 | bytes 65536 | tf_op jit(solution)/shard_map/pallas_call | solution.py:677
  143.5 0.8 copy-done.13
  144.3 6.3 %shard_map.157 = bf16[512,2048]{1,0:T(8,128)(2,1)} custom-call(s32[1]{0:T(128)} %bitcast.core_ref, bf16[512,2048]{1,0:T(8,128)(2,1)} %shard_map.151.y_ref, bf16[512,512]{1,0:T(8,128)(2,1)} %get-tuple-element.50.pair_ref.c_ref, f32[32,512]{1,0:T(8,128)} %get-tuple-element.70.log_ref, bf16[1024,256]{1,0:T(8,128)(2,1)} %bitcast.46, ...), custom_call_target="tpu_custom_call" | custom-call | flops 1048576 | bytes 65536 | tf_op jit(solution)/shard_map/pallas_call | solution.py:404
  (58 shorter events, 0.3 us)
Async XLA Ops:
  0.6 1.2 copy-start
  0.6 8.9 %slice-start = ((bf16[512,2048]{1,0:T(8,128)(2,1)}), bf16[16,2048]{1,0:T(8,128)(2,1)S(1)}, s32[]{:S(2)}) async-start(bf16[512,2048]{1,0:T(8,128)(2,1)} %before_ref.1), calls=%async_computation.3 | async-start | bytes 131072 | tf_op jit(solution)/shard_map/slice | solution.py:716
  0.7 14.9 %copy-start.19 = (bf16[512,128]{1,0:T(8,128)(2,1)S(1)}, bf16[512,128]{1,0:T(8,128)(2,1)}, u32[]{:S(2)}) copy-start(bf16[512,128]{1,0:T(8,128)(2,1)} %param.26) | copy-start | bytes 393220
  0.7 15.0 %copy-start.20 = (bf16[512,128]{1,0:T(8,128)(2,1)S(1)}, bf16[512,128]{1,0:T(8,128)(2,1)}, u32[]{:S(2)}) copy-start(bf16[512,128]{1,0:T(8,128)(2,1)} %param.27) | copy-start | bytes 393220
  0.7 18.5 %copy-start.21 = (f32[4,1,512]{2,1,0:T(1,128)S(1)}, f32[4,1,512]{2,1,0:T(1,128)}, u32[]{:S(2)}) copy-start(f32[4,1,512]{2,1,0:T(1,128)} %param.22) | copy-start | bytes 24580
  4.2 22.3 %all-to-all-start = ((f32[8,32,512]{2,1,0:T(8,128)}), f32[8,32,512]{2,1,0:T(8,128)S(1)}, u32[]{:S(2)}, u32[]{:S(2)}) async-start(f32[8,32,512]{2,1,0:T(8,128)} %bitcast.2), calls=%async_computation | async-start | bytes 1048576 | tf_op jit(solution)/shard_map/all_to_all | solution.py:720
  9.6 10.2 %collective-permute-start = (bf16[16,2560]{1,0:T(8,128)(2,1)S(1)}, bf16[16,2560]{1,0:T(8,128)(2,1)S(1)}, u32[]{:S(2)}, u32[]{:S(2)}) collective-permute-start(bf16[16,2560]{1,0:T(8,128)(2,1)S(1)} %pad_maximum_fusion.2), channel_id=1, source_target_pairs={{0,8},{8,16},{16,24},{24,32},{32,40},{40,48},{48,56},{56,64},{64,7... | collective-permute-start | bytes 245768 | tf_op jit(solution)/shard_map/ppermute | solution.py:719
  15.7 20.9 %collective-permute-start.2 = (bf16[512,256]{1,0:T(8,128)(2,1)S(1)}, bf16[512,256]{1,0:T(8,128)(2,1)S(1)}, u32[]{:S(2)}, u32[]{:S(2)}) collective-permute-start(bf16[512,256]{1,0:T(8,128)(2,1)S(1)} %constant_dynamic-update-slice_fusion), channel_id=1, source_target_pairs={{0,48},{8,56},{16,0},{24,8},{32,16},{40,24},{48,32},{56,40},{64,11... | collective-permute-start | bytes 786440 | tf_op jit(solution)/shard_map/ppermute | solution.py:41
  17.3 19.3 %collective-permute-start.1 = (bf16[512,256]{1,0:T(8,128)(2,1)S(1)}, bf16[512,256]{1,0:T(8,128)(2,1)S(1)}, u32[]{:S(2)}, u32[]{:S(2)}) collective-permute-start(bf16[512,256]{1,0:T(8,128)(2,1)S(1)} %constant_dynamic-update-slice_fusion), channel_id=1, source_target_pairs={{0,16},{8,24},{16,32},{24,40},{32,48},{40,56},{48,0},{56,8},{64,80... | collective-permute-start | bytes 786440 | tf_op jit(solution)/shard_map/ppermute | solution.py:41
  19.8 0.6 copy-start.14
  20.4 6.1 %copy-start.22 = (f32[32]{0:T(128)S(1)}, f32[32]{0:T(128)}, u32[]{:S(2)}) copy-start(f32[32]{0:T(128)} %param.17) | copy-start | bytes 388
  20.4 6.2 %copy-start.23 = (f32[32]{0:T(128)S(1)}, f32[32]{0:T(128)}, u32[]{:S(2)}) copy-start(f32[32]{0:T(128)} %param.16) | copy-start | bytes 388
  26.5 19.9 %copy-start.24 = (f32[32]{0:T(128)S(1)}, f32[32]{0:T(128)}, u32[]{:S(2)}) copy-start(f32[32]{0:T(128)} %param.18) | copy-start | bytes 388
  36.6 11.0 %copy-start.15 = (bf16[512,256]{1,0:T(8,128)(2,1)}, bf16[512,256]{1,0:T(8,128)(2,1)S(1)}, u32[]{:S(2)}) copy-start(bf16[512,256]{1,0:T(8,128)(2,1)S(1)} %collective-permute-done.2) | copy-start | bytes 786436
  36.6 11.0 %copy-start.17 = (bf16[512,256]{1,0:T(8,128)(2,1)}, bf16[512,256]{1,0:T(8,128)(2,1)S(1)}, u32[]{:S(2)}) copy-start(bf16[512,256]{1,0:T(8,128)(2,1)S(1)} %collective-permute-done.1) | copy-start | bytes 786436
  36.6 10.7 %collective-permute-start.3 = (bf16[1040,256]{1,0:T(8,128)(2,1)}, bf16[1040,256]{1,0:T(8,128)(2,1)S(1)}, u32[]{:S(2)}, u32[]{:S(2)}) collective-permute-start(bf16[1040,256]{1,0:T(8,128)(2,1)} %get-tuple-element.55), channel_id=1, source_target_pairs={{0,8},{8,0},{16,24},{24,16},{32,40},{40,32},{48,56},{56,48},{64,72... | collective-permute-start | bytes 1597448 | tf_op jit(solution)/shard_map/ppermute | solution.py:41
  36.7 22.0 %collective-permute-start.4 = (bf16[512,256]{1,0:T(8,128)(2,1)S(1)}, bf16[512,256]{1,0:T(8,128)(2,1)}, u32[]{:S(2)}, u32[]{:S(2)}) collective-permute-start(bf16[512,256]{1,0:T(8,128)(2,1)S(1)} %constant_dynamic-update-slice_fusion), channel_id=1, source_target_pairs={{0,32},{8,40},{16,48},{24,56},{32,0},{40,8},{48,16},{56,24},{64,96... | collective-permute-start | bytes 786440 | tf_op jit(solution)/shard_map/ppermute | solution.py:41
  48.8 1.3 copy-start.11
  48.8 9.8 %copy-start.16 = (bf16[512,256]{1,0:T(8,128)(2,1)S(1)}, bf16[512,256]{1,0:T(8,128)(2,1)}, u32[]{:S(2)}) copy-start(bf16[512,256]{1,0:T(8,128)(2,1)} %copy-done.15) | copy-start | bytes 786436
  48.8 9.8 %copy-start.18 = (bf16[512,256]{1,0:T(8,128)(2,1)S(1)}, bf16[512,256]{1,0:T(8,128)(2,1)}, u32[]{:S(2)}) copy-start(bf16[512,256]{1,0:T(8,128)(2,1)} %copy-done.17) | copy-start | bytes 786436
  49.2 16.2 %copy-start.2 = (bf16[512,512]{1,0:T(8,128)(2,1)S(1)}, bf16[512,512]{1,0:T(8,128)(2,1)}, u32[]{:S(2)}) copy-start(bf16[512,512]{1,0:T(8,128)(2,1)} %q_ref.1) | copy-start | bytes 1572868
  50.1 33.2 %all-to-all-start.1 = ((bf16[16,80,256]{2,1,0:T(8,128)(2,1)}), bf16[16,80,256]{2,1,0:T(8,128)(2,1)}, u32[]{:S(2)}, u32[]{:S(2)}) async-start(bf16[16,80,256]{2,1,0:T(8,128)(2,1)} %pad_maximum_fusion.1), calls=%async_computation.1 | async-start | bytes 1310720 | tf_op jit(solution)/shard_map/all_to_all | solution.py:374
  59.7 43.2 %collective-permute-start.8 = (bf16[4,512,256]{2,1,0:T(8,128)(2,1)S(1)}, bf16[4,512,256]{2,1,0:T(8,128)(2,1)}, u32[]{:S(2)}, u32[]{:S(2)}) collective-permute-start(bf16[4,512,256]{2,1,0:T(8,128)(2,1)S(1)} %pad_maximum_fusion.refs_0_), channel_id=1, source_target_pairs={{0,192},{8,200},{16,208},{24,216},{32,224},{40,232},{48,240},{56,2... | collective-permute-start | bytes 3145736 | tf_op jit(solution)/shard_map/ppermute | solution.py:41
  61.4 41.5 %collective-permute-start.7 = (bf16[4,512,256]{2,1,0:T(8,128)(2,1)S(1)}, bf16[4,512,256]{2,1,0:T(8,128)(2,1)}, u32[]{:S(2)}, u32[]{:S(2)}) collective-permute-start(bf16[4,512,256]{2,1,0:T(8,128)(2,1)S(1)} %pad_maximum_fusion.refs_0_), channel_id=1, source_target_pairs={{0,64},{8,72},{16,80},{24,88},{32,96},{40,104},{48,112},{56,120},{... | collective-permute-start | bytes 3145736 | tf_op jit(solution)/shard_map/ppermute | solution.py:41
  64.2 9.7 %collective-permute-start.5 = (bf16[4,512,256]{2,1,0:T(8,128)(2,1)S(1)}, bf16[4,512,256]{2,1,0:T(8,128)(2,1)S(1)}, u32[]{:S(2)}, u32[]{:S(2)}) collective-permute-start(bf16[4,512,256]{2,1,0:T(8,128)(2,1)S(1)} %pad_maximum_fusion.refs_0_), channel_id=1, source_target_pairs={{0,8},{8,0},{16,24},{24,16},{32,40},{40,32},{48,56},{56,48},{64,72... | collective-permute-start | bytes 3145736 | tf_op jit(solution)/shard_map/ppermute | solution.py:41
  65.4 36.7 %collective-permute-start.6 = (bf16[512,512]{1,0:T(8,128)(2,1)S(1)}, bf16[512,512]{1,0:T(8,128)(2,1)S(1)}, u32[]{:S(2)}, u32[]{:S(2)}) collective-permute-start(bf16[512,512]{1,0:T(8,128)(2,1)S(1)} %copy-done.2), channel_id=1, source_target_pairs={{128,0},{136,8},{144,16},{152,24},{160,32},{168,40},{176,48},{184,... | collective-permute-start | bytes 1572872 | tf_op jit(solution)/shard_map/ppermute | solution.py:41
  80.0 1.3 copy-start.3
  81.3 1.0 copy-start.5
  82.3 1.0 copy-start.7
  85.3 51.6 %all-to-all-start.2 = ((bf16[16,64,256]{2,1,0:T(8,128)(2,1)}), bf16[16,64,256]{2,1,0:T(8,128)(2,1)}, u32[]{:S(2)}, u32[]{:S(2)}) async-start(bf16[16,64,256]{2,1,0:T(8,128)(2,1)} %shard_map.153), calls=%async_computation.2 | async-start | bytes 1048576 | tf_op jit(solution)/shard_map/all_to_all | solution.py:374
  102.1 0.8 copy-start.9
  102.9 18.9 %copy-start.4 = (f32[4,512,256]{2,1,0:T(8,128)S(1)}, f32[4,512,256]{2,1,0:T(8,128)}, u32[]{:S(2)}) copy-start(f32[4,512,256]{2,1,0:T(8,128)} %copy-done.3) | copy-start | bytes 6291460
  102.9 18.9 %copy-start.6 = (f32[4,512,128]{2,1,0:T(8,128)S(1)}, f32[4,512,128]{2,1,0:T(8,128)}, u32[]{:S(2)}) copy-start(f32[4,512,128]{2,1,0:T(8,128)} %copy-done.5) | copy-start | bytes 3145732
  102.9 18.8 %collective-permute-start.9 = (bf16[4,512,256]{2,1,0:T(8,128)(2,1)}, bf16[4,512,256]{2,1,0:T(8,128)(2,1)S(1)}, u32[]{:S(2)}, u32[]{:S(2)}) collective-permute-start(bf16[4,512,256]{2,1,0:T(8,128)(2,1)} %collective-permute-done.7.refs_0_), channel_id=1, source_target_pairs={{0,8},{8,0},{16,24},{24,16},{32,40},{40,32},{48,56},{56,48},{64,72... | collective-permute-start | bytes 3145736 | tf_op jit(solution)/shard_map/ppermute | solution.py:41
  103.9 17.9 %collective-permute-start.10 = (bf16[4,512,256]{2,1,0:T(8,128)(2,1)}, bf16[4,512,256]{2,1,0:T(8,128)(2,1)S(1)}, u32[]{:S(2)}, u32[]{:S(2)}) collective-permute-start(bf16[4,512,256]{2,1,0:T(8,128)(2,1)} %collective-permute-done.8.refs_2_), channel_id=1, source_target_pairs={{0,8},{8,0},{16,24},{24,16},{32,40},{40,32},{48,56},{56,48},{64,72... | collective-permute-start | bytes 3145736 | tf_op jit(solution)/shard_map/ppermute | solution.py:41
  104.0 1.2 copy-start.8
  105.2 1.0 copy-start.10
  119.5 17.4 %copy-start.12 = (bf16[1024,256]{1,0:T(8,128)(2,1)S(1)}, bf16[1024,256]{1,0:T(8,128)(2,1)}, u32[]{:S(2)}) copy-start(bf16[1024,256]{1,0:T(8,128)(2,1)} %copy-done.11) | copy-start | bytes 1572868
  119.5 21.3 %collective-permute-start.12 = (bf16[512,640]{1,0:T(8,128)(2,1)S(1)}, bf16[512,640]{1,0:T(8,128)(2,1)}, u32[]{:S(2)}, u32[]{:S(2)}) collective-permute-start(bf16[512,640]{1,0:T(8,128)(2,1)S(1)} %shard_map.154), channel_id=1, source_target_pairs={{0,128},{8,136},{16,144},{24,152},{32,160},{40,168},{48,176},{56,1... | collective-permute-start | bytes 1966088 | tf_op jit(solution)/shard_map/ppermute | solution.py:41
  136.0 0.8 copy-start.1
  139.5 4.0 %collective-permute-start.11 = (bf16[1024,256]{1,0:T(8,128)(2,1)S(1)}, bf16[1024,256]{1,0:T(8,128)(2,1)S(1)}, u32[]{:S(2)}, u32[]{:S(2)}) collective-permute-start(bf16[1024,256]{1,0:T(8,128)(2,1)S(1)} %bitcast.48), channel_id=1, source_target_pairs={{0,8},{8,0},{16,24},{24,16},{32,40},{40,32},{48,56},{56,48},{64,72... | collective-permute-start | bytes 1572872 | tf_op jit(solution)/shard_map/ppermute | solution.py:41
  143.4 0.8 copy-start.13

commit v5 on v4

--- a/solution.py
+++ b/solution.py
@@ -20,7 +20,7 @@
 HBC = HB * PSIZE
 CHUNK = 1024
 VMEM_LIMIT = 58 << 20
-ATTEND_LIMIT = 28 << 20
+ATTEND_LIMIT = 22 << 20
 CONV_ROWS = 256
 END_ROWS = 256
 
@@ -657,18 +657,24 @@
 
 
 def merge_kernel(flag_ref, mine_ref, other_ref, out_ref):
-    row = lax.broadcasted_iota(jnp.int32, (HD, HD), 0)
     with_other = flag_ref[0] > 0
-    logs = [ref[:, QHEADS * HD :] for ref in (mine_ref, other_ref)]
-    for head in range(QHEADS):
-        pick = jnp.where((row >= 32 * head) & (row < 32 * head + 3), 1.0, 0.0).astype(BF)
-        mine, other = [jnp.dot(log, pick, preferred_element_type=F32) for log in logs]
-        other = jnp.where(with_other, other, -1e30)
-        new = jnp.maximum(mine, other)
-        mine, other = jnp.exp2(mine - new), jnp.exp2(other - new)
-        columns = slice(head * HD, (head + 1) * HD)
-        joint = mine_ref[:, columns].astype(F32) * mine + other_ref[:, columns].astype(F32) * other
-        out_ref[:, columns] = (joint / (mine + other)).astype(BF)
+
+    @pl.when(jnp.logical_not(with_other))
+    def _():
+        out_ref[...] = mine_ref[:, : QHEADS * HD]
+
+    @pl.when(with_other)
+    def _():
+        row = lax.broadcasted_iota(jnp.int32, (HD, HD), 0)
+        logs = [ref[:, QHEADS * HD :] for ref in (mine_ref, other_ref)]
+        for head in range(QHEADS):
+            pick = jnp.where((row >= 32 * head) & (row < 32 * head + 3), 1.0, 0.0).astype(BF)
+            mine, other = [jnp.dot(log, pick, preferred_element_type=F32) for log in logs]
+            new = jnp.maximum(mine, other)
+            mine, other = jnp.exp2(mine - new), jnp.exp2(other - new)
+            columns = slice(head * HD, (head + 1) * HD)
+            joint = mine_ref[:, columns].astype(F32) * mine + other_ref[:, columns].astype(F32) * other
+            out_ref[:, columns] = (joint / (mine + other)).astype(BF)
 
 
 def merge(flags, part, other):
@@ -680,7 +686,7 @@
         in_specs=[pl.BlockSpec(memory_space=pltpu.SMEM), wide, wide],
         out_specs=pl.BlockSpec((rows, QHEADS * HD), lambda r: (r, 0)),
         out_shape=jax.ShapeDtypeStruct((TOK, QHEADS * HD), BF),
-        compiler_params=pltpu.CompilerParams(vmem_limit_bytes=VMEM_LIMIT),
+        compiler_params=pltpu.CompilerParams(vmem_limit_bytes=ATTEND_LIMIT),
         cost_estimate=pl.CostEstimate(flops=1 << 20, bytes_accessed=1 << 16, transcendentals=0),
     )(flags, part, other)
 

time: 151 us -> 150 us (level); the launches traced: 151 us -> 147 us
  local copies, waits for them, and re-layouts: 11.5 us -> 9.6 us
    unnamed x52 -> x40, local copies, waits for them, and re-layouts: 9.64 us -> 7.74 us
  transfers between devices with their start and end apart: 16 -> 16, of which waited for: 1 -> 2; matrix products, arithmetic and copies ran while one was open for 6% -> 6% of each run, Pallas kernels for 40% -> 41%
where the time goes in v5:
time: 150 us; the launch traced here: 147 us
  Pallas kernels  66.5 us (44%)
  starting transfers between devices  58 us (39%)
  local copies, waits for them, and re-layouts  9.6 us (6%)
  other arithmetic  7.76 us (5%)
  matrix products  2.31 us (2%)
  waiting for transfers between devices  2.2 us (1%)
    pallas_call x3, Pallas kernels, attend(): pl.pallas_call(functools.partial(attend_kernel, planes=planes, own=own, f...  34.4 us
    all_to_all x2, starting transfers between devices, exchanged(): lax.all_to_all(value, 'ctx', 0, 0, tiled=True, axis_index_groups=SAME_CORE)  23.6 us
    ppermute x12, starting transfers between devices, send(): return lax.ppermute(value, 'ctx', pairs_of(move))  23 us
    pallas_call x1, Pallas kernels, own_states(): pl.pallas_call(states_kernel, grid=(TOK // SPAN,), in_specs=[pl.BlockSpec...  9.12 us
    unnamed x40, local copies, waits for them, and re-layouts  7.74 us
    pallas_call x1, Pallas kernels, inside_blocks(): pl.pallas_call(inside_kernel, grid=(TOK // SPAN, blocks), in_specs=[pl.Bl...  7.23 us
    pallas_call x1, Pallas kernels, finish(): pl.pallas_call(finish_kernel, grid=(TOK // END_ROWS,), in_specs=[pl.Block...  6.27 us
    pallas_call x1, Pallas kernels, convolved(): pl.pallas_call(conv_kernel, grid=(TOK // CONV_ROWS,), in_specs=[pl.BlockS...  6.07 us
  transfers between devices with their start and end apart: 16, of which 2 were waited for; matrix products, arithmetic and copies ran while one was open for 6% of the time, Pallas kernels for 41%

profile of v5, /device:TPU:35, one launch (start us, length us, event | category | flops | bytes accessed | tf_op | source)
XLA Modules:
  0.0 147.4 jit_solution(4078274396627290155)
XLA Ops:
  0.6 0.0 copy-start
  0.6 0.0 slice-start
  0.7 0.8 slice_bitcast_fusion
  1.5 0.4 copy-done
  1.9 2.3 %fusion.10 = f32[256,512]{1,0:T(8,128)} fusion(bf16[1024,256]{1,0:T(8,128)(2,1)} %param.15, bf16[512,1024]{1,0:T(8,128)(2,1)S(1)} %copy-done), kind=kOutput, calls=%fused_computation.41 | convolution fusion | flops 268435456 | bytes 2097152 | tf_op jit(solution)/shard_map/dot_general | solution.py:718
  4.2 5.4 %all-to-all-start = ((f32[8,32,512]{2,1,0:T(8,128)}), f32[8,32,512]{2,1,0:T(8,128)S(1)}, u32[]{:S(2)}, u32[]{:S(2)}) async-start(f32[8,32,512]{2,1,0:T(8,128)} %bitcast.2), calls=%async_computation | async-start | bytes 1048576 | tf_op jit(solution)/shard_map/all_to_all | solution.py:726
  9.6 6.0 %collective-permute-start = (bf16[16,2560]{1,0:T(8,128)(2,1)S(1)}, bf16[16,2560]{1,0:T(8,128)(2,1)S(1)}, u32[]{:S(2)}, u32[]{:S(2)}) collective-permute-start(bf16[16,2560]{1,0:T(8,128)(2,1)S(1)} %pad_maximum_fusion.2), channel_id=1, source_target_pairs={{0,8},{8,16},{16,24},{24,32},{32,40},{40,48},{48,56},{56,64},{64,7... | collective-permute-start | bytes 245768 | tf_op jit(solution)/shard_map/ppermute | solution.py:725
  15.7 1.6 %collective-permute-start.2 = (bf16[512,256]{1,0:T(8,128)(2,1)S(1)}, bf16[512,256]{1,0:T(8,128)(2,1)S(1)}, u32[]{:S(2)}, u32[]{:S(2)}) collective-permute-start(bf16[512,256]{1,0:T(8,128)(2,1)S(1)} %constant_dynamic-update-slice_fusion), channel_id=1, source_target_pairs={{0,48},{8,56},{16,0},{24,8},{32,16},{40,24},{48,32},{56,40},{64,11... | collective-permute-start | bytes 786440 | tf_op jit(solution)/shard_map/ppermute | solution.py:41
  17.3 1.9 %collective-permute-start.1 = (bf16[512,256]{1,0:T(8,128)(2,1)S(1)}, bf16[512,256]{1,0:T(8,128)(2,1)S(1)}, u32[]{:S(2)}, u32[]{:S(2)}) collective-permute-start(bf16[512,256]{1,0:T(8,128)(2,1)S(1)} %constant_dynamic-update-slice_fusion), channel_id=1, source_target_pairs={{0,16},{8,24},{16,32},{24,40},{32,48},{40,56},{48,0},{56,8},{64,80... | collective-permute-start | bytes 786440 | tf_op jit(solution)/shard_map/ppermute | solution.py:41
  19.2 0.6 copy.18
  19.8 0.0 collective-permute-done.xtail_ref.ptail_ref
  19.8 0.6 copy-done.10
  20.4 6.1 %shard_map.149 = (bf16[512,2048]{1,0:T(8,128)(2,1)}, bf16[512,512]{1,0:T(8,128)(2,1)}) custom-call(bf16[512,2048]{1,0:T(8,128)(2,1)} %before_ref.1, bf16[512,2048]{1,0:T(8,128)(2,1)} %before_ref.1, bf16[16,2560]{1,0:T(8,128)(2,1)} %copy-done.10, bf16[512,512]{1,0:T(8,128)(2,1)} %bitcast.43, bf16[512,512]{1,0:T(8,128)(2,1)} %bitcast.44, ...), custom_call_target="tpu_custom_call" | custom-call | flops 1048576 | bytes 65536 | tf_op jit(solution)/shard_map/pallas_call | solution.py:102
  26.5 0.0 all-to-all-done
  26.6 0.9 fusion.9
  27.4 9.1 %shard_map.150 = (f32[32,512]{1,0:T(8,128)}, f32[32,512]{1,0:T(8,128)}, bf16[512,2048]{1,0:T(8,128)(2,1)}, bf16[1024,256]{1,0:T(8,128)(2,1)}, bf16[1040,256]{1,0:T(8,128)(2,1)}) custom-call(s32[1]{0:T(128)} %bitcast.core_ref, bf16[512,2048]{1,0:T(8,128)(2,1)} %get-tuple-element.59.xin_ref, bf16[512,512]{1,0:T(8,128)(2,1)} %get-tuple-element.50.pair_ref.c_ref, ...), custom_call_target="tpu_custom_call" | custom-call | flops 1048576 | bytes 65536 | tf_op jit(solution)/shard_map/pallas_call | solution.py:212
  36.6 0.7 copy-done.11
  37.3 0.1 copy-done.12
  37.4 9.7 %collective-permute-start.4 = (bf16[512,256]{1,0:T(8,128)(2,1)S(1)}, bf16[512,256]{1,0:T(8,128)(2,1)}, u32[]{:S(2)}, u32[]{:S(2)}) collective-permute-start(bf16[512,256]{1,0:T(8,128)(2,1)S(1)} %constant_dynamic-update-slice_fusion), channel_id=1, source_target_pairs={{0,32},{8,40},{16,48},{24,56},{32,0},{40,8},{48,16},{56,24},{64,96... | collective-permute-start | bytes 786440 | tf_op jit(solution)/shard_map/ppermute | solution.py:41
  47.0 0.1 broadcast_in_dim.46
  47.1 0.7 broadcast_in_dim_reshape.3.skip_ref
  47.8 0.1 add_add_fusion.flag_ref
  47.9 0.1 add_add_fusion.1
  47.9 0.0 collective-permute-done.3
  48.0 0.1 reshape.90
  48.1 0.1 select_n.112
  48.2 0.1 select_n.108
  48.3 1.1 broadcast_select_fusion.1
  49.4 0.2 fusion.1
  49.6 0.1 select_convert_fusion
  49.8 0.0 copy-start.1
  49.8 0.9 pad_maximum_fusion.1
  50.7 6.9 %all-to-all-start.1 = ((bf16[16,80,256]{2,1,0:T(8,128)(2,1)}), bf16[16,80,256]{2,1,0:T(8,128)(2,1)}, u32[]{:S(2)}, u32[]{:S(2)}) async-start(bf16[16,80,256]{2,1,0:T(8,128)(2,1)} %pad_maximum_fusion.1), calls=%async_computation.1 | async-start | bytes 1310720 | tf_op jit(solution)/shard_map/all_to_all | solution.py:374
  57.6 1.9 %collective-permute-done.4 = bf16[512,256]{1,0:T(8,128)(2,1)} collective-permute-done((bf16[512,256]{1,0:T(8,128)(2,1)S(1)}, bf16[512,256]{1,0:T(8,128)(2,1)}, u32[]{:S(2)}, u32[]{:S(2)}) %collective-permute-start.4) | collective-permute-done | bytes 262176 | tf_op jit(solution)/shard_map/ppermute | solution.py:41
  59.4 1.2 pad_maximum_fusion.refs_0_
  60.7 1.7 %collective-permute-start.8 = (bf16[4,512,256]{2,1,0:T(8,128)(2,1)S(1)}, bf16[4,512,256]{2,1,0:T(8,128)(2,1)}, u32[]{:S(2)}, u32[]{:S(2)}) collective-permute-start(bf16[4,512,256]{2,1,0:T(8,128)(2,1)S(1)} %pad_maximum_fusion.refs_0_), channel_id=1, source_target_pairs={{0,192},{8,200},{16,208},{24,216},{32,224},{40,232},{48,240},{56,2... | collective-permute-start | bytes 3145736 | tf_op jit(solution)/shard_map/ppermute | solution.py:41
  62.3 2.8 %collective-permute-start.7 = (bf16[4,512,256]{2,1,0:T(8,128)(2,1)S(1)}, bf16[4,512,256]{2,1,0:T(8,128)(2,1)}, u32[]{:S(2)}, u32[]{:S(2)}) collective-permute-start(bf16[4,512,256]{2,1,0:T(8,128)(2,1)S(1)} %pad_maximum_fusion.refs_0_), channel_id=1, source_target_pairs={{0,64},{8,72},{16,80},{24,88},{32,96},{40,104},{48,112},{56,120},{... | collective-permute-start | bytes 3145736 | tf_op jit(solution)/shard_map/ppermute | solution.py:41
  65.2 1.0 collective-permute-start.5
  66.2 1.3 collective-permute-start.6
  67.5 7.2 %shard_map.151.y_ref = bf16[512,2048]{1,0:T(8,128)(2,1)} custom-call(bf16[512,2048]{1,0:T(8,128)(2,1)} %get-tuple-element.59.xin_ref, bf16[512,512]{1,0:T(8,128)(2,1)} %get-tuple-element.50.pair_ref.c_ref, f32[32,512]{1,0:T(8,128)} %get-tuple-element.60.cum_ref, f32[32,512]{1,0:T(8,128)} %get-tuple-element.90.steps_ref, ...), custom_call_target="tpu_custom_call" | custom-call | flops 17179869184 | bytes 65536 | tf_op jit(solution)/shard_map/pallas_call | solution.py:314
  74.8 0.0 collective-permute-done.5.refs_1_
  74.8 6.1 %shard_map.152 = (f32[4,512,256]{2,1,0:T(8,128)S(1)}, f32[4,512,128]{2,1,0:T(8,128)S(1)}) custom-call(s32[3]{0:T(128)S(1)} %add_add_fusion.flag_ref, bf16[512,512]{1,0:T(8,128)(2,1)S(1)} %copy-done.1, bf16[4,512,256]{2,1,0:T(8,128)(2,1)S(1)} %pad_maximum_fusion.refs_0_, bf16[4,512,256]{2,1,0:T(8,128)(2,1)S(1)} %collective-permute-done.5.refs_1_), custom_call_target="tpu_custom_call" | custom-call | flops 1048576 | bytes 65536 | tf_op jit(solution)/shard_map/pallas_call | solution.py:632
  80.9 0.0 copy-start.2
  80.9 1.3 copy-done.2
  82.2 1.0 copy-done.4
  83.2 1.0 copy-done.6
  84.1 2.0 %shard_map.153 = bf16[16,64,256]{2,1,0:T(8,128)(2,1)} custom-call(bf16[16,80,256]{2,1,0:T(8,128)(2,1)} %all-to-all-done.1.from_ref), custom_call_target="tpu_custom_call" | custom-call | flops 1048576 | bytes 65536 | tf_op jit(solution)/shard_map/pallas_call | solution.py:355
  86.2 16.7 %all-to-all-start.2 = ((bf16[16,64,256]{2,1,0:T(8,128)(2,1)}), bf16[16,64,256]{2,1,0:T(8,128)(2,1)}, u32[]{:S(2)}, u32[]{:S(2)}) async-start(bf16[16,64,256]{2,1,0:T(8,128)(2,1)} %shard_map.153), calls=%async_computation.2 | async-start | bytes 1048576 | tf_op jit(solution)/shard_map/all_to_all | solution.py:374
  102.9 0.0 collective-permute-done.6.q_ref
  102.9 0.0 collective-permute-done.7.refs_0_
  102.9 0.0 copy-start.3
  102.9 0.9 collective-permute-start.9
  103.8 0.1 collective-permute-start.10
  103.9 1.2 copy-done.7
  105.1 14.1 %shard_map.154 = bf16[512,640]{1,0:T(8,128)(2,1)} custom-call(s32[3]{0:T(128)S(1)} %get-tuple-element.72.flag_ref, bf16[512,512]{1,0:T(8,128)(2,1)S(1)} %collective-permute-done.6.q_ref, bf16[4,512,256]{2,1,0:T(8,128)(2,1)S(1)} %pad_maximum_fusion.refs_0_, bf16[4,512,256]{2,1,0:T(8,128)(2,1)S(1)} %copy-done.7), custom_call_target="tpu_custom_call" | custom-call | flops 34359738368 | bytes 65536 | tf_op jit(solution)/shard_map/pallas_call | solution.py:632
  119.3 1.3 collective-permute-start.12
  120.7 14.2 %shard_map.155.mine_ref = bf16[512,640]{1,0:T(8,128)(2,1)S(1)} custom-call(s32[3]{0:T(128)S(1)} %get-tuple-element.75.flag_ref, bf16[512,512]{1,0:T(8,128)(2,1)S(1)} %copy-done.1, bf16[4,512,256]{2,1,0:T(8,128)(2,1)} %collective-permute-done.7.refs_0_, bf16[4,512,256]{2,1,0:T(8,128)(2,1)S(1)} %collective-permute-done.9.refs_1_, ...), custom_call_target="tpu_custom_call" | custom-call | flops 1048576 | bytes 65536 | tf_op jit(solution)/shard_map/pallas_call | solution.py:632
  134.9 2.9 %fusion.3 = (bf16[16,64,256]{2,1,0:T(8,128)(2,1)}, bf16[16,64,256]{2,1,0:T(8,128)(2,1)}) fusion(bf16[16,64,256]{2,1,0:T(8,128)(2,1)} %all-to-all-done.2, bf16[16,64,256]{2,1,0:T(8,128)(2,1)} %bitcast.42, f32[16]{0:T(128)S(1)} %get-tuple-element.95, pred[]{:T(512)S(6)} %eq.44), kind=kLoop, calls=%fused_computation.6 | loop fusion | flops 1835008 | bytes 2097217 | tf_op jit(solution)/shard_map/jit(_where)/select_n | solution.py:776
  137.9 0.7 collective-permute-start.11
  138.6 0.1 add_add_fusion.3.flag_ref
  138.6 1.4 shard_map.156
  140.0 0.3 collective-permute-done.11.other_ref
  140.3 0.8 copy-done.9
  141.1 6.3 %shard_map.157 = bf16[512,2048]{1,0:T(8,128)(2,1)} custom-call(s32[1]{0:T(128)} %bitcast.core_ref, bf16[512,2048]{1,0:T(8,128)(2,1)} %shard_map.151.y_ref, bf16[512,512]{1,0:T(8,128)(2,1)} %get-tuple-element.50.pair_ref.c_ref, f32[32,512]{1,0:T(8,128)} %get-tuple-element.70.log_ref, bf16[1024,256]{1,0:T(8,128)(2,1)} %bitcast.46, ...), custom_call_target="tpu_custom_call" | custom-call | flops 1048576 | bytes 65536 | tf_op jit(solution)/shard_map/pallas_call | solution.py:404
  (46 shorter events, 0.3 us)
Async XLA Ops:
  0.6 1.2 copy-start
  0.6 8.9 %slice-start = ((bf16[512,2048]{1,0:T(8,128)(2,1)}), bf16[16,2048]{1,0:T(8,128)(2,1)S(1)}, s32[]{:S(2)}) async-start(bf16[512,2048]{1,0:T(8,128)(2,1)} %before_ref.1), calls=%async_computation.3 | async-start | bytes 131072 | tf_op jit(solution)/shard_map/slice | solution.py:722
  0.7 14.9 %copy-start.13 = (bf16[512,128]{1,0:T(8,128)(2,1)S(1)}, bf16[512,128]{1,0:T(8,128)(2,1)}, u32[]{:S(2)}) copy-start(bf16[512,128]{1,0:T(8,128)(2,1)} %param.26) | copy-start | bytes 393220
  0.7 15.0 %copy-start.14 = (bf16[512,128]{1,0:T(8,128)(2,1)S(1)}, bf16[512,128]{1,0:T(8,128)(2,1)}, u32[]{:S(2)}) copy-start(bf16[512,128]{1,0:T(8,128)(2,1)} %param.27) | copy-start | bytes 393220
  0.7 18.5 %copy-start.15 = (f32[4,1,512]{2,1,0:T(1,128)S(1)}, f32[4,1,512]{2,1,0:T(1,128)}, u32[]{:S(2)}) copy-start(f32[4,1,512]{2,1,0:T(1,128)} %param.22) | copy-start | bytes 24580
  4.2 22.3 %all-to-all-start = ((f32[8,32,512]{2,1,0:T(8,128)}), f32[8,32,512]{2,1,0:T(8,128)S(1)}, u32[]{:S(2)}, u32[]{:S(2)}) async-start(f32[8,32,512]{2,1,0:T(8,128)} %bitcast.2), calls=%async_computation | async-start | bytes 1048576 | tf_op jit(solution)/shard_map/all_to_all | solution.py:726
  9.6 10.2 %collective-permute-start = (bf16[16,2560]{1,0:T(8,128)(2,1)S(1)}, bf16[16,2560]{1,0:T(8,128)(2,1)S(1)}, u32[]{:S(2)}, u32[]{:S(2)}) collective-permute-start(bf16[16,2560]{1,0:T(8,128)(2,1)S(1)} %pad_maximum_fusion.2), channel_id=1, source_target_pairs={{0,8},{8,16},{16,24},{24,32},{32,40},{40,48},{48,56},{56,64},{64,7... | collective-permute-start | bytes 245768 | tf_op jit(solution)/shard_map/ppermute | solution.py:725
  15.7 20.9 %collective-permute-start.2 = (bf16[512,256]{1,0:T(8,128)(2,1)S(1)}, bf16[512,256]{1,0:T(8,128)(2,1)S(1)}, u32[]{:S(2)}, u32[]{:S(2)}) collective-permute-start(bf16[512,256]{1,0:T(8,128)(2,1)S(1)} %constant_dynamic-update-slice_fusion), channel_id=1, source_target_pairs={{0,48},{8,56},{16,0},{24,8},{32,16},{40,24},{48,32},{56,40},{64,11... | collective-permute-start | bytes 786440 | tf_op jit(solution)/shard_map/ppermute | solution.py:41
  17.3 19.3 %collective-permute-start.1 = (bf16[512,256]{1,0:T(8,128)(2,1)S(1)}, bf16[512,256]{1,0:T(8,128)(2,1)S(1)}, u32[]{:S(2)}, u32[]{:S(2)}) collective-permute-start(bf16[512,256]{1,0:T(8,128)(2,1)S(1)} %constant_dynamic-update-slice_fusion), channel_id=1, source_target_pairs={{0,16},{8,24},{16,32},{24,40},{32,48},{40,56},{48,0},{56,8},{64,80... | collective-permute-start | bytes 786440 | tf_op jit(solution)/shard_map/ppermute | solution.py:41
  19.8 0.6 copy-start.10
  20.4 6.1 %copy-start.16 = (f32[32]{0:T(128)S(1)}, f32[32]{0:T(128)}, u32[]{:S(2)}) copy-start(f32[32]{0:T(128)} %param.17) | copy-start | bytes 388
  20.4 6.2 %copy-start.17 = (f32[32]{0:T(128)S(1)}, f32[32]{0:T(128)}, u32[]{:S(2)}) copy-start(f32[32]{0:T(128)} %param.16) | copy-start | bytes 388
  26.5 20.5 %copy-start.18 = (f32[32]{0:T(128)S(1)}, f32[32]{0:T(128)}, u32[]{:S(2)}) copy-start(f32[32]{0:T(128)} %param.18) | copy-start | bytes 388
  36.6 0.7 copy-start.11
  36.6 0.8 copy-start.12
  37.4 10.6 %collective-permute-start.3 = (bf16[1040,256]{1,0:T(8,128)(2,1)}, bf16[1040,256]{1,0:T(8,128)(2,1)S(1)}, u32[]{:S(2)}, u32[]{:S(2)}) collective-permute-start(bf16[1040,256]{1,0:T(8,128)(2,1)} %get-tuple-element.55), channel_id=1, source_target_pairs={{0,8},{8,0},{16,24},{24,16},{32,40},{40,32},{48,56},{56,48},{64,72... | collective-permute-start | bytes 1597448 | tf_op jit(solution)/shard_map/ppermute | solution.py:41
  37.4 22.1 %collective-permute-start.4 = (bf16[512,256]{1,0:T(8,128)(2,1)S(1)}, bf16[512,256]{1,0:T(8,128)(2,1)}, u32[]{:S(2)}, u32[]{:S(2)}) collective-permute-start(bf16[512,256]{1,0:T(8,128)(2,1)S(1)} %constant_dynamic-update-slice_fusion), channel_id=1, source_target_pairs={{0,32},{8,40},{16,48},{24,56},{32,0},{40,8},{48,16},{56,24},{64,96... | collective-permute-start | bytes 786440 | tf_op jit(solution)/shard_map/ppermute | solution.py:41
  49.4 1.3 copy-start.8
  49.8 16.5 %copy-start.1 = (bf16[512,512]{1,0:T(8,128)(2,1)S(1)}, bf16[512,512]{1,0:T(8,128)(2,1)}, u32[]{:S(2)}) copy-start(bf16[512,512]{1,0:T(8,128)(2,1)} %q_ref.1) | copy-start | bytes 1572868
  50.7 33.5 %all-to-all-start.1 = ((bf16[16,80,256]{2,1,0:T(8,128)(2,1)}), bf16[16,80,256]{2,1,0:T(8,128)(2,1)}, u32[]{:S(2)}, u32[]{:S(2)}) async-start(bf16[16,80,256]{2,1,0:T(8,128)(2,1)} %pad_maximum_fusion.1), calls=%async_computation.1 | async-start | bytes 1310720 | tf_op jit(solution)/shard_map/all_to_all | solution.py:374
  60.7 42.2 %collective-permute-start.8 = (bf16[4,512,256]{2,1,0:T(8,128)(2,1)S(1)}, bf16[4,512,256]{2,1,0:T(8,128)(2,1)}, u32[]{:S(2)}, u32[]{:S(2)}) collective-permute-start(bf16[4,512,256]{2,1,0:T(8,128)(2,1)S(1)} %pad_maximum_fusion.refs_0_), channel_id=1, source_target_pairs={{0,192},{8,200},{16,208},{24,216},{32,224},{40,232},{48,240},{56,2... | collective-permute-start | bytes 3145736 | tf_op jit(solution)/shard_map/ppermute | solution.py:41
  62.3 40.5 %collective-permute-start.7 = (bf16[4,512,256]{2,1,0:T(8,128)(2,1)S(1)}, bf16[4,512,256]{2,1,0:T(8,128)(2,1)}, u32[]{:S(2)}, u32[]{:S(2)}) collective-permute-start(bf16[4,512,256]{2,1,0:T(8,128)(2,1)S(1)} %pad_maximum_fusion.refs_0_), channel_id=1, source_target_pairs={{0,64},{8,72},{16,80},{24,88},{32,96},{40,104},{48,112},{56,120},{... | collective-permute-start | bytes 3145736 | tf_op jit(solution)/shard_map/ppermute | solution.py:41
  65.2 9.6 %collective-permute-start.5 = (bf16[4,512,256]{2,1,0:T(8,128)(2,1)S(1)}, bf16[4,512,256]{2,1,0:T(8,128)(2,1)S(1)}, u32[]{:S(2)}, u32[]{:S(2)}) collective-permute-start(bf16[4,512,256]{2,1,0:T(8,128)(2,1)S(1)} %pad_maximum_fusion.refs_0_), channel_id=1, source_target_pairs={{0,8},{8,0},{16,24},{24,16},{32,40},{40,32},{48,56},{56,48},{64,72... | collective-permute-start | bytes 3145736 | tf_op jit(solution)/shard_map/ppermute | solution.py:41
  66.2 36.6 %collective-permute-start.6 = (bf16[512,512]{1,0:T(8,128)(2,1)S(1)}, bf16[512,512]{1,0:T(8,128)(2,1)S(1)}, u32[]{:S(2)}, u32[]{:S(2)}) collective-permute-start(bf16[512,512]{1,0:T(8,128)(2,1)S(1)} %copy-done.1), channel_id=1, source_target_pairs={{128,0},{136,8},{144,16},{152,24},{160,32},{168,40},{176,48},{184,... | collective-permute-start | bytes 1572872 | tf_op jit(solution)/shard_map/ppermute | solution.py:41
  80.9 1.3 copy-start.2
  82.2 1.0 copy-start.4
  83.2 1.0 copy-start.6
  86.2 48.7 %all-to-all-start.2 = ((bf16[16,64,256]{2,1,0:T(8,128)(2,1)}), bf16[16,64,256]{2,1,0:T(8,128)(2,1)}, u32[]{:S(2)}, u32[]{:S(2)}) async-start(bf16[16,64,256]{2,1,0:T(8,128)(2,1)} %shard_map.153), calls=%async_computation.2 | async-start | bytes 1048576 | tf_op jit(solution)/shard_map/all_to_all | solution.py:374
  102.9 17.8 %copy-start.3 = (f32[4,512,256]{2,1,0:T(8,128)S(1)}, f32[4,512,256]{2,1,0:T(8,128)}, u32[]{:S(2)}) copy-start(f32[4,512,256]{2,1,0:T(8,128)} %copy-done.2) | copy-start | bytes 6291460
  102.9 17.8 %copy-start.5 = (f32[4,512,128]{2,1,0:T(8,128)S(1)}, f32[4,512,128]{2,1,0:T(8,128)}, u32[]{:S(2)}) copy-start(f32[4,512,128]{2,1,0:T(8,128)} %copy-done.4) | copy-start | bytes 3145732
  102.9 17.7 %collective-permute-start.9 = (bf16[4,512,256]{2,1,0:T(8,128)(2,1)}, bf16[4,512,256]{2,1,0:T(8,128)(2,1)S(1)}, u32[]{:S(2)}, u32[]{:S(2)}) collective-permute-start(bf16[4,512,256]{2,1,0:T(8,128)(2,1)} %collective-permute-done.7.refs_0_), channel_id=1, source_target_pairs={{0,8},{8,0},{16,24},{24,16},{32,40},{40,32},{48,56},{56,48},{64,72... | collective-permute-start | bytes 3145736 | tf_op jit(solution)/shard_map/ppermute | solution.py:41
  103.8 16.8 %collective-permute-start.10 = (bf16[4,512,256]{2,1,0:T(8,128)(2,1)}, bf16[4,512,256]{2,1,0:T(8,128)(2,1)S(1)}, u32[]{:S(2)}, u32[]{:S(2)}) collective-permute-start(bf16[4,512,256]{2,1,0:T(8,128)(2,1)} %collective-permute-done.8.refs_2_), channel_id=1, source_target_pairs={{0,8},{8,0},{16,24},{24,16},{32,40},{40,32},{48,56},{56,48},{64,72... | collective-permute-start | bytes 3145736 | tf_op jit(solution)/shard_map/ppermute | solution.py:41
  103.9 1.2 copy-start.7
  119.3 19.3 %collective-permute-start.12 = (bf16[512,640]{1,0:T(8,128)(2,1)}, bf16[512,640]{1,0:T(8,128)(2,1)S(1)}, u32[]{:S(2)}, u32[]{:S(2)}) collective-permute-start(bf16[512,640]{1,0:T(8,128)(2,1)} %shard_map.154), channel_id=1, source_target_pairs={{0,128},{8,136},{16,144},{24,152},{32,160},{40,168},{48,176},{56,1... | collective-permute-start | bytes 1966088 | tf_op jit(solution)/shard_map/ppermute | solution.py:41
  137.9 2.4 %collective-permute-start.11 = (bf16[1024,256]{1,0:T(8,128)(2,1)}, bf16[1024,256]{1,0:T(8,128)(2,1)S(1)}, u32[]{:S(2)}, u32[]{:S(2)}) collective-permute-start(bf16[1024,256]{1,0:T(8,128)(2,1)} %bitcast.19), channel_id=1, source_target_pairs={{0,8},{8,0},{16,24},{24,16},{32,40},{40,32},{48,56},{56,48},{64,72... | collective-permute-start | bytes 1572872 | tf_op jit(solution)/shard_map/ppermute | solution.py:41
  140.3 0.8 copy-start.9

commit v6 on v5

--- a/solution.py
+++ b/solution.py
@@ -244,7 +244,8 @@
     )(core, xin, pair, steps, drop)
 
 
-def inside_kernel(
+def inside_span(
+    part,
     xin_ref,
     pair_ref,
     cum_ref,
@@ -262,7 +263,7 @@
     block = pl.program_id(1)
     cmat = pair_ref[:, STATE:]
 
-    @pl.when((block == 0) & (pl.program_id(0) == 0))
+    @pl.when((block == 0) & (pl.program_id(0) == 0) & (part == 0))
     def _():
         spread_s[...] = spread_heads()
         column_s[...] = spread_columns()
@@ -309,20 +310,36 @@
         ).astype(BF)
 
 
+def inside_kernel(xin_ref, pair_ref, cum_ref, steps_ref, read_ref, skip_ref, y_ref, *scratch):
+    for part in range(2):
+        at = pl.ds(part * SPAN, SPAN)
+        inside_span(
+            part,
+            xin_ref.at[at, :],
+            pair_ref.at[at, :],
+            cum_ref.at[:, at],
+            steps_ref.at[:, at],
+            read_ref.at[at, :],
+            skip_ref,
+            y_ref.at[at, :],
+            *scratch,
+        )
+
+
 def inside_blocks(xin, pair, cum, steps, read, skip):
     blocks = HEADS // HB
     return pl.pallas_call(
         inside_kernel,
-        grid=(TOK // SPAN, blocks),
+        grid=(TOK // (2 * SPAN), blocks),
         in_specs=[
-            pl.BlockSpec((SPAN, HBC), lambda s, b: (s, b)),
-            pl.BlockSpec((SPAN, 2 * STATE), lambda s, b: (s, 0)),
-            pl.BlockSpec((HEADS, SPAN), lambda s, b: (0, s)),
-            pl.BlockSpec((HEADS, SPAN), lambda s, b: (0, s)),
-            pl.BlockSpec((SPAN, HBC), lambda s, b: (s, b)),
+            pl.BlockSpec((2 * SPAN, HBC), lambda s, b: (s, b)),
+            pl.BlockSpec((2 * SPAN, 2 * STATE), lambda s, b: (s, 0)),
+            pl.BlockSpec((HEADS, 2 * SPAN), lambda s, b: (0, s)),
+            pl.BlockSpec((HEADS, 2 * SPAN), lambda s, b: (0, s)),
+            pl.BlockSpec((2 * SPAN, HBC), lambda s, b: (s, b)),
             pl.BlockSpec((1, HBC), lambda s, b: (0, b)),
         ],
-        out_specs=pl.BlockSpec((SPAN, HBC), lambda s, b: (s, b)),
+        out_specs=pl.BlockSpec((2 * SPAN, HBC), lambda s, b: (s, b)),
         out_shape=jax.ShapeDtypeStruct((TOK, CHAN), BF),
         scratch_shapes=[
             pltpu.VMEM((SPAN, SPAN), F32),

time: 150 us -> 150 us (level)
  no operation moved by 1% of the time
where the time goes in v6:
time: 150 us; the launch traced here: 147 us
  Pallas kernels  66.3 us (44%)
  starting transfers between devices  58.1 us (39%)
  local copies, waits for them, and re-layouts  9.6 us (6%)
  other arithmetic  7.76 us (5%)
  matrix products  2.31 us (2%)
  waiting for transfers between devices  2.2 us (1%)
    pallas_call x3, Pallas kernels, attend(): pl.pallas_call(functools.partial(attend_kernel, planes=planes, own=own, f...  34.5 us
    all_to_all x2, starting transfers between devices, exchanged(): lax.all_to_all(value, 'ctx', 0, 0, tiled=True, axis_index_groups=SAME_CORE)  23.6 us
    ppermute x12, starting transfers between devices, send(): return lax.ppermute(value, 'ctx', pairs_of(move))  23.1 us
    pallas_call x1, Pallas kernels, own_states(): pl.pallas_call(states_kernel, grid=(TOK // SPAN,), in_specs=[pl.BlockSpec...  9.12 us
    unnamed x40, local copies, waits for them, and re-layouts  7.74 us
    pallas_call x1, Pallas kernels, inside_blocks(): pl.pallas_call(inside_kernel, grid=(TOK // (2 * SPAN), blocks), in_specs=...  6.96 us
    pallas_call x1, Pallas kernels, finish(): pl.pallas_call(finish_kernel, grid=(TOK // END_ROWS,), in_specs=[pl.Block...  6.27 us
    pallas_call x1, Pallas kernels, convolved(): pl.pallas_call(conv_kernel, grid=(TOK // CONV_ROWS,), in_specs=[pl.BlockS...  6.07 us
  transfers between devices with their start and end apart: 16, of which 2 were waited for; matrix products, arithmetic and copies ran while one was open for 6% of the time, Pallas kernels for 41%

profile of v6, /device:TPU:35, one launch (start us, length us, event | category | flops | bytes accessed | tf_op | source)
XLA Modules:
  0.0 147.2 jit_solution(15090512070313456122)
XLA Ops:
  0.6 0.0 copy-start
  0.6 0.0 slice-start
  0.7 0.8 slice_bitcast_fusion
  1.5 0.4 copy-done
  1.9 2.3 %fusion.10 = f32[256,512]{1,0:T(8,128)} fusion(bf16[1024,256]{1,0:T(8,128)(2,1)} %param.15, bf16[512,1024]{1,0:T(8,128)(2,1)S(1)} %copy-done), kind=kOutput, calls=%fused_computation.41 | convolution fusion | flops 268435456 | bytes 2097152 | tf_op jit(solution)/shard_map/dot_general | solution.py:735
  4.2 5.4 %all-to-all-start = ((f32[8,32,512]{2,1,0:T(8,128)}), f32[8,32,512]{2,1,0:T(8,128)S(1)}, u32[]{:S(2)}, u32[]{:S(2)}) async-start(f32[8,32,512]{2,1,0:T(8,128)} %bitcast.2), calls=%async_computation | async-start | bytes 1048576 | tf_op jit(solution)/shard_map/all_to_all | solution.py:743
  9.6 6.0 %collective-permute-start = (bf16[16,2560]{1,0:T(8,128)(2,1)S(1)}, bf16[16,2560]{1,0:T(8,128)(2,1)S(1)}, u32[]{:S(2)}, u32[]{:S(2)}) collective-permute-start(bf16[16,2560]{1,0:T(8,128)(2,1)S(1)} %pad_maximum_fusion.2), channel_id=1, source_target_pairs={{0,8},{8,16},{16,24},{24,32},{32,40},{40,48},{48,56},{56,64},{64,7... | collective-permute-start | bytes 245768 | tf_op jit(solution)/shard_map/ppermute | solution.py:742
  15.7 1.6 %collective-permute-start.2 = (bf16[512,256]{1,0:T(8,128)(2,1)S(1)}, bf16[512,256]{1,0:T(8,128)(2,1)S(1)}, u32[]{:S(2)}, u32[]{:S(2)}) collective-permute-start(bf16[512,256]{1,0:T(8,128)(2,1)S(1)} %constant_dynamic-update-slice_fusion), channel_id=1, source_target_pairs={{0,48},{8,56},{16,0},{24,8},{32,16},{40,24},{48,32},{56,40},{64,11... | collective-permute-start | bytes 786440 | tf_op jit(solution)/shard_map/ppermute | solution.py:41
  17.3 1.9 %collective-permute-start.1 = (bf16[512,256]{1,0:T(8,128)(2,1)S(1)}, bf16[512,256]{1,0:T(8,128)(2,1)S(1)}, u32[]{:S(2)}, u32[]{:S(2)}) collective-permute-start(bf16[512,256]{1,0:T(8,128)(2,1)S(1)} %constant_dynamic-update-slice_fusion), channel_id=1, source_target_pairs={{0,16},{8,24},{16,32},{24,40},{32,48},{40,56},{48,0},{56,8},{64,80... | collective-permute-start | bytes 786440 | tf_op jit(solution)/shard_map/ppermute | solution.py:41
  19.2 0.6 copy.18
  19.8 0.0 collective-permute-done.xtail_ref.ptail_ref
  19.8 0.6 copy-done.10
  20.4 6.1 %shard_map.149 = (bf16[512,2048]{1,0:T(8,128)(2,1)}, bf16[512,512]{1,0:T(8,128)(2,1)}) custom-call(bf16[512,2048]{1,0:T(8,128)(2,1)} %before_ref.1, bf16[512,2048]{1,0:T(8,128)(2,1)} %before_ref.1, bf16[16,2560]{1,0:T(8,128)(2,1)} %copy-done.10, bf16[512,512]{1,0:T(8,128)(2,1)} %bitcast.43, bf16[512,512]{1,0:T(8,128)(2,1)} %bitcast.44, ...), custom_call_target="tpu_custom_call" | custom-call | flops 1048576 | bytes 65536 | tf_op jit(solution)/shard_map/pallas_call | solution.py:102
  26.5 0.0 all-to-all-done
  26.6 0.9 fusion.9
  27.4 9.1 %shard_map.150 = (f32[32,512]{1,0:T(8,128)}, f32[32,512]{1,0:T(8,128)}, bf16[512,2048]{1,0:T(8,128)(2,1)}, bf16[1024,256]{1,0:T(8,128)(2,1)}, bf16[1040,256]{1,0:T(8,128)(2,1)}) custom-call(s32[1]{0:T(128)} %bitcast.core_ref, bf16[512,2048]{1,0:T(8,128)(2,1)} %get-tuple-element.59.xin_ref, bf16[512,512]{1,0:T(8,128)(2,1)} %get-tuple-element.50.pair_ref.c_ref, ...), custom_call_target="tpu_custom_call" | custom-call | flops 1048576 | bytes 65536 | tf_op jit(solution)/shard_map/pallas_call | solution.py:212
  36.6 0.0 collective-permute-done.1
  36.6 0.7 copy-done.11
  37.3 0.1 copy-done.12
  37.4 0.0 collective-permute-start.3
  37.4 9.7 %collective-permute-start.4 = (bf16[512,256]{1,0:T(8,128)(2,1)S(1)}, bf16[512,256]{1,0:T(8,128)(2,1)}, u32[]{:S(2)}, u32[]{:S(2)}) collective-permute-start(bf16[512,256]{1,0:T(8,128)(2,1)S(1)} %constant_dynamic-update-slice_fusion), channel_id=1, source_target_pairs={{0,32},{8,40},{16,48},{24,56},{32,0},{40,8},{48,16},{56,24},{64,96... | collective-permute-start | bytes 786440 | tf_op jit(solution)/shard_map/ppermute | solution.py:41
  47.0 0.1 broadcast_in_dim.46
  47.1 0.7 broadcast_in_dim_reshape.3.skip_ref
  47.8 0.1 add_add_fusion.flag_ref
  47.9 0.1 add_add_fusion.1
  47.9 0.0 collective-permute-done.3
  48.0 0.1 reshape.90
  48.1 0.1 select_n.112
  48.2 0.1 select_n.108
  48.3 1.1 broadcast_select_fusion.1
  49.4 0.2 fusion.1
  49.6 0.1 select_convert_fusion
  49.8 0.0 copy-start.1
  49.8 0.9 pad_maximum_fusion.1
  50.7 6.9 %all-to-all-start.1 = ((bf16[16,80,256]{2,1,0:T(8,128)(2,1)}), bf16[16,80,256]{2,1,0:T(8,128)(2,1)}, u32[]{:S(2)}, u32[]{:S(2)}) async-start(bf16[16,80,256]{2,1,0:T(8,128)(2,1)} %pad_maximum_fusion.1), calls=%async_computation.1 | async-start | bytes 1310720 | tf_op jit(solution)/shard_map/all_to_all | solution.py:391
  57.6 1.9 %collective-permute-done.4 = bf16[512,256]{1,0:T(8,128)(2,1)} collective-permute-done((bf16[512,256]{1,0:T(8,128)(2,1)S(1)}, bf16[512,256]{1,0:T(8,128)(2,1)}, u32[]{:S(2)}, u32[]{:S(2)}) %collective-permute-start.4) | collective-permute-done | bytes 262176 | tf_op jit(solution)/shard_map/ppermute | solution.py:41
  59.4 1.2 pad_maximum_fusion.refs_0_
  60.7 1.7 %collective-permute-start.8 = (bf16[4,512,256]{2,1,0:T(8,128)(2,1)S(1)}, bf16[4,512,256]{2,1,0:T(8,128)(2,1)}, u32[]{:S(2)}, u32[]{:S(2)}) collective-permute-start(bf16[4,512,256]{2,1,0:T(8,128)(2,1)S(1)} %pad_maximum_fusion.refs_0_), channel_id=1, source_target_pairs={{0,192},{8,200},{16,208},{24,216},{32,224},{40,232},{48,240},{56,2... | collective-permute-start | bytes 3145736 | tf_op jit(solution)/shard_map/ppermute | solution.py:41
  62.3 2.8 %collective-permute-start.7 = (bf16[4,512,256]{2,1,0:T(8,128)(2,1)S(1)}, bf16[4,512,256]{2,1,0:T(8,128)(2,1)}, u32[]{:S(2)}, u32[]{:S(2)}) collective-permute-start(bf16[4,512,256]{2,1,0:T(8,128)(2,1)S(1)} %pad_maximum_fusion.refs_0_), channel_id=1, source_target_pairs={{0,64},{8,72},{16,80},{24,88},{32,96},{40,104},{48,112},{56,120},{... | collective-permute-start | bytes 3145736 | tf_op jit(solution)/shard_map/ppermute | solution.py:41
  65.2 1.0 collective-permute-start.5
  66.2 1.3 collective-permute-start.6
  67.5 7.0 %shard_map.151.y_ref = bf16[512,2048]{1,0:T(8,128)(2,1)} custom-call(bf16[512,2048]{1,0:T(8,128)(2,1)} %get-tuple-element.59.xin_ref, bf16[512,512]{1,0:T(8,128)(2,1)} %get-tuple-element.50.pair_ref.c_ref, f32[32,512]{1,0:T(8,128)} %get-tuple-element.60.cum_ref, f32[32,512]{1,0:T(8,128)} %get-tuple-element.90.steps_ref, ...), custom_call_target="tpu_custom_call" | custom-call | flops 17179869184 | bytes 65536 | tf_op jit(solution)/shard_map/pallas_call | solution.py:331
  74.5 0.0 collective-permute-done.5.refs_1_
  74.5 6.1 %shard_map.152 = (f32[4,512,256]{2,1,0:T(8,128)S(1)}, f32[4,512,128]{2,1,0:T(8,128)S(1)}) custom-call(s32[3]{0:T(128)S(1)} %add_add_fusion.flag_ref, bf16[512,512]{1,0:T(8,128)(2,1)S(1)} %copy-done.1, bf16[4,512,256]{2,1,0:T(8,128)(2,1)S(1)} %pad_maximum_fusion.refs_0_, bf16[4,512,256]{2,1,0:T(8,128)(2,1)S(1)} %collective-permute-done.5.refs_1_), custom_call_target="tpu_custom_call" | custom-call | flops 1048576 | bytes 65536 | tf_op jit(solution)/shard_map/pallas_call | solution.py:649
  80.6 0.0 copy-start.2
  80.6 1.3 copy-done.2
  81.9 1.0 copy-done.4
  82.9 1.0 copy-done.6
  83.9 2.0 %shard_map.153 = bf16[16,64,256]{2,1,0:T(8,128)(2,1)} custom-call(bf16[16,80,256]{2,1,0:T(8,128)(2,1)} %all-to-all-done.1.from_ref), custom_call_target="tpu_custom_call" | custom-call | flops 1048576 | bytes 65536 | tf_op jit(solution)/shard_map/pallas_call | solution.py:372
  85.9 16.7 %all-to-all-start.2 = ((bf16[16,64,256]{2,1,0:T(8,128)(2,1)}), bf16[16,64,256]{2,1,0:T(8,128)(2,1)}, u32[]{:S(2)}, u32[]{:S(2)}) async-start(bf16[16,64,256]{2,1,0:T(8,128)(2,1)} %shard_map.153), calls=%async_computation.2 | async-start | bytes 1048576 | tf_op jit(solution)/shard_map/all_to_all | solution.py:391
  102.6 0.0 copy-start.3
  102.6 1.0 collective-permute-start.9
  103.6 0.1 collective-permute-start.10
  103.7 1.2 copy-done.7
  104.9 14.1 %shard_map.154 = bf16[512,640]{1,0:T(8,128)(2,1)} custom-call(s32[3]{0:T(128)S(1)} %get-tuple-element.72.flag_ref, bf16[512,512]{1,0:T(8,128)(2,1)S(1)} %collective-permute-done.6.q_ref, bf16[4,512,256]{2,1,0:T(8,128)(2,1)S(1)} %pad_maximum_fusion.refs_0_, bf16[4,512,256]{2,1,0:T(8,128)(2,1)S(1)} %copy-done.7), custom_call_target="tpu_custom_call" | custom-call | flops 34359738368 | bytes 65536 | tf_op jit(solution)/shard_map/pallas_call | solution.py:649
  119.1 1.3 collective-permute-start.12
  120.5 14.2 %shard_map.155.mine_ref = bf16[512,640]{1,0:T(8,128)(2,1)S(1)} custom-call(s32[3]{0:T(128)S(1)} %get-tuple-element.75.flag_ref, bf16[512,512]{1,0:T(8,128)(2,1)S(1)} %copy-done.1, bf16[4,512,256]{2,1,0:T(8,128)(2,1)} %collective-permute-done.7.refs_0_, bf16[4,512,256]{2,1,0:T(8,128)(2,1)S(1)} %collective-permute-done.9.refs_1_, ...), custom_call_target="tpu_custom_call" | custom-call | flops 1048576 | bytes 65536 | tf_op jit(solution)/shard_map/pallas_call | solution.py:649
  134.7 2.9 %fusion.3 = (bf16[16,64,256]{2,1,0:T(8,128)(2,1)}, bf16[16,64,256]{2,1,0:T(8,128)(2,1)}) fusion(bf16[16,64,256]{2,1,0:T(8,128)(2,1)} %all-to-all-done.2, bf16[16,64,256]{2,1,0:T(8,128)(2,1)} %bitcast.42, f32[16]{0:T(128)S(1)} %get-tuple-element.95, pred[]{:T(512)S(6)} %eq.44), kind=kLoop, calls=%fused_computation.6 | loop fusion | flops 1835008 | bytes 2097217 | tf_op jit(solution)/shard_map/jit(_where)/select_n | solution.py:793
  137.7 0.7 collective-permute-start.11
  138.4 0.1 add_add_fusion.3.flag_ref
  138.4 1.4 shard_map.156
  139.8 0.3 collective-permute-done.11.other_ref
  140.1 0.8 copy-done.9
  140.9 6.3 %shard_map.157 = bf16[512,2048]{1,0:T(8,128)(2,1)} custom-call(s32[1]{0:T(128)} %bitcast.core_ref, bf16[512,2048]{1,0:T(8,128)(2,1)} %shard_map.151.y_ref, bf16[512,512]{1,0:T(8,128)(2,1)} %get-tuple-element.50.pair_ref.c_ref, f32[32,512]{1,0:T(8,128)} %get-tuple-element.70.log_ref, bf16[1024,256]{1,0:T(8,128)(2,1)} %bitcast.46, ...), custom_call_target="tpu_custom_call" | custom-call | flops 1048576 | bytes 65536 | tf_op jit(solution)/shard_map/pallas_call | solution.py:421
  (46 shorter events, 0.3 us)
Async XLA Ops:
  0.6 1.2 copy-start
  0.6 8.9 %slice-start = ((bf16[512,2048]{1,0:T(8,128)(2,1)}), bf16[16,2048]{1,0:T(8,128)(2,1)S(1)}, s32[]{:S(2)}) async-start(bf16[512,2048]{1,0:T(8,128)(2,1)} %before_ref.1), calls=%async_computation.3 | async-start | bytes 131072 | tf_op jit(solution)/shard_map/slice | solution.py:739
  0.7 14.9 %copy-start.13 = (bf16[512,128]{1,0:T(8,128)(2,1)S(1)}, bf16[512,128]{1,0:T(8,128)(2,1)}, u32[]{:S(2)}) copy-start(bf16[512,128]{1,0:T(8,128)(2,1)} %param.26) | copy-start | bytes 393220
  0.7 15.0 %copy-start.14 = (bf16[512,128]{1,0:T(8,128)(2,1)S(1)}, bf16[512,128]{1,0:T(8,128)(2,1)}, u32[]{:S(2)}) copy-start(bf16[512,128]{1,0:T(8,128)(2,1)} %param.27) | copy-start | bytes 393220
  0.7 18.5 %copy-start.15 = (f32[4,1,512]{2,1,0:T(1,128)S(1)}, f32[4,1,512]{2,1,0:T(1,128)}, u32[]{:S(2)}) copy-start(f32[4,1,512]{2,1,0:T(1,128)} %param.22) | copy-start | bytes 24580
  4.2 22.3 %all-to-all-start = ((f32[8,32,512]{2,1,0:T(8,128)}), f32[8,32,512]{2,1,0:T(8,128)S(1)}, u32[]{:S(2)}, u32[]{:S(2)}) async-start(f32[8,32,512]{2,1,0:T(8,128)} %bitcast.2), calls=%async_computation | async-start | bytes 1048576 | tf_op jit(solution)/shard_map/all_to_all | solution.py:743
  9.6 10.2 %collective-permute-start = (bf16[16,2560]{1,0:T(8,128)(2,1)S(1)}, bf16[16,2560]{1,0:T(8,128)(2,1)S(1)}, u32[]{:S(2)}, u32[]{:S(2)}) collective-permute-start(bf16[16,2560]{1,0:T(8,128)(2,1)S(1)} %pad_maximum_fusion.2), channel_id=1, source_target_pairs={{0,8},{8,16},{16,24},{24,32},{32,40},{40,48},{48,56},{56,64},{64,7... | collective-permute-start | bytes 245768 | tf_op jit(solution)/shard_map/ppermute | solution.py:742
  15.7 20.9 %collective-permute-start.2 = (bf16[512,256]{1,0:T(8,128)(2,1)S(1)}, bf16[512,256]{1,0:T(8,128)(2,1)S(1)}, u32[]{:S(2)}, u32[]{:S(2)}) collective-permute-start(bf16[512,256]{1,0:T(8,128)(2,1)S(1)} %constant_dynamic-update-slice_fusion), channel_id=1, source_target_pairs={{0,48},{8,56},{16,0},{24,8},{32,16},{40,24},{48,32},{56,40},{64,11... | collective-permute-start | bytes 786440 | tf_op jit(solution)/shard_map/ppermute | solution.py:41
  17.3 19.3 %collective-permute-start.1 = (bf16[512,256]{1,0:T(8,128)(2,1)S(1)}, bf16[512,256]{1,0:T(8,128)(2,1)S(1)}, u32[]{:S(2)}, u32[]{:S(2)}) collective-permute-start(bf16[512,256]{1,0:T(8,128)(2,1)S(1)} %constant_dynamic-update-slice_fusion), channel_id=1, source_target_pairs={{0,16},{8,24},{16,32},{24,40},{32,48},{40,56},{48,0},{56,8},{64,80... | collective-permute-start | bytes 786440 | tf_op jit(solution)/shard_map/ppermute | solution.py:41
  19.8 0.6 copy-start.10
  20.4 6.1 %copy-start.16 = (f32[32]{0:T(128)S(1)}, f32[32]{0:T(128)}, u32[]{:S(2)}) copy-start(f32[32]{0:T(128)} %param.17) | copy-start | bytes 388
  20.4 6.2 %copy-start.17 = (f32[32]{0:T(128)S(1)}, f32[32]{0:T(128)}, u32[]{:S(2)}) copy-start(f32[32]{0:T(128)} %param.16) | copy-start | bytes 388
  26.5 20.5 %copy-start.18 = (f32[32]{0:T(128)S(1)}, f32[32]{0:T(128)}, u32[]{:S(2)}) copy-start(f32[32]{0:T(128)} %param.18) | copy-start | bytes 388
  36.6 0.7 copy-start.11
  36.6 0.8 copy-start.12
  37.4 10.6 %collective-permute-start.3 = (bf16[1040,256]{1,0:T(8,128)(2,1)}, bf16[1040,256]{1,0:T(8,128)(2,1)S(1)}, u32[]{:S(2)}, u32[]{:S(2)}) collective-permute-start(bf16[1040,256]{1,0:T(8,128)(2,1)} %get-tuple-element.55), channel_id=1, source_target_pairs={{0,8},{8,0},{16,24},{24,16},{32,40},{40,32},{48,56},{56,48},{64,72... | collective-permute-start | bytes 1597448 | tf_op jit(solution)/shard_map/ppermute | solution.py:41
  37.4 22.1 %collective-permute-start.4 = (bf16[512,256]{1,0:T(8,128)(2,1)S(1)}, bf16[512,256]{1,0:T(8,128)(2,1)}, u32[]{:S(2)}, u32[]{:S(2)}) collective-permute-start(bf16[512,256]{1,0:T(8,128)(2,1)S(1)} %constant_dynamic-update-slice_fusion), channel_id=1, source_target_pairs={{0,32},{8,40},{16,48},{24,56},{32,0},{40,8},{48,16},{56,24},{64,96... | collective-permute-start | bytes 786440 | tf_op jit(solution)/shard_map/ppermute | solution.py:41
  49.4 1.3 copy-start.8
  49.8 16.5 %copy-start.1 = (bf16[512,512]{1,0:T(8,128)(2,1)S(1)}, bf16[512,512]{1,0:T(8,128)(2,1)}, u32[]{:S(2)}) copy-start(bf16[512,512]{1,0:T(8,128)(2,1)} %q_ref.1) | copy-start | bytes 1572868
  50.7 33.2 %all-to-all-start.1 = ((bf16[16,80,256]{2,1,0:T(8,128)(2,1)}), bf16[16,80,256]{2,1,0:T(8,128)(2,1)}, u32[]{:S(2)}, u32[]{:S(2)}) async-start(bf16[16,80,256]{2,1,0:T(8,128)(2,1)} %pad_maximum_fusion.1), calls=%async_computation.1 | async-start | bytes 1310720 | tf_op jit(solution)/shard_map/all_to_all | solution.py:391
  60.7 41.9 %collective-permute-start.8 = (bf16[4,512,256]{2,1,0:T(8,128)(2,1)S(1)}, bf16[4,512,256]{2,1,0:T(8,128)(2,1)}, u32[]{:S(2)}, u32[]{:S(2)}) collective-permute-start(bf16[4,512,256]{2,1,0:T(8,128)(2,1)S(1)} %pad_maximum_fusion.refs_0_), channel_id=1, source_target_pairs={{0,192},{8,200},{16,208},{24,216},{32,224},{40,232},{48,240},{56,2... | collective-permute-start | bytes 3145736 | tf_op jit(solution)/shard_map/ppermute | solution.py:41
  62.3 40.3 %collective-permute-start.7 = (bf16[4,512,256]{2,1,0:T(8,128)(2,1)S(1)}, bf16[4,512,256]{2,1,0:T(8,128)(2,1)}, u32[]{:S(2)}, u32[]{:S(2)}) collective-permute-start(bf16[4,512,256]{2,1,0:T(8,128)(2,1)S(1)} %pad_maximum_fusion.refs_0_), channel_id=1, source_target_pairs={{0,64},{8,72},{16,80},{24,88},{32,96},{40,104},{48,112},{56,120},{... | collective-permute-start | bytes 3145736 | tf_op jit(solution)/shard_map/ppermute | solution.py:41
  65.2 9.3 %collective-permute-start.5 = (bf16[4,512,256]{2,1,0:T(8,128)(2,1)S(1)}, bf16[4,512,256]{2,1,0:T(8,128)(2,1)S(1)}, u32[]{:S(2)}, u32[]{:S(2)}) collective-permute-start(bf16[4,512,256]{2,1,0:T(8,128)(2,1)S(1)} %pad_maximum_fusion.refs_0_), channel_id=1, source_target_pairs={{0,8},{8,0},{16,24},{24,16},{32,40},{40,32},{48,56},{56,48},{64,72... | collective-permute-start | bytes 3145736 | tf_op jit(solution)/shard_map/ppermute | solution.py:41
  66.2 36.3 %collective-permute-start.6 = (bf16[512,512]{1,0:T(8,128)(2,1)S(1)}, bf16[512,512]{1,0:T(8,128)(2,1)S(1)}, u32[]{:S(2)}, u32[]{:S(2)}) collective-permute-start(bf16[512,512]{1,0:T(8,128)(2,1)S(1)} %copy-done.1), channel_id=1, source_target_pairs={{128,0},{136,8},{144,16},{152,24},{160,32},{168,40},{176,48},{184,... | collective-permute-start | bytes 1572872 | tf_op jit(solution)/shard_map/ppermute | solution.py:41
  80.6 1.3 copy-start.2
  81.9 1.0 copy-start.4
  82.9 1.0 copy-start.6
  85.9 48.8 %all-to-all-start.2 = ((bf16[16,64,256]{2,1,0:T(8,128)(2,1)}), bf16[16,64,256]{2,1,0:T(8,128)(2,1)}, u32[]{:S(2)}, u32[]{:S(2)}) async-start(bf16[16,64,256]{2,1,0:T(8,128)(2,1)} %shard_map.153), calls=%async_computation.2 | async-start | bytes 1048576 | tf_op jit(solution)/shard_map/all_to_all | solution.py:391
  102.6 17.8 %copy-start.3 = (f32[4,512,256]{2,1,0:T(8,128)S(1)}, f32[4,512,256]{2,1,0:T(8,128)}, u32[]{:S(2)}) copy-start(f32[4,512,256]{2,1,0:T(8,128)} %copy-done.2) | copy-start | bytes 6291460
  102.6 17.8 %copy-start.5 = (f32[4,512,128]{2,1,0:T(8,128)S(1)}, f32[4,512,128]{2,1,0:T(8,128)}, u32[]{:S(2)}) copy-start(f32[4,512,128]{2,1,0:T(8,128)} %copy-done.4) | copy-start | bytes 3145732
  102.6 17.8 %collective-permute-start.9 = (bf16[4,512,256]{2,1,0:T(8,128)(2,1)}, bf16[4,512,256]{2,1,0:T(8,128)(2,1)S(1)}, u32[]{:S(2)}, u32[]{:S(2)}) collective-permute-start(bf16[4,512,256]{2,1,0:T(8,128)(2,1)} %collective-permute-done.7.refs_0_), channel_id=1, source_target_pairs={{0,8},{8,0},{16,24},{24,16},{32,40},{40,32},{48,56},{56,48},{64,72... | collective-permute-start | bytes 3145736 | tf_op jit(solution)/shard_map/ppermute | solution.py:41
  103.6 16.8 %collective-permute-start.10 = (bf16[4,512,256]{2,1,0:T(8,128)(2,1)}, bf16[4,512,256]{2,1,0:T(8,128)(2,1)S(1)}, u32[]{:S(2)}, u32[]{:S(2)}) collective-permute-start(bf16[4,512,256]{2,1,0:T(8,128)(2,1)} %collective-permute-done.8.refs_2_), channel_id=1, source_target_pairs={{0,8},{8,0},{16,24},{24,16},{32,40},{40,32},{48,56},{56,48},{64,72... | collective-permute-start | bytes 3145736 | tf_op jit(solution)/shard_map/ppermute | solution.py:41
  103.7 1.2 copy-start.7
  119.1 19.4 %collective-permute-start.12 = (bf16[512,640]{1,0:T(8,128)(2,1)}, bf16[512,640]{1,0:T(8,128)(2,1)S(1)}, u32[]{:S(2)}, u32[]{:S(2)}) collective-permute-start(bf16[512,640]{1,0:T(8,128)(2,1)} %shard_map.154), channel_id=1, source_target_pairs={{0,128},{8,136},{16,144},{24,152},{32,160},{40,168},{48,176},{56,1... | collective-permute-start | bytes 1966088 | tf_op jit(solution)/shard_map/ppermute | solution.py:41
  137.7 2.4 %collective-permute-start.11 = (bf16[1024,256]{1,0:T(8,128)(2,1)}, bf16[1024,256]{1,0:T(8,128)(2,1)S(1)}, u32[]{:S(2)}, u32[]{:S(2)}) collective-permute-start(bf16[1024,256]{1,0:T(8,128)(2,1)} %bitcast.19), channel_id=1, source_target_pairs={{0,8},{8,0},{16,24},{24,16},{32,40},{40,32},{48,56},{56,48},{64,72... | collective-permute-start | bytes 1572872 | tf_op jit(solution)/shard_map/ppermute | solution.py:41
  140.1 0.8 copy-start.9
